TPU v7x, 256 devices: a whole 4x4x8 slice. The times are simulated.
256 devices in a mesh: dp: 16 (over x, y), mp: 16 (over z, core).
Axes of the slice: x: 4, y: 4, z: 8, core: 2. Of those that a mesh axis runs over, the one named last changes fastest.
Arguments:
- grad_out: bfloat16 [16384, 2560], P(('dp', 'mp')), may hold values from -0.5 to 0.5
- hidden_act: bfloat16 [16384, 13824], P('dp', 'mp'), may hold values from -6 to 6
- carried: bfloat16 [16, 13824, 2560], P('dp', 'mp'), may hold values from -6 to 6
- prior_right: float32 [2560, 64], replicated, may hold values from -6 to 6
Outputs:
- residual_out: bfloat16 [16, 13824, 2560], P('dp', 'mp')
- next_right: float32 [2560, 64], replicated
All inputs are finite; a program needn't handle non-finite values.
Results may differ from a plain program's by a relative error of at most 0.0058.
Values may be sent and summed in bfloat16 or wider, within the bound.
No kernel may reach another device: no remote copies, remote signals or barrier semaphores. Data moves between devices by JAX's collectives and lax.ppermute only.
A program may use at most 64 MiB of HBM per device.

v0:
```python
import jax
import jax.numpy as jnp
from jax import lax
from jax.sharding import Mesh
from jax.sharding import PartitionSpec as P

MP = ("mp_0", "mp_1")
DP = ("dp_0", "dp_1")
DP_MP = ("dp_0", "dp_1", "mp_0", "mp_1")


highest = lax.Precision.HIGHEST
over_rows = (((0,), (0,)), ((), ()))


def sent_to_all(array, axis):
    devices = lax.axis_size(axis)
    return lax.all_to_all(
        jnp.broadcast_to(array[None], (devices, *array.shape)), axis, 0, 0, tiled=True
    )


def joined_along(parts, dim):
    dims = list(parts.shape[1:])
    dims[dim] *= parts.shape[0]
    return jnp.moveaxis(parts, 0, dim).reshape(dims)


def gather_directly(array, axis, dim):
    parts = sent_to_all(array, axis)
    return joined_along(parts, dim)


def rows_for(lines, devices):
    spare = -lines.shape[0] % devices
    if not spare:
        return lines
    return jnp.concatenate([lines, jnp.zeros((spare, *lines.shape[1:]), lines.dtype)])


def in_blocks(array, dim, devices):
    dims = array.shape
    parts = array.reshape(*dims[:dim], devices, dims[dim] // devices, *dims[dim + 1 :])
    return jnp.moveaxis(parts, dim, 0)


def sum_at_owner(array, axis, dim):
    devices = lax.axis_size(axis)
    parts = lax.all_to_all(in_blocks(array, dim, devices), axis, 0, 0, tiled=True)
    return jnp.sum(parts.astype(jnp.float32), axis=0)


def nested_sum(array, axes):
    lines = array.reshape(-1, array.shape[-1])
    padded = rows_for(lines, lax.axis_size(axes))
    whole = gather_directly(sum_at_owner(padded, axes, 0).astype(jnp.bfloat16), axes, 0)
    return lax.slice_in_dim(whole, 0, len(lines)).reshape(array.shape).astype(jnp.float32)


def of_everyone(array, axis):
    return sent_to_all(array, axis).sum(axis=0)


def gathered_by_axis(array, axes, dim):
    far, near = axes
    leading = sent_to_all(array, far)
    parts = jnp.swapaxes(sent_to_all(leading, near), 0, 1)
    return joined_along(parts.reshape(-1, *array.shape), dim)


def summed_rows(array, axes, dim):
    far, near = axes
    own = sum_at_owner(in_blocks(array, dim, lax.axis_size(far)), near, dim + 1)
    return jnp.sum(
        lax.all_to_all(own.astype(jnp.bfloat16), far, 0, 0, tiled=True).astype(jnp.float32), axis=0
    )


def sum_by_parts(array, axes):
    lines = array.reshape(-1, array.shape[-1])
    padded = rows_for(lines, lax.axis_size(axes[0]) * lax.axis_size(axes[1]))
    whole = gathered_by_axis(summed_rows(padded, axes, 0).astype(jnp.bfloat16), axes, 0)
    return lax.slice_in_dim(whole, 0, len(lines)).reshape(array.shape).astype(jnp.float32)


def ortho_from(gram_matrix, left_rows):
    rank_size = gram_matrix.shape[0]
    identity = jnp.eye(rank_size, dtype=jnp.float32)
    ridge_shift = 0.001 * jnp.trace(gram_matrix) / rank_size
    cholesky_factor = jnp.linalg.cholesky(gram_matrix + ridge_shift * identity)
    inverse = lax.linalg.triangular_solve(cholesky_factor, identity, left_side=True, lower=True)
    return jnp.dot(left_rows, inverse.T, precision=highest, preferred_element_type=jnp.float32)


def merged_block(grad_out, hidden_act, carried):
    weight_grad = lax.dot_general(
        hidden_act,
        lax.all_gather(grad_out, MP, axis=0, tiled=True),
        over_rows,
        preferred_element_type=jnp.float32,
    )
    return carried[0].astype(jnp.float32) + weight_grad


def per_device(grad_out, hidden_act, carried, prior_right):
    out_proj = jnp.dot(
        grad_out.astype(jnp.float32),
        prior_right,
        precision=highest,
        preferred_element_type=jnp.float32,
    )
    gathered_proj = gather_directly(out_proj, MP, 0)
    left_local = jnp.dot(
        carried[0].astype(jnp.float32),
        prior_right,
        precision=highest,
        preferred_element_type=jnp.float32,
    )
    left_local = left_local + lax.dot_general(
        hidden_act.astype(jnp.float32),
        gathered_proj,
        over_rows,
        precision=highest,
        preferred_element_type=jnp.float32,
    )
    left_whole = nested_sum(left_local.astype(jnp.bfloat16), DP)
    gram_part = jnp.dot(
        left_whole.T, left_whole, precision=highest, preferred_element_type=jnp.float32
    )
    gram_matrix = of_everyone(gram_part, MP)
    ortho_left = ortho_from(gram_matrix, left_whole)
    merged = merged_block(grad_out, hidden_act, carried)
    right_part = lax.dot_general(
        merged, ortho_left, over_rows, precision=highest, preferred_element_type=jnp.float32
    )
    next_right = sum_by_parts(
        right_part.astype(jnp.bfloat16), ("dp_0", ("dp_1", "mp_0", "mp_1"))
    ) / lax.axis_size(DP)
    low_rank = jnp.dot(
        ortho_left, next_right.T, precision=highest, preferred_element_type=jnp.float32
    )
    residual_out = (merged - low_rank).astype(jnp.bfloat16)[None]
    return (residual_out, next_right)


def solution(mesh):
    split = Mesh(mesh.devices.reshape(4, 4, 8, 2), ("dp_0", "dp_1", "mp_0", "mp_1"))
    placed = (P(DP_MP, None), P(DP, MP), P(DP, MP, None), P())
    return jax.shard_map(
        per_device, mesh=split, in_specs=placed, out_specs=(P(DP, MP, None), P()), check_vma=False
    )
```

profile of v0, /device:TPU:1, one launch (start us, length us, event | category | flops | bytes accessed | tf_op | source)
XLA Modules:
  0.0 194.8 jit_solution(3649999145474643968)
XLA Ops:
  7.2 0.0 copy-start
  7.2 0.0 all-gather.2.cloned.1.call-start
  7.2 0.7 all-gather.2.cloned.1.call-update
  7.9 1.6 fusion.14
  9.6 1.0 reshape.35
  10.6 10.0 %all-to-all-start = ((f32[16,1,4096]{2,1,0:T(1,128)}), f32[16,1,4096]{2,1,0:T(1,128)S(1)}, u32[]{:S(2)}, u32[]{:S(2)}) async-start(f32[16,1,4096]{2,1,0:T(1,128)} %reshape.35), calls=%async_computation | async-start | bytes 524288 | tf_op jit(solution)/shard_map/all_to_all | solution.py:18
  20.6 6.2 %fusion.2 = f32[864,64]{0,1:T(8,128)S(1)} fusion(f32[2560,64]{0,1:T(8,128)} %param.7, bf16[1,864,2560]{2,1,0:T(8,128)(2,1)} %param.6), kind=kOutput, calls=%fused_computation.4 | convolution fusion | flops 1698693120 | bytes 5300224 | tf_op jit(solution)/shard_map/dot_general | solution.py:113
  26.8 6.2 %all-to-all-done = f32[16,1,4096]{2,1,0:T(1,128)S(1)} async-done(((f32[16,1,4096]{2,1,0:T(1,128)}), f32[16,1,4096]{2,1,0:T(1,128)S(1)}, u32[]{:S(2)}, u32[]{:S(2)}) %all-to-all-start) | async-done | bytes 262176 | tf_op jit(solution)/shard_map/all_to_all | solution.py:18
  33.0 0.5 broadcast.60
  33.5 1.3 reduce.9
  34.7 0.2 reshape.36
  35.0 1.9 fusion.7
  36.9 0.4 reshape.31
  37.3 0.3 copy.51
  37.7 0.2 reshape.37
  37.8 13.7 %all_to_all.40 = bf16[16,2,1728]{2,1,0:T(2,128)(2,1)S(1)} all-to-all(bf16[16,2,1728]{2,1,0:T(2,128)(2,1)S(1)} %reshape.37), channel_id=1, replica_groups=mesh['dp_0'=4,'dp_1'=4,'mp_0'=8,'mp_1'=2] {'dp_0','dp_1'}, dimensions={0} | all-to-all | bytes 221184 | tf_op jit(solution)/shard_map/all_to_all | solution.py:49
  51.6 0.2 reshape.38
  51.8 0.1 reduce_sum.57
  51.9 0.2 reshape.39
  52.1 10.2 %all_to_all.41 = bf16[16,2,1728]{2,1,0:T(2,128)(2,1)S(1)} all-to-all(bf16[16,2,1728]{2,1,0:T(2,128)(2,1)S(1)} %reshape.39), channel_id=1, replica_groups=mesh['dp_0'=4,'dp_1'=4,'mp_0'=8,'mp_1'=2] {'dp_0','dp_1'}, dimensions={0} | all-to-all | bytes 221184 | tf_op jit(solution)/shard_map/all_to_all | solution.py:18
  62.3 0.2 reshape.40
  62.5 0.2 convolution_bitcast_fusion.1
  62.8 1.0 reshape.41
  63.9 5.2 %all-to-all-start.3 = ((f32[16,1,4096]{2,1,0:T(1,128)}), f32[16,1,4096]{2,1,0:T(1,128)S(1)}, u32[]{:S(2)}, u32[]{:S(2)}) async-start(f32[16,1,4096]{2,1,0:T(1,128)} %reshape.41), calls=%async_computation.3 | async-start | bytes 524288 | tf_op jit(solution)/shard_map/all_to_all | solution.py:18
  69.1 0.1 reshape.34
  69.2 11.6 %all-to-all-done.3 = f32[16,1,4096]{2,1,0:T(1,128)S(1)} async-done(((f32[16,1,4096]{2,1,0:T(1,128)}), f32[16,1,4096]{2,1,0:T(1,128)S(1)}, u32[]{:S(2)}, u32[]{:S(2)}) %all-to-all-start.3) | async-done | bytes 262176 | tf_op jit(solution)/shard_map/all_to_all | solution.py:18
  80.8 1.3 reduce.10
  82.1 0.2 reshape.42
  82.4 0.1 copy.55
  82.4 0.6 select_reduce_fusion.1
  83.7 5.8 %cholesky.18 = f32[64,64]{1,0:T(8,128)S(1)} custom-call(f32[64,64]{1,0:T(8,128)S(1)} %fusion.12), custom_call_target="Cholesky" | custom-call | tf_op jit(solution)/shard_map/jit(cholesky)/cholesky | solution.py:90
  89.6 0.6 compare_reduce_fusion
  90.3 0.7 fusion.8
  90.9 4.9 %custom-call.6 = f32[1,64,64]{1,2,0:T(8,128)S(1)} custom-call(f32[1,64,64]{2,1,0:T(8,128)S(1)} %fusion.8), custom_call_target="InvertDiagBlocksLowerTriangular" | custom-call | tf_op jit(solution)/shard_map/triangular_solve | solution.py:91
  95.8 0.2 fusion.9
  96.1 0.3 fusion.15
  96.4 0.0 copy-start.2
  96.4 0.0 all-gather.2.cloned.1.call-done
  96.4 6.7 %fusion.13 = f32[864,2560]{1,0:T(8,128)S(1)} fusion(bf16[1024,864]{0,1:T(8,128)(2,1)S(1)} %copy-done, bf16[1024,2560]{1,0:T(8,128)(2,1)} %all-gather.2.cloned.1.call-done), kind=kOutput, calls=%fused_computation.29 | convolution fusion | flops 4529848320 | bytes 15859712 | tf_op jit(solution)/shard_map/dot_general | solution.py:96
  103.2 3.4 %copy-done.1 = f32[864,2560]{1,0:T(8,128)} copy-done((f32[864,2560]{1,0:T(8,128)}, f32[864,2560]{1,0:T(8,128)S(1)}, u32[]{:S(2)}) %copy-start.1) | copy-done | bytes 8847384
  106.6 8.6 %fusion.5 = bf16[2560,64]{0,1:T(8,128)(2,1)S(1)} fusion(f32[864,64]{0,1:T(8,128)S(1)} %fusion.15, f32[864,2560]{1,0:T(8,128)S(1)} %fusion.13, bf16[1,864,2560]{2,1,0:T(8,128)(2,1)} %param.6), kind=kOutput, calls=%fused_computation.7 | convolution fusion | flops 1703280640 | bytes 13819904 | tf_op jit(solution)/shard_map/dot_general | solution.py:133
  115.2 0.3 copy.56
  115.5 0.2 reshape_reshape.4
  115.8 0.8 copy.65
  116.6 0.4 reshape.43
  117.0 17.4 %all_to_all.42 = bf16[64,2,1280]{2,1,0:T(2,128)(2,1)S(1)} all-to-all(bf16[64,2,1280]{2,1,0:T(2,128)(2,1)S(1)} %reshape.43), channel_id=1, replica_groups=mesh['dp_0'=4,'dp_1'=4,'mp_0'=8,'mp_1'=2] {'dp_1','mp_0','mp_1'}, dimensions={0} | all-to-all | bytes 655360 | tf_op jit(solution)/shard_map/all_to_all | solution.py:49
  134.4 0.4 reshape.44
  134.8 0.4 bitcast_reduce_fusion
  135.2 0.1 reshape.45
  135.3 6.5 %all_to_all.43 = bf16[4,2,320]{2,1,0:T(2,128)(2,1)S(1)} all-to-all(bf16[4,2,320]{2,1,0:T(2,128)(2,1)S(1)} %reshape.45), channel_id=1, replica_groups=mesh['dp_0'=4,'dp_1'=4,'mp_0'=8,'mp_1'=2] {'dp_0'}, dimensions={0} | all-to-all | bytes 10240 | tf_op jit(solution)/shard_map/all_to_all | solution.py:75
  141.8 0.1 reshape.46
  141.9 0.1 reshape.47
  142.0 6.5 %all_to_all.44 = bf16[4,2,320]{2,1,0:T(2,128)(2,1)S(1)} all-to-all(bf16[4,2,320]{2,1,0:T(2,128)(2,1)S(1)} %reshape.47), channel_id=1, replica_groups=mesh['dp_0'=4,'dp_1'=4,'mp_0'=8,'mp_1'=2] {'dp_0'}, dimensions={0} | all-to-all | bytes 10240 | tf_op jit(solution)/shard_map/all_to_all | solution.py:18
  148.5 0.1 reshape.48
  148.6 0.2 broadcast_bitcast_fusion
  148.8 0.4 reshape.49
  149.2 21.5 %all_to_all.45 = bf16[64,2,1280]{2,1,0:T(2,128)(2,1)S(1)} all-to-all(bf16[64,2,1280]{2,1,0:T(2,128)(2,1)S(1)} %reshape.49), channel_id=1, replica_groups=mesh['dp_0'=4,'dp_1'=4,'mp_0'=8,'mp_1'=2] {'dp_1','mp_0','mp_1'}, dimensions={0} | all-to-all | bytes 655360 | tf_op jit(solution)/shard_map/all_to_all | solution.py:18
  170.7 0.4 reshape.50
  171.1 0.0 copy-start.3
  171.1 0.3 multiply_bitcast_fusion
  171.4 1.5 copy.60
  172.9 1.6 div.27
  174.6 12.2 %fusion.1 = bf16[1,864,2560]{2,1,0:T(8,128)(2,1)} fusion(f32[864,64]{0,1:T(8,128)S(1)} %copy-done.3, f32[2560,64]{1,0:T(8,128)S(1)} %div.27, f32[864,2560]{1,0:T(8,128)} %copy-done.1, bf16[1,864,2560]{2,1,0:T(8,128)(2,1)} %param.6), kind=kOutput, calls=%fused_computation.3 | convolution fusion | flops 1707540480 | bytes 18571264 | tf_op jit(solution)/shard_map/dot_general | solution.py:139
  186.8 1.2 copy.61
  (14 shorter events, 0.3 us)
Async XLA Ops:
  7.2 27.8 %copy-start = (bf16[1024,864]{0,1:T(8,128)(2,1)S(1)}, bf16[1024,864]{0,1:T(8,128)(2,1)}, u32[]{:S(2)}) copy-start(bf16[1024,864]{0,1:T(8,128)(2,1)} %param.5) | copy-start | bytes 5308420
  7.2 89.3 %all-gather.2.cloned.1.call-start = ((), (), s32[]{:S(2)}) async-start(), calls=%async_computation.8 | async-start | bytes 5570560 | tf_op jit(solution)/shard_map/all_gather | solution.py:98
  10.6 22.3 %all-to-all-start = ((f32[16,1,4096]{2,1,0:T(1,128)}), f32[16,1,4096]{2,1,0:T(1,128)S(1)}, u32[]{:S(2)}, u32[]{:S(2)}) async-start(f32[16,1,4096]{2,1,0:T(1,128)} %reshape.35), calls=%async_computation | async-start | bytes 524288 | tf_op jit(solution)/shard_map/all_to_all | solution.py:18
  63.9 17.0 %all-to-all-start.3 = ((f32[16,1,4096]{2,1,0:T(1,128)}), f32[16,1,4096]{2,1,0:T(1,128)S(1)}, u32[]{:S(2)}, u32[]{:S(2)}) async-start(f32[16,1,4096]{2,1,0:T(1,128)} %reshape.41), calls=%async_computation.3 | async-start | bytes 524288 | tf_op jit(solution)/shard_map/all_to_all | solution.py:18
  96.4 6.8 %copy-start.2 = (f32[864,64]{0,1:T(8,128)}, f32[864,64]{0,1:T(8,128)S(1)}, u32[]{:S(2)}) copy-start(f32[864,64]{0,1:T(8,128)S(1)} %fusion.15) | copy-start | bytes 663556
  103.2 3.4 %copy-start.1 = (f32[864,2560]{1,0:T(8,128)}, f32[864,2560]{1,0:T(8,128)S(1)}, u32[]{:S(2)}) copy-start(f32[864,2560]{1,0:T(8,128)S(1)} %fusion.13) | copy-start | bytes 26542084
  171.1 3.5 %copy-start.3 = (f32[864,64]{0,1:T(8,128)S(1)}, f32[864,64]{0,1:T(8,128)}, u32[]{:S(2)}) copy-start(f32[864,64]{0,1:T(8,128)} %copy-done.2) | copy-start | bytes 663556
Sparse Core Ops, SparseCore 0:
  9.8 49.0 all-gather.1
where the time goes:
time: 195 us
  blocking collectives  75.8 us (39%)
  matrix products  38 us (19%)
  waiting for transfers between devices  18.5 us (9%)
  local copies, waits for them, and re-layouts  16.1 us (8%)
  other arithmetic  16 us (8%)
  starting transfers between devices  15.3 us (8%)
  between operations  15 us (8%)
    all_to_all x3, blocking collectives, sent_to_all(): lax.all_to_all(jnp.broadcast_to(array[None], (devices, *array.shape)), ax...  38.2 us
    all_to_all x2, blocking collectives, sum_at_owner(): lax.all_to_all(in_blocks(array, dim, devices), axis, 0, 0, tiled=True)  31.1 us
    all_to_all x2, waiting for transfers between devices, sent_to_all(): lax.all_to_all(jnp.broadcast_to(array[None], (devices, *array.shape)), ax...  17.8 us
    all_to_all x2, starting transfers between devices, sent_to_all(): lax.all_to_all(jnp.broadcast_to(array[None], (devices, *array.shape)), ax...  15.2 us
    dot_general x1, matrix products, per_device(): jnp.dot(ortho_left, next_right.T, precision=highest, preferred_element_ty...  12.2 us
    unnamed x26, local copies, waits for them, and re-layouts  10 us
    dot_general x1, matrix products, per_device(): lax.dot_general(merged, ortho_left, over_rows, precision=highest, preferr...  8.6 us
    dot_general x1, matrix products, merged_block(): lax.dot_general(hidden_act, lax.all_gather(grad_out, MP, axis=0, tiled=Tr...  6.73 us
  transfers between devices with their start and end apart: 3, of which 2 were waited for; matrix products, arithmetic and copies ran while one was open for 16% of the time, Pallas kernels for 0%

commit v1 on v0

v1 whole, which is shorter than its diff:
```python
import jax
import jax.numpy as jnp
from jax import lax
from jax.sharding import Mesh
from jax.sharding import PartitionSpec as P

MP = ("mp_0", "mp_1")
DP = ("dp_0", "dp_1")
DP_MP = ("dp_0", "dp_1", "mp_0", "mp_1")

bf16 = jnp.bfloat16
f32 = jnp.float32
highest = lax.Precision.HIGHEST


def product(left, right, left_dim, right_dim):
    return lax.dot_general(
        left, right, (((left_dim,), (right_dim,)), ((), ())), preferred_element_type=f32
    )


def sent_to_all(array, axis):
    devices = lax.axis_size(axis)
    return lax.all_to_all(
        jnp.broadcast_to(array[None], (devices, *array.shape)), axis, 0, 0, tiled=True
    )


def halves(array):
    high = lax.reduce_precision(array, 8, 7)
    return high.astype(bf16), (array - high).astype(bf16)


def inverse_factor(gram_matrix):
    rank = gram_matrix.shape[0]
    identity = jnp.eye(rank, dtype=f32)
    shift = 0.001 * jnp.trace(gram_matrix) / rank
    factor = jnp.linalg.cholesky(gram_matrix + shift * identity)
    return lax.linalg.triangular_solve(factor, identity, left_side=True, lower=True)


def per_device(grad_out, hidden_act, carried, prior_right):
    own = carried[0]
    rank = prior_right.shape[1]
    replicas = lax.axis_size(DP)
    rows = own.shape[0] // 2

    gathered = lax.all_gather(grad_out, MP, axis=0, tiled=True)
    prior = jnp.concatenate(halves(prior_right), axis=1)
    proj = product(grad_out, prior, 1, 0)
    proj = jnp.concatenate(halves(proj[:, :rank] + proj[:, rank:]), axis=1)
    proj = sent_to_all(proj, MP).reshape(-1, 2 * rank)
    left = product(own, prior, 1, 0) + product(hidden_act, proj, 0, 0)
    left = left[:, :rank] + left[:, rank:]
    left = jnp.concatenate([left[:rows], left[rows:]], axis=1).astype(bf16)
    left = jnp.sum(sent_to_all(left, DP).astype(f32), axis=0).astype(bf16)
    left = jnp.concatenate([left[:, :rank], left[:, rank:]], axis=0)

    gram = jnp.sum(sent_to_all(product(left, left, 0, 0), MP), axis=0)
    act_left = jnp.concatenate(halves(product(left, hidden_act, 0, 1)), axis=0)
    act_left = product(act_left, gathered, 1, 0)
    right = product(left, own, 0, 0) + act_left[:rank] + act_left[rank:]
    features = right.shape[1] // 4
    right = right.astype(bf16).reshape(4, rank // 4, 4, features)
    right = jnp.swapaxes(right, 1, 2).reshape(16, rank // 4, features)
    right = lax.all_to_all(right, DP, 0, 0, tiled=True)
    right = jnp.sum(right.astype(f32), axis=0).astype(bf16)
    right = jnp.sum(sent_to_all(right, MP).astype(f32), axis=0).astype(bf16)
    right = sent_to_all(right, DP).reshape(4, 4, rank // 4, features)
    right = jnp.swapaxes(right, 1, 2).reshape(rank, 4 * features).astype(f32)

    merged = own.astype(f32) + product(hidden_act, gathered, 0, 0)
    inverse = inverse_factor(gram)
    right = jnp.dot(inverse / replicas, right, precision=highest, preferred_element_type=f32)
    ortho = lax.dot_general(
        left.astype(f32), inverse, (((1,), (1,)), ((), ())), precision=highest,
        preferred_element_type=f32,
    )
    ortho_high, ortho_low = halves(ortho)
    right_high, right_low = halves(right)
    low_rank = product(
        jnp.concatenate([ortho_high, ortho_low, ortho_high], axis=1),
        jnp.concatenate([right_high, right_high, right_low], axis=0),
        1,
        0,
    )
    residual_out = (merged - low_rank).astype(bf16)[None]
    return (residual_out, right.T)


def solution(mesh):
    split = Mesh(mesh.devices.reshape(4, 4, 8, 2), DP_MP)
    placed = (P(DP_MP, None), P(DP, MP), P(DP, MP, None), P())
    return jax.shard_map(
        per_device, mesh=split, in_specs=placed, out_specs=(P(DP, MP, None), P()), check_vma=False
    )
```

time: 195 us -> 159 us (0.82)
  blocking collectives: 75.8 us -> 31.4 us
  waiting for transfers between devices: 18.5 us -> 31.3 us
  starting transfers between devices: 15.3 us -> 25.1 us
  local copies, waits for them, and re-layouts: 16.1 us -> 6.46 us
  matrix products: 38 us -> 32.3 us
    all_to_all x3 -> x0, blocking collectives: 37.6 us -> none  [the longest x2 31.1 us: sum_at_owner(): lax.all_to_all(in_blocks(array, dim, devices), axis, 0, 0, tiled=True)]
    all_to_all x2 -> x4, waiting for transfers between devices: 17.8 us -> 27.4 us  [sent_to_all(): lax.all_to_all(jnp.broadcast_to(array[None], (devices, *array.shape)), ax...]
    unnamed x26 -> x5, local copies, waits for them, and re-layouts: 10 us -> 1.29 us
    all_to_all x3 -> x1, blocking collectives: 38.2 us -> 31.4 us  [sent_to_all(): lax.all_to_all(jnp.broadcast_to(array[None], (devices, *array.shape)), ax...]
    all_to_all x2 -> x4, starting transfers between devices: 15.2 us -> 21.4 us  [sent_to_all(): lax.all_to_all(jnp.broadcast_to(array[None], (devices, *array.shape)), ax...]
    dot_general x8 -> x11, matrix products: 37.8 us -> 32 us  [the longest x9 30.4 us: product(): lax.dot_general(left, right, (((left_dim,), (right_dim,)), ((), ())), pre...]
    all_to_all x0 -> x1, starting transfers between devices: none -> 3.62 us  [per_device(): right = lax.all_to_all(right, DP, 0, 0, tiled=True)]
    all_to_all x0 -> x1, waiting for transfers between devices: none -> 3.24 us  [per_device(): right = lax.all_to_all(right, DP, 0, 0, tiled=True)]
  transfers between devices with their start and end apart: 3 -> 6, of which waited for: 2 -> 4; matrix products, arithmetic and copies ran while one was open for 16% -> 23% of each run, Pallas kernels for 0% -> 0%
where the time goes in v1:
time: 159 us; the launch traced here: 158 us
  matrix products  32.3 us (20%)
  blocking collectives  31.4 us (20%)
  waiting for transfers between devices  31.3 us (20%)
  starting transfers between devices  25.1 us (16%)
  other arithmetic  16.7 us (11%)
  between operations  14.9 us (9%)
  local copies, waits for them, and re-layouts  6.46 us (4%)
    all_to_all x1, blocking collectives, sent_to_all(): lax.all_to_all(jnp.broadcast_to(array[None], (devices, *array.shape)), ax...  31.4 us
    dot_general x9, matrix products, product(): lax.dot_general(left, right, (((left_dim,), (right_dim,)), ((), ())), pre...  30.4 us
    all_to_all x4, waiting for transfers between devices, sent_to_all(): lax.all_to_all(jnp.broadcast_to(array[None], (devices, *array.shape)), ax...  27.4 us
    all_to_all x4, starting transfers between devices, sent_to_all(): lax.all_to_all(jnp.broadcast_to(array[None], (devices, *array.shape)), ax...  21.4 us
    another operation x3, other arithmetic, inverse_factor(): factor = jnp.linalg.cholesky(gram_matrix + shift * identity)  6.52 us
    another operation x2, other arithmetic, inverse_factor(): lax.linalg.triangular_solve(factor, identity, left_side=True, lower=True)  5.55 us
    all_to_all x1, starting transfers between devices, per_device(): right = lax.all_to_all(right, DP, 0, 0, tiled=True)  3.62 us
    all_to_all x1, waiting for transfers between devices, per_device(): right = lax.all_to_all(right, DP, 0, 0, tiled=True)  3.24 us
  transfers between devices with their start and end apart: 6, of which 4 were waited for; matrix products, arithmetic and copies ran while one was open for 23% of the time, Pallas kernels for 0%

profile of v1, /device:TPU:1, one launch (start us, length us, event | category | flops | bytes accessed | tf_op | source)
XLA Modules:
  0.0 158.1 jit_solution(14825325146472186733)
XLA Ops:
  7.2 0.0 copy-start
  7.2 0.0 all-gather.2.cloned.1.call-start
  7.2 0.7 all-gather.2.cloned.1.call-update
  7.9 1.2 reduce-precision_convert_fusion.1
  9.1 1.3 convolution_bitcast_fusion
  10.4 0.1 reduce-precision_convert_fusion.4
  10.5 0.1 pad_maximum_fusion.5
  10.6 0.8 broadcast_in_dim.16
  11.3 10.0 %all-to-all-start = ((bf16[16,64,128]{2,1,0:T(8,128)(2,1)}), bf16[16,64,128]{2,1,0:T(8,128)(2,1)S(1)}, u32[]{:S(2)}, u32[]{:S(2)}) async-start(bf16[16,64,128]{2,1,0:T(8,128)(2,1)} %broadcast_in_dim.16), calls=%async_computation | async-start | bytes 524288 | tf_op jit(solution)/shard_map/all_to_all | solution.py:24
  21.3 3.5 %fusion.3 = f32[128,864]{0,1:T(8,128)S(1)} fusion(bf16[1,864,2560]{2,1,0:T(8,128)(2,1)} %param.6, bf16[2560,64]{0,1:T(8,128)(2,1)S(1)} %get-tuple-element.5, bf16[2560,64]{0,1:T(8,128)(2,1)S(1)} %get-tuple-element.4), kind=kOutput, calls=%fused_computation.4 | convolution fusion | flops 567541760 | bytes 5521408 | tf_op jit(solution)/shard_map/dot_general | solution.py:17
  24.8 9.1 %all-to-all-done = bf16[16,64,128]{2,1,0:T(8,128)(2,1)S(1)} async-done(((bf16[16,64,128]{2,1,0:T(8,128)(2,1)}), bf16[16,64,128]{2,1,0:T(8,128)(2,1)S(1)}, u32[]{:S(2)}, u32[]{:S(2)}) %all-to-all-start) | async-done | bytes 262176 | tf_op jit(solution)/shard_map/all_to_all | solution.py:24
  34.0 0.0 copy-done
  34.0 0.6 fusion.14
  34.6 0.2 fusion.22
  34.8 0.1 pad_maximum_fusion.4
  34.9 0.2 broadcast_in_dim.17
  35.2 31.4 %all_to_all.30 = bf16[16,432,128]{2,1,0:T(8,128)(2,1)S(1)} all-to-all(bf16[16,432,128]{2,1,0:T(8,128)(2,1)S(1)} %broadcast_in_dim.17), channel_id=1, replica_groups=mesh['dp_0'=4,'dp_1'=4,'mp_0'=8,'mp_1'=2] {'dp_0','dp_1'}, dimensions={0} | all-to-all | bytes 3538944 | tf_op jit(solution)/shard_map/all_to_all | solution.py:24
  66.6 0.9 reduce_sum.57
  67.5 1.1 fusion.52
  68.6 0.2 fusion.50
  68.8 1.0 reshape.52
  69.9 3.9 %all-to-all-start.2 = ((f32[16,1,4096]{2,1,0:T(1,128)}), f32[16,1,4096]{2,1,0:T(1,128)S(1)}, u32[]{:S(2)}, u32[]{:S(2)}) async-start(f32[16,1,4096]{2,1,0:T(1,128)} %reshape.52), calls=%async_computation.2 | async-start | bytes 524288 | tf_op jit(solution)/shard_map/all_to_all | solution.py:24
  73.7 0.5 reduce-precision_convert_fusion.2
  74.2 11.4 %all-to-all-done.2 = f32[16,1,4096]{2,1,0:T(1,128)S(1)} async-done(((f32[16,1,4096]{2,1,0:T(1,128)}), f32[16,1,4096]{2,1,0:T(1,128)S(1)}, u32[]{:S(2)}, u32[]{:S(2)}) %all-to-all-start.2) | async-done | bytes 262176 | tf_op jit(solution)/shard_map/all_to_all | solution.py:24
  85.6 0.5 broadcast.55
  86.1 1.3 reduce.9
  87.4 0.2 reshape.53
  87.7 0.1 copy.18
  87.7 0.6 select_reduce_fusion.1
  89.0 0.0 all-gather.2.cloned.1.call-done
  89.0 3.3 %fusion.29 = f32[128,2560]{1,0:T(8,128)S(1)} fusion(bf16[1024,2560]{1,0:T(8,128)(2,1)} %all-gather.2.cloned.1.call-done, bf16[64,1024]{1,0:T(8,128)(2,1)S(1)} %get-tuple-element.7, bf16[64,1024]{1,0:T(8,128)(2,1)S(1)} %get-tuple-element.6), kind=kOutput, calls=%fused_computation.36 | convolution fusion | flops 671612928 | bytes 6815744 | tf_op jit(solution)/shard_map/dot_general | solution.py:17
  92.4 3.2 %fusion.11 = bf16[64,2560]{1,0:T(8,128)(2,1)S(1)} fusion(bf16[1,864,2560]{2,1,0:T(8,128)(2,1)} %param.6, f32[128,2560]{1,0:T(8,128)S(1)} %fusion.29, bf16[432,64]{1,0:T(8,128)(2,1)S(1)} %get-tuple-element.13, bf16[432,64]{1,0:T(8,128)(2,1)S(1)} %get-tuple-element.12), kind=kOutput, calls=%fused_computation.8 | convolution fusion | flops 283828224 | bytes 6172672 | tf_op jit(solution)/shard_map/dot_general | solution.py:17
  95.6 0.1 reshape.48
  95.7 0.8 copy.19
  96.4 3.6 %all-to-all-start.3 = ((bf16[16,16,640]{2,1,0:T(8,128)(2,1)}), bf16[16,16,640]{2,1,0:T(8,128)(2,1)S(1)}, u32[]{:S(2)}, u32[]{:S(2)}) async-start(bf16[16,16,640]{2,1,0:T(8,128)(2,1)} %bitcast.8), calls=%async_computation.3 | async-start | bytes 655360 | tf_op jit(solution)/shard_map/all_to_all | solution.py:66
  100.1 5.8 %cholesky.18 = f32[64,64]{1,0:T(8,128)S(1)} custom-call(f32[64,64]{1,0:T(8,128)S(1)} %fusion.39), custom_call_target="Cholesky" | custom-call | tf_op jit(solution)/shard_map/jit(cholesky)/cholesky | solution.py:38
  106.0 0.6 compare_reduce_fusion
  106.6 3.2 %all-to-all-done.3 = bf16[16,16,640]{2,1,0:T(8,128)(2,1)S(1)} async-done(((bf16[16,16,640]{2,1,0:T(8,128)(2,1)}), bf16[16,16,640]{2,1,0:T(8,128)(2,1)S(1)}, u32[]{:S(2)}, u32[]{:S(2)}) %all-to-all-start.3) | async-done | bytes 327712 | tf_op jit(solution)/shard_map/all_to_all | solution.py:66
  109.9 0.1 reduce_sum.61
  109.9 0.8 broadcast_in_dim.20
  110.7 3.9 %all-to-all-start.4 = ((bf16[16,16,640]{2,1,0:T(8,128)(2,1)}), bf16[16,16,640]{2,1,0:T(8,128)(2,1)S(1)}, u32[]{:S(2)}, u32[]{:S(2)}) async-start(bf16[16,16,640]{2,1,0:T(8,128)(2,1)} %broadcast_in_dim.20), calls=%async_computation.4 | async-start | bytes 655360 | tf_op jit(solution)/shard_map/all_to_all | solution.py:24
  114.5 0.7 fusion.34
  115.2 4.9 %custom-call.6 = f32[1,64,64]{1,2,0:T(8,128)S(1)} custom-call(f32[1,64,64]{2,1,0:T(8,128)S(1)} %fusion.34), custom_call_target="InvertDiagBlocksLowerTriangular" | custom-call | tf_op jit(solution)/shard_map/triangular_solve | solution.py:39
  120.1 0.2 fusion.36
  120.3 0.3 fusion.33
  120.7 6.9 %all-to-all-done.4 = bf16[16,16,640]{2,1,0:T(8,128)(2,1)S(1)} async-done(((bf16[16,16,640]{2,1,0:T(8,128)(2,1)}), bf16[16,16,640]{2,1,0:T(8,128)(2,1)S(1)}, u32[]{:S(2)}, u32[]{:S(2)}) %all-to-all-start.4) | async-done | bytes 327712 | tf_op jit(solution)/shard_map/all_to_all | solution.py:24
  127.6 0.1 reduce_sum.62
  127.6 0.8 broadcast_in_dim.22
  128.4 3.7 %all-to-all-start.5 = ((bf16[16,16,640]{2,1,0:T(8,128)(2,1)}), bf16[16,16,640]{2,1,0:T(8,128)(2,1)S(1)}, u32[]{:S(2)}, u32[]{:S(2)}) async-start(bf16[16,16,640]{2,1,0:T(8,128)(2,1)} %broadcast_in_dim.22), calls=%async_computation.5 | async-start | bytes 655360 | tf_op jit(solution)/shard_map/all_to_all | solution.py:24
  132.1 9.5 %fusion.53 = f32[864,2560]{1,0:T(8,128)} fusion(bf16[1024,864]{0,1:T(8,128)(2,1)S(1)} %copy-done, bf16[1024,2560]{1,0:T(8,128)(2,1)} %all-gather.2.cloned.1.call-done), kind=kOutput, calls=%fused_computation.74 | convolution fusion | flops 4529848320 | bytes 15859712 | tf_op jit(solution)/shard_map/dot_general | solution.py:17
  141.6 0.0 all-to-all-done.5
  141.6 0.1 copy.20
  141.8 1.3 reduce-precision_convert_fusion
  143.1 8.2 %fusion = bf16[1,864,2560]{2,1,0:T(8,128)(2,1)} fusion(f32[864,2560]{1,0:T(8,128)} %fusion.53, bf16[1,864,2560]{2,1,0:T(8,128)(2,1)} %param.6, bf16[64,2560]{1,0:T(8,128)(2,1)S(1)} %get-tuple-element.3, bf16[64,2560]{1,0:T(8,128)(2,1)S(1)} %get-tuple-element.2, bf16[864,64]{0,1:T(8,128)(2,1)S(1)} %get-tuple-element.9, bf16[864,64]{0,1:T(8,128)(2,1)S(1)} %get-tuple-element.8), kind=kOutput, calls=%fused_computation.1 | convolution fusion | flops 862138368 | bytes 18571264 | tf_op jit(solution)/shard_map/dot_general | solution.py:17
  (6 shorter events, 0.2 us)
Async XLA Ops:
  7.2 26.8 %copy-start = (bf16[1024,864]{0,1:T(8,128)(2,1)S(1)}, bf16[1024,864]{0,1:T(8,128)(2,1)}, u32[]{:S(2)}) copy-start(bf16[1024,864]{0,1:T(8,128)(2,1)} %param.5) | copy-start | bytes 5308420
  7.2 81.9 %all-gather.2.cloned.1.call-start = ((), (), s32[]{:S(2)}) async-start(), calls=%async_computation.6 | async-start | bytes 5570560 | tf_op jit(solution)/shard_map/all_gather | solution.py:48
  11.3 22.6 %all-to-all-start = ((bf16[16,64,128]{2,1,0:T(8,128)(2,1)}), bf16[16,64,128]{2,1,0:T(8,128)(2,1)S(1)}, u32[]{:S(2)}, u32[]{:S(2)}) async-start(bf16[16,64,128]{2,1,0:T(8,128)(2,1)} %broadcast_in_dim.16), calls=%async_computation | async-start | bytes 524288 | tf_op jit(solution)/shard_map/all_to_all | solution.py:24
  69.9 15.7 %all-to-all-start.2 = ((f32[16,1,4096]{2,1,0:T(1,128)}), f32[16,1,4096]{2,1,0:T(1,128)S(1)}, u32[]{:S(2)}, u32[]{:S(2)}) async-start(f32[16,1,4096]{2,1,0:T(1,128)} %reshape.52), calls=%async_computation.2 | async-start | bytes 524288 | tf_op jit(solution)/shard_map/all_to_all | solution.py:24
  96.4 13.4 %all-to-all-start.3 = ((bf16[16,16,640]{2,1,0:T(8,128)(2,1)}), bf16[16,16,640]{2,1,0:T(8,128)(2,1)S(1)}, u32[]{:S(2)}, u32[]{:S(2)}) async-start(bf16[16,16,640]{2,1,0:T(8,128)(2,1)} %bitcast.8), calls=%async_computation.3 | async-start | bytes 655360 | tf_op jit(solution)/shard_map/all_to_all | solution.py:66
  110.7 16.9 %all-to-all-start.4 = ((bf16[16,16,640]{2,1,0:T(8,128)(2,1)}), bf16[16,16,640]{2,1,0:T(8,128)(2,1)S(1)}, u32[]{:S(2)}, u32[]{:S(2)}) async-start(bf16[16,16,640]{2,1,0:T(8,128)(2,1)} %broadcast_in_dim.20), calls=%async_computation.4 | async-start | bytes 655360 | tf_op jit(solution)/shard_map/all_to_all | solution.py:24
  128.4 13.2 %all-to-all-start.5 = ((bf16[16,16,640]{2,1,0:T(8,128)(2,1)}), bf16[16,16,640]{2,1,0:T(8,128)(2,1)S(1)}, u32[]{:S(2)}, u32[]{:S(2)}) async-start(bf16[16,16,640]{2,1,0:T(8,128)(2,1)} %broadcast_in_dim.22), calls=%async_computation.5 | async-start | bytes 655360 | tf_op jit(solution)/shard_map/all_to_all | solution.py:24
Sparse Core Ops, SparseCore 0:
  9.8 49.8 all-gather.1

commit v2 on v1

v2 whole, which is shorter than its diff:
```python
import functools

import jax
import jax.numpy as jnp
from jax import lax
from jax.experimental import pallas as pl
from jax.experimental.pallas import tpu as pltpu
from jax.sharding import Mesh
from jax.sharding import PartitionSpec as P

MP = ("mp_0", "mp_1")
DP = ("dp_0", "dp_1")
DP_MP = ("dp_0", "dp_1", "mp_0", "mp_1")

bf16 = jnp.bfloat16
f32 = jnp.float32
highest = lax.Precision.HIGHEST
VMEM = pltpu.VMEM
whole = pl.BlockSpec(memory_space=pltpu.VMEM)
anywhere = pl.BlockSpec(memory_space=pltpu.HBM)
scalars = pl.BlockSpec(memory_space=pltpu.SMEM)
MIB = 1024 * 1024


def product(left, right, left_dim, right_dim):
    return lax.dot_general(
        left, right, (((left_dim,), (right_dim,)), ((), ())), preferred_element_type=f32
    )


def sent(array, axis):
    return lax.all_to_all(array, axis, 0, 0, tiled=True)


def sent_to_all(array, axis):
    devices = lax.axis_size(axis)
    return sent(jnp.broadcast_to(array[None], (devices, *array.shape)), axis)


def halves(array):
    high = lax.reduce_precision(array, 8, 7)
    return high.astype(bf16), (array - high).astype(bf16)


def split(array):
    high = array.astype(bf16)
    return high, (array - high.astype(f32)).astype(bf16)


def call(kernel, out_shape, **options):
    return pl.pallas_call(
        kernel,
        out_shape=out_shape,
        compiler_params=pltpu.CompilerParams(vmem_limit_bytes=48 * MIB),
        **options,
    )


def of(shape, kind):
    return jax.ShapeDtypeStruct(shape, kind)


def left_kernel(parts_ref, own_ref, act_ref, left_ref, gram_ref, right_ref, act_left_ref):
    rows, lanes = left_ref.shape
    rank = lanes // 2
    total = parts_ref[0].astype(f32)
    for i in range(1, parts_ref.shape[0]):
        total = total + parts_ref[i].astype(f32)
    left = total.astype(bf16)
    left_ref[...] = left
    turned = left.astype(f32).T.astype(bf16)
    gram = product(left, left, 0, 0)
    gram = gram[:rank, :rank] + gram[rank:, rank:]
    gram_ref[...] = jnp.concatenate([gram[: rank // 2], gram[rank // 2 :]], axis=1)
    upper, lower = turned[:rank], turned[rank:]
    act_left = product(upper, act_ref[:rows], 1, 0) + product(lower, act_ref[rows:], 1, 0)
    act_left_ref[...] = jnp.concatenate(split(act_left), axis=0)
    right_ref[...] = product(upper, own_ref[:rows], 1, 0) + product(lower, own_ref[rows:], 1, 0)


def chunk_copies(place_ref, chunk_refs, full_ref, sems):
    steps = len(chunk_refs) // 2
    tokens = chunk_refs[0].shape[0]
    copies = []
    for k in range(steps):
        far = lax.rem(place_ref[0] + (steps - k), steps)
        for side in range(2):
            near = place_ref[1] if side == 0 else 1 - place_ref[1]
            row = pl.multiple_of((far * 2 + near) * tokens, tokens)
            i = 2 * k + side
            copies.append(
                pltpu.make_async_copy(
                    chunk_refs[i], full_ref.at[pl.ds(row, tokens), :], sems.at[i]
                )
            )
    return copies


def in_terms(rows):
    high, low = split(rows)
    least = rows - high.astype(f32) - low.astype(f32)
    spare = jnp.zeros((16 - 3 * rows.shape[0], rows.shape[1]), f32)
    return jnp.concatenate([high.astype(f32), low.astype(f32), least, spare], axis=0).astype(bf16)


def from_terms(block):
    return block[0:2] + block[2:4] + block[4:6]


def right_kernel(count, *refs):
    place_ref, act_left_ref, right_ref, gram_ref = refs[:4]
    chunk_refs = refs[4 : 4 + count]
    out_ref, full_ref, sems = refs[4 + count :]
    copies = chunk_copies(place_ref, chunk_refs, full_ref, sems)
    for copy in copies:
        copy.start()
    for copy in copies:
        copy.wait()
    rank = right_ref.shape[0]
    both = product(act_left_ref[...], full_ref[...], 1, 0)
    right = (right_ref[...] + both[:rank] + both[rank:]).astype(bf16)
    height = out_ref.shape[1]
    width = right.shape[1] // 4
    for a in range(4):
        for b in range(4):
            piece = 4 * a + b
            out_ref[piece, :, :width] = right[
                a * height : (a + 1) * height, b * width : (b + 1) * width
            ]
            out_ref[piece, :, width:] = in_terms(gram_ref[2 * piece : 2 * piece + 2, :])


def summed_kernel(parts_ref, out_ref):
    total = parts_ref[0].astype(f32)
    for i in range(1, parts_ref.shape[0]):
        total = total + parts_ref[i].astype(f32)
    width = total.shape[1] - 128
    total = jnp.concatenate(
        [total[:, :width].astype(bf16), in_terms(from_terms(total[:, width:]))], axis=1
    )
    for i in range(out_ref.shape[0]):
        out_ref[i] = total


def merged_kernel(count, *refs):
    place_ref, act_ref, own_ref = refs[:3]
    chunk_refs = refs[3 : 3 + count]
    out_ref, full_ref, sems = refs[3 + count :]
    step = pl.program_id(0)

    @pl.when(step == 0)
    def _():
        copies = chunk_copies(place_ref, chunk_refs, full_ref, sems)
        for copy in copies:
            copy.start()
        for copy in copies:
            copy.wait()

    width = out_ref.shape[1]
    columns = full_ref[:, pl.ds(pl.multiple_of(step * width, width), width)]
    out_ref[...] = own_ref[...].astype(f32) + product(act_ref[...], columns, 1, 0)


def inverse_of(gram):
    rank = gram.shape[0]
    row = lax.broadcasted_iota(jnp.int32, (rank, rank), 0)
    column = lax.broadcasted_iota(jnp.int32, (rank, rank), 1)
    diagonal = row == column
    trace = jnp.sum(jnp.where(diagonal, gram, 0.0), keepdims=True)
    gram = gram + jnp.where(diagonal, 0.001 * (trace / rank), 0.0)
    work = jnp.concatenate([gram, jnp.where(diagonal, 1.0, 0.0)], axis=1)
    rows = lax.broadcasted_iota(jnp.int32, (rank, 1), 0)
    for k in range(rank - 1):
        factor = work[:, k : k + 1] * (1.0 / work[k : k + 1, k : k + 1])
        factor = jnp.where(rows > k, factor, 0.0)
        work = work - factor * work[k : k + 1, :]
    pivots = jnp.sum(jnp.where(diagonal, work[:, :rank], 0.0), axis=1, keepdims=True)
    return work[:, rank:] * lax.rsqrt(pivots)


def residual_kernel(
    replicas, gram_ref, left_ref, right_ref, merged_ref, out_ref, next_ref, ortho_ref, inverse_ref
):
    rows = left_ref.shape[0]
    rank = inverse_ref.shape[0]

    @pl.when(pl.program_id(0) == 0)
    def _():
        gram = jnp.concatenate(
            [from_terms(gram_ref[a, b].astype(f32)) for a in range(4) for b in range(4)], axis=0
        ) * (1.0 / replicas)
        inverse = inverse_of(jnp.concatenate([gram[:, :rank], gram[:, rank:]], axis=0))
        inverse_ref[...] = inverse
        left = left_ref[...]
        high, low = split(inverse)
        least = (inverse - high.astype(f32) - low.astype(f32)).astype(bf16)
        for i in range(2):
            part = left[:, i * rank : (i + 1) * rank]
            ortho = product(part, high, 1, 1) + product(part, low, 1, 1) + product(part, least, 1, 1)
            high_part, low_part = split(ortho)
            ortho_ref[i * rows : (i + 1) * rows, :] = jnp.concatenate(
                [high_part, low_part, high_part], axis=1
            )

    right = jnp.concatenate([right_ref[a, 0] for a in range(4)], axis=0).astype(f32)
    turned = jnp.dot(
        inverse_ref[...], right, precision=highest, preferred_element_type=f32
    ) * (1.0 / replicas)
    next_ref[...] = turned
    high, low = split(turned)
    low_rank = product(ortho_ref[...], jnp.concatenate([high, high, low], axis=0), 1, 0)
    out_ref[...] = (merged_ref[...] - low_rank).astype(bf16)


def ring_of(own):
    size = lax.axis_size("mp_0")
    chunks = {0: own}
    for back in range(1, size // 2 + 1):
        chunks[back] = lax.ppermute(
            chunks[back - 1], "mp_0", [(i, (i + 1) % size) for i in range(size)]
        )
        if back < size // 2:
            chunks[size - back] = lax.ppermute(
                chunks[(size - back + 1) % size], "mp_0", [(i, (i - 1) % size) for i in range(size)]
            )
    both = []
    for k in range(size):
        both += [chunks[k], lax.ppermute(chunks[k], "mp_1", [(0, 1), (1, 0)])]
    return both


def per_device(grad_out, hidden_act, carried, prior_right):
    own = carried[0]
    act = hidden_act.T
    features = own.shape[1]
    rank = prior_right.shape[1]
    replicas = lax.axis_size(DP)
    rows = own.shape[0] // 2
    tokens = hidden_act.shape[0]
    place = jnp.stack([lax.axis_index("mp_0"), lax.axis_index("mp_1")]).astype(jnp.int32)

    prior = jnp.concatenate(halves(prior_right), axis=1)
    proj = product(grad_out, prior, 1, 0)
    proj = jnp.concatenate(halves(proj[:, :rank] + proj[:, rank:]), axis=1)
    proj = sent_to_all(proj, MP).reshape(-1, 2 * rank)
    chunks = ring_of(grad_out)
    proj, chunks[2], chunks[14] = lax.optimization_barrier((proj, chunks[2], chunks[14]))
    left = product(own, prior, 1, 0) + product(hidden_act, proj, 0, 0)
    left = left[:, :rank] + left[:, rank:]
    left = jnp.concatenate([left[:rows], left[rows:]], axis=1).astype(bf16)
    parts = sent_to_all(left, DP)

    left, gram, right, act_left = call(
        left_kernel,
        (
            of((rows, 2 * rank), bf16),
            of((rank // 2, 2 * rank), f32),
            of((rank, features), f32),
            of((2 * rank, tokens), bf16),
        ),
        in_specs=[whole] * 3,
        out_specs=(whole,) * 4,
        name="left_sum",
    )(parts, own, act)

    scratch = [VMEM((tokens, features), bf16), pltpu.SemaphoreType.DMA((len(chunks),))]
    width = features // 4
    right = call(
        functools.partial(right_kernel, len(chunks)),
        of((16, rank // 4, width + 128), bf16),
        in_specs=[scalars, whole, whole, whole] + [anywhere] * len(chunks),
        out_specs=whole,
        scratch_shapes=scratch,
        name="right_product",
    )(place, act_left, right, gram, *chunks)

    merged = call(
        functools.partial(merged_kernel, len(chunks)),
        of(own.shape, f32),
        grid=(4,),
        in_specs=[scalars, whole, pl.BlockSpec((2 * rows, width), lambda j: (0, j))]
        + [anywhere] * len(chunks),
        out_specs=pl.BlockSpec((2 * rows, width), lambda j: (0, j)),
        scratch_shapes=scratch,
        name="merged",
    )(place, act, own, *chunks)

    for axis in (DP, MP):
        right = call(
            summed_kernel,
            of((16, rank // 4, width + 128), bf16),
            in_specs=[whole],
            out_specs=whole,
            name="summed",
        )(sent(right, axis))
    right = sent(right, DP).reshape(4, 4, rank // 4, width + 128)

    residual_out, next_right = call(
        functools.partial(residual_kernel, replicas),
        (of(own.shape, bf16), of((rank, features), f32)),
        grid=(4,),
        in_specs=[
            pl.BlockSpec((4, 4, rank // 4, 128), lambda j: (0, 0, 0, width // 128)),
            pl.BlockSpec((rows, 2 * rank), lambda j: (0, 0)),
            pl.BlockSpec((4, 1, rank // 4, width), lambda j: (0, j, 0, 0)),
            pl.BlockSpec((2 * rows, width), lambda j: (0, j)),
        ],
        out_specs=(
            pl.BlockSpec((2 * rows, width), lambda j: (0, j)),
            pl.BlockSpec((rank, width), lambda j: (0, j)),
        ),
        scratch_shapes=[VMEM((2 * rows, 3 * rank), bf16), VMEM((rank, rank), f32)],
        name="residual",
    )(right, left, right, merged)
    return (residual_out[None], next_right.T)


def solution(mesh):
    parted = Mesh(mesh.devices.reshape(4, 4, 8, 2), DP_MP)
    placed = (P(DP_MP, None), P(DP, MP), P(DP, MP, None), P())
    return jax.shard_map(
        per_device, mesh=parted, in_specs=placed, out_specs=(P(DP, MP, None), P()), check_vma=False
    )
```

time: 159 us -> 148 us (0.931)
  Pallas kernels: 0 us -> 35.3 us
  matrix products: 32.3 us -> 5.48 us
  other arithmetic: 16.7 us -> 1.74 us
  between operations: 14.9 us -> 0.93 us
  starting transfers between devices: 25.1 us -> 39 us
  waiting for transfers between devices: 31.3 us -> 21.1 us
  blocking collectives: 31.4 us -> 37.5 us
    pallas_call x0 -> x6, Pallas kernels: none -> 35.3 us  [the longest x1 13.6 us: per_device(): call(functools.partial(residual_kernel, replicas), (of(own.shape, bf16),...]
    all_to_all x5 -> x3, waiting for transfers between devices: 30.6 us -> 0.01 us  [sent(): return lax.all_to_all(array, axis, 0, 0, tiled=True)]
    dot_general x9 -> x3, matrix products: 30.4 us -> 5.48 us  [product(): lax.dot_general(left, right, (((left_dim,), (right_dim,)), ((), ())), pre...]
    ppermute x0 -> x15, waiting for transfers between devices: none -> 21.1 us  [the longest x4 12.2 us: ring_of(): lax.ppermute(chunks[back - 1], 'mp_0', [(i, (i + 1) % size) for i in rang...]
    ppermute x0 -> x15, starting transfers between devices: none -> 18.7 us  [the longest x8 10.3 us: ring_of(): both += [chunks[k], lax.ppermute(chunks[k], 'mp_1', [(0, 1), (1, 0)])]]
    another operation x6 -> x2, other arithmetic: 12.2 us -> 0.26 us  [the longest x3 6.52 us: inverse_factor(): factor = jnp.linalg.cholesky(gram_matrix + shift * identity)]
    all_to_all x1 -> x2, blocking collectives: 31.4 us -> 37.5 us  [sent(): return lax.all_to_all(array, axis, 0, 0, tiled=True)]
    all_to_all x5 -> x3, starting transfers between devices: 25.1 us -> 20.3 us  [sent(): return lax.all_to_all(array, axis, 0, 0, tiled=True)]
  transfers between devices with their start and end apart: 6 -> 18, of which waited for: 4 -> 5; matrix products, arithmetic and copies ran while one was open for 23% -> 2% of each run, Pallas kernels for 0% -> 11%
where the time goes in v2:
time: 148 us
  starting transfers between devices  39 us (26%)
  blocking collectives  37.5 us (25%)
  Pallas kernels  35.3 us (24%)
  waiting for transfers between devices  21.1 us (14%)
  local copies, waits for them, and re-layouts  6.65 us (4%)
  matrix products  5.48 us (4%)
  other arithmetic  1.74 us (1%)
    all_to_all x2, blocking collectives, sent(): return lax.all_to_all(array, axis, 0, 0, tiled=True)  37.5 us
    all_to_all x3, starting transfers between devices, sent(): return lax.all_to_all(array, axis, 0, 0, tiled=True)  20.3 us
    pallas_call x1, Pallas kernels, per_device(): call(functools.partial(residual_kernel, replicas), (of(own.shape, bf16),...  13.6 us
    pallas_call x1, Pallas kernels, per_device(): call(functools.partial(merged_kernel, len(chunks)), of(own.shape, f32), g...  12.6 us
    ppermute x4, waiting for transfers between devices, ring_of(): lax.ppermute(chunks[back - 1], 'mp_0', [(i, (i + 1) % size) for i in rang...  12.2 us
    ppermute x8, starting transfers between devices, ring_of(): both += [chunks[k], lax.ppermute(chunks[k], 'mp_1', [(0, 1), (1, 0)])]  10.3 us
    ppermute x3, waiting for transfers between devices, ring_of(): lax.ppermute(chunks[(size - back + 1) % size], 'mp_0', [(i, (i - 1) % siz...  8.85 us
    ppermute x3, starting transfers between devices, ring_of(): lax.ppermute(chunks[(size - back + 1) % size], 'mp_0', [(i, (i - 1) % siz...  7.71 us
  transfers between devices with their start and end apart: 18, of which 5 were waited for; matrix products, arithmetic and copies ran while one was open for 2% of the time, Pallas kernels for 11%

profile of v2, /device:TPU:1, one launch (start us, length us, event | category | flops | bytes accessed | tf_op | source)
XLA Modules:
  0.0 147.7 jit_solution(13866245908833650308)
XLA Ops:
  0.6 0.0 copy-start.1
  0.6 1.2 reduce-precision_convert_fusion
  1.9 1.3 convolution_bitcast_fusion
  3.2 0.1 reduce-precision_convert_fusion.1
  3.3 0.1 pad_maximum_fusion.4
  3.3 0.8 broadcast_in_dim.6
  4.1 10.0 %all-to-all-start = ((bf16[16,64,128]{2,1,0:T(8,128)(2,1)}), bf16[16,64,128]{2,1,0:T(8,128)(2,1)S(1)}, u32[]{:S(2)}, u32[]{:S(2)}) async-start(bf16[16,64,128]{2,1,0:T(8,128)(2,1)} %broadcast_in_dim.6), calls=%async_computation | async-start | bytes 524288 | tf_op jit(solution)/shard_map/all_to_all | solution.py:32
  14.1 0.0 copy-start
  14.1 2.7 %collective-permute-start.1 = (bf16[64,2560]{1,0:T(8,128)(2,1)S(1)}, bf16[64,2560]{1,0:T(8,128)(2,1)S(1)}, u32[]{:S(2)}, u32[]{:S(2)}) collective-permute-start(bf16[64,2560]{1,0:T(8,128)(2,1)S(1)} %copy-done.1), channel_id=1, source_target_pairs={{0,14},{2,0},{4,2},{6,4},{8,6},{10,8},{12,10},{14,12},{1,15},{3,1}... | collective-permute-start | bytes 983048 | tf_op jit(solution)/shard_map/ppermute | solution.py:223
  16.8 0.0 collective-permute-start
  16.8 3.5 %fusion.3 = f32[128,864]{0,1:T(8,128)S(1)} fusion(bf16[2560,64]{0,1:T(8,128)(2,1)S(1)} %get-tuple-element.21, bf16[2560,64]{0,1:T(8,128)(2,1)S(1)} %get-tuple-element.20, bf16[1,864,2560]{2,1,0:T(8,128)(2,1)} %param.6), kind=kOutput, calls=%fused_computation.9 | convolution fusion | flops 567541760 | bytes 5521408 | tf_op jit(solution)/shard_map/dot_general | solution.py:26
  20.3 8.8 %collective-permute-done.1.refs_18_.refs_17_ = bf16[64,2560]{1,0:T(8,128)(2,1)S(1)} collective-permute-done((bf16[64,2560]{1,0:T(8,128)(2,1)S(1)}, bf16[64,2560]{1,0:T(8,128)(2,1)S(1)}, u32[]{:S(2)}, u32[]{:S(2)}) %collective-permute-start.1) | collective-permute-done | bytes 327712 | tf_op jit(solution)/shard_map/ppermute | solution.py:223
  29.2 0.7 copy-done.4
  29.9 0.5 collective-permute-done.refs_6_.refs_5_
  30.4 0.0 all-to-all-done
  30.4 0.6 fusion
  31.0 0.2 fusion.2
  31.2 0.1 pad_maximum_fusion.3
  31.4 1.4 broadcast_in_dim.7
  32.8 6.7 %all-to-all-start.1 = ((bf16[16,432,128]{2,1,0:T(8,128)(2,1)}), bf16[16,432,128]{2,1,0:T(8,128)(2,1)S(1)}, u32[]{:S(2)}, u32[]{:S(2)}) async-start(bf16[16,432,128]{2,1,0:T(8,128)(2,1)} %broadcast_in_dim.7), calls=%async_computation.1 | async-start | bytes 3538944 | tf_op jit(solution)/shard_map/all_to_all | solution.py:32
  39.5 0.7 collective-permute-start.4
  40.2 2.1 %collective-permute-start.10 = (bf16[64,2560]{1,0:T(8,128)(2,1)}, bf16[64,2560]{1,0:T(8,128)(2,1)}, u32[]{:S(2)}, u32[]{:S(2)}) collective-permute-start(bf16[64,2560]{1,0:T(8,128)(2,1)} %copy-done.4), channel_id=1, source_target_pairs={{0,14},{2,0},{4,2},{6,4},{8,6},{10,8},{12,10},{14,12},{1,15},{3,1}... | collective-permute-start | bytes 983048 | tf_op jit(solution)/shard_map/ppermute | solution.py:223
  42.3 6.9 %collective-permute-done.4.refs_8_.refs_7_ = bf16[64,2560]{1,0:T(8,128)(2,1)} collective-permute-done((bf16[64,2560]{1,0:T(8,128)(2,1)}, bf16[64,2560]{1,0:T(8,128)(2,1)}, u32[]{:S(2)}, u32[]{:S(2)}) %collective-permute-start.4) | collective-permute-done | bytes 327712 | tf_op jit(solution)/shard_map/ppermute | solution.py:219
  49.2 0.0 collective-permute-start.6
  49.2 2.1 %collective-permute-start.2 = (bf16[64,2560]{1,0:T(8,128)(2,1)}, bf16[64,2560]{1,0:T(8,128)(2,1)S(1)}, u32[]{:S(2)}, u32[]{:S(2)}) collective-permute-start(bf16[64,2560]{1,0:T(8,128)(2,1)} %refs_3_.1), channel_id=1, source_target_pairs={{0,1},{1,0},{2,3},{3,2},{4,5},{5,4},{6,7},{7,6},{8,9},{9,8},{10,11... | collective-permute-start | bytes 983048 | tf_op jit(solution)/shard_map/ppermute | solution.py:228
  51.3 0.0 collective-permute-start.14
  51.3 0.5 collective-permute-start.3
  51.8 0.0 collective-permute-done.10.refs_16_.refs_15_
  51.8 3.0 %collective-permute-start.11 = (bf16[64,2560]{1,0:T(8,128)(2,1)}, bf16[64,2560]{1,0:T(8,128)(2,1)}, u32[]{:S(2)}, u32[]{:S(2)}) collective-permute-start(bf16[64,2560]{1,0:T(8,128)(2,1)} %collective-permute-done.10.refs_16_.refs_15_), channel_id=1, source_target_pairs={{0,14},{2,0},{4,2},{6,4},{8,6},{10,8},{12,10},{14,12},{1,15},{3,1}... | collective-permute-start | bytes 983048 | tf_op jit(solution)/shard_map/ppermute | solution.py:223
  54.7 3.1 %collective-permute-done.6.refs_10_.refs_9_ = bf16[64,2560]{1,0:T(8,128)(2,1)} collective-permute-done((bf16[64,2560]{1,0:T(8,128)(2,1)}, bf16[64,2560]{1,0:T(8,128)(2,1)}, u32[]{:S(2)}, u32[]{:S(2)}) %collective-permute-start.6) | collective-permute-done | bytes 327712 | tf_op jit(solution)/shard_map/ppermute | solution.py:219
  57.8 0.0 collective-permute-start.8
  57.9 0.0 collective-permute-done.2.refs_5_.refs_4_
  57.9 0.7 copy-done.7
  58.6 3.0 %collective-permute-start.13 = (bf16[64,2560]{1,0:T(8,128)(2,1)}, bf16[64,2560]{1,0:T(8,128)(2,1)}, u32[]{:S(2)}, u32[]{:S(2)}) collective-permute-start(bf16[64,2560]{1,0:T(8,128)(2,1)} %collective-permute-done.10.refs_16_.refs_15_), channel_id=1, source_target_pairs={{0,1},{1,0},{2,3},{3,2},{4,5},{5,4},{6,7},{7,6},{8,9},{9,8},{10,11... | collective-permute-start | bytes 983048 | tf_op jit(solution)/shard_map/ppermute | solution.py:228
  61.6 0.0 collective-permute-done.14.refs_19_.refs_18_
  61.6 0.7 copy-done.10
  62.3 0.0 collective-permute-start.5
  62.3 0.0 collective-permute-done.3.refs_7_.refs_6_
  62.3 0.7 copy-done.13
  63.1 0.5 collective-permute-start.7
  63.6 0.0 collective-permute-done.11.refs_14_.refs_13_
  63.6 0.0 collective-permute-start.12
  63.6 1.7 %collective-permute-done.8.refs_12_.refs_11_ = bf16[64,2560]{1,0:T(8,128)(2,1)} collective-permute-done((bf16[64,2560]{1,0:T(8,128)(2,1)}, bf16[64,2560]{1,0:T(8,128)(2,1)}, u32[]{:S(2)}, u32[]{:S(2)}) %collective-permute-start.8) | collective-permute-done | bytes 327712 | tf_op jit(solution)/shard_map/ppermute | solution.py:219
  65.3 4.2 %collective-permute-start.9 = (bf16[64,2560]{1,0:T(8,128)(2,1)}, bf16[64,2560]{1,0:T(8,128)(2,1)}, u32[]{:S(2)}, u32[]{:S(2)}) collective-permute-start(bf16[64,2560]{1,0:T(8,128)(2,1)} %collective-permute-done.8.refs_12_.refs_11_), channel_id=1, source_target_pairs={{0,1},{1,0},{2,3},{3,2},{4,5},{5,4},{6,7},{7,6},{8,9},{9,8},{10,11... | collective-permute-start | bytes 983048 | tf_op jit(solution)/shard_map/ppermute | solution.py:228
  69.5 0.1 pad_add_fusion.refs_0_
  69.6 0.0 all-to-all-done.1.parts_ref
  69.6 3.9 %left_sum.1 = (bf16[432,128]{1,0:T(8,128)(2,1)S(1)}, f32[32,128]{1,0:T(8,128)S(1)}, f32[64,2560]{1,0:T(8,128)S(1)}, bf16[128,1024]{1,0:T(8,128)(2,1)S(1)}) custom-call(bf16[16,432,128]{2,1,0:T(8,128)(2,1)S(1)} %all-to-all-done.1.parts_ref, bf16[864,2560]{1,0:T(8,128)(2,1)} %bitcast.21, bf16[864,1024]{1,0:T(8,128)(2,1)S(1)} %bitcast.18), custom_call_target="tpu_custom_call" | custom-call | tf_op jit(solution)/shard_map/left_sum/pallas_call | solution.py:253
  73.5 0.0 copy-start.16
  73.5 0.8 copy-done.16
  74.4 0.6 copy-done.17
  75.0 0.0 collective-permute-done.13.refs_17_.refs_16_
  75.0 0.0 collective-permute-done.5.refs_9_.refs_8_
  75.0 0.0 collective-permute-done.12.refs_15_.refs_14_
  75.0 0.0 collective-permute-done.7.refs_11_.refs_10_
  75.1 4.4 %right_product.1 = bf16[16,16,768]{2,1,0:T(8,128)(2,1)S(1)} custom-call(s32[2]{0:T(128)S(1)} %pad_add_fusion.refs_0_, bf16[128,1024]{1,0:T(8,128)(2,1)S(1)} %get-tuple-element.12.refs_1_, f32[64,2560]{1,0:T(8,128)} %copy-done.16, f32[32,128]{1,0:T(8,128)S(1)} %get-tuple-element.14.refs_3_, bf16[64,2560]{1,0:T(8,128)(2,1)S(1)} %copy-done.2, ...), custom_call_target="tpu_custom_call" | custom-call | tf_op jit(solution)/shard_map/right_product/pallas_call | solution.py:268
  79.5 15.1 %all_to_all.25.parts_ref = bf16[16,16,768]{2,1,0:T(8,128)(2,1)S(1)} all-to-all(bf16[16,16,768]{2,1,0:T(8,128)(2,1)S(1)} %right_product.1), channel_id=1, replica_groups=mesh['dp_0'=4,'dp_1'=4,'mp_0'=8,'mp_1'=2] {'dp_0','dp_1'}, dimensions={0} | all-to-all | bytes 786432 | tf_op jit(solution)/shard_map/all_to_all | solution.py:32
  94.6 0.1 summed.2
  94.7 22.4 %all_to_all.26.parts_ref = bf16[16,16,768]{2,1,0:T(8,128)(2,1)S(1)} all-to-all(bf16[16,16,768]{2,1,0:T(8,128)(2,1)S(1)} %summed.2), channel_id=1, replica_groups=mesh['dp_0'=4,'dp_1'=4,'mp_0'=8,'mp_1'=2] {'mp_0','mp_1'}, dimensions={0} | all-to-all | bytes 786432 | tf_op jit(solution)/shard_map/all_to_all | solution.py:32
  117.0 0.8 summed.3
  117.9 3.6 %all-to-all-start.4 = ((bf16[16,16,768]{2,1,0:T(8,128)(2,1)}), bf16[16,16,768]{2,1,0:T(8,128)(2,1)S(1)}, u32[]{:S(2)}, u32[]{:S(2)}) async-start(bf16[16,16,768]{2,1,0:T(8,128)(2,1)} %summed.3), calls=%async_computation.4 | async-start | bytes 786432 | tf_op jit(solution)/shard_map/all_to_all | solution.py:32
  121.5 0.0 copy-start.18
  121.5 12.6 %merged.1.merged_ref = f32[864,2560]{1,0:T(8,128)} custom-call(s32[2]{0:T(128)S(1)} %pad_add_fusion.refs_0_, bf16[864,1024]{1,0:T(8,128)(2,1)} %bitcast.17, bf16[864,2560]{1,0:T(8,128)(2,1)} %bitcast.22, bf16[64,2560]{1,0:T(8,128)(2,1)S(1)} %copy-done.3, bf16[64,2560]{1,0:T(8,128)(2,1)S(1)} %copy-done.9, ...), custom_call_target="tpu_custom_call" | custom-call | tf_op jit(solution)/shard_map/merged/pallas_call | solution.py:277
  134.1 0.0 all-to-all-done.4
  134.1 13.6 %residual.1 = (bf16[864,2560]{1,0:T(8,128)(2,1)}, f32[64,2560]{1,0:T(8,128)}) custom-call(bf16[4,4,16,768]{3,2,1,0:T(8,128)(2,1)S(1)} %bitcast.19, bf16[432,128]{1,0:T(8,128)(2,1)S(1)} %copy-done.18, bf16[4,4,16,768]{3,2,1,0:T(8,128)(2,1)S(1)} %bitcast.20, f32[864,2560]{1,0:T(8,128)} %merged.1.merged_ref), custom_call_target="tpu_custom_call" | custom-call | tf_op jit(solution)/shard_map/residual/pallas_call | solution.py:298
  (30 shorter events, 0.1 us)
Async XLA Ops:
  0.6 13.5 %copy-start.1 = (bf16[64,2560]{1,0:T(8,128)(2,1)S(1)}, bf16[64,2560]{1,0:T(8,128)(2,1)}, u32[]{:S(2)}) copy-start(bf16[64,2560]{1,0:T(8,128)(2,1)} %refs_3_.1) | copy-start | bytes 983044
  4.1 26.3 %all-to-all-start = ((bf16[16,64,128]{2,1,0:T(8,128)(2,1)}), bf16[16,64,128]{2,1,0:T(8,128)(2,1)S(1)}, u32[]{:S(2)}, u32[]{:S(2)}) async-start(bf16[16,64,128]{2,1,0:T(8,128)(2,1)} %broadcast_in_dim.6), calls=%async_computation | async-start | bytes 524288 | tf_op jit(solution)/shard_map/all_to_all | solution.py:32
  14.1 16.3 %copy-start = (bf16[1024,864]{0,1:T(8,128)(2,1)S(1)}, bf16[1024,864]{0,1:T(8,128)(2,1)}, u32[]{:S(2)}) copy-start(bf16[1024,864]{0,1:T(8,128)(2,1)} %param.5) | copy-start | bytes 5308420
  14.1 15.1 %collective-permute-start.1 = (bf16[64,2560]{1,0:T(8,128)(2,1)S(1)}, bf16[64,2560]{1,0:T(8,128)(2,1)S(1)}, u32[]{:S(2)}, u32[]{:S(2)}) collective-permute-start(bf16[64,2560]{1,0:T(8,128)(2,1)S(1)} %copy-done.1), channel_id=1, source_target_pairs={{0,14},{2,0},{4,2},{6,4},{8,6},{10,8},{12,10},{14,12},{1,15},{3,1}... | collective-permute-start | bytes 983048 | tf_op jit(solution)/shard_map/ppermute | solution.py:223
  16.8 13.6 %collective-permute-start = (bf16[64,2560]{1,0:T(8,128)(2,1)S(1)}, bf16[64,2560]{1,0:T(8,128)(2,1)}, u32[]{:S(2)}, u32[]{:S(2)}) collective-permute-start(bf16[64,2560]{1,0:T(8,128)(2,1)S(1)} %copy-done.1), channel_id=1, source_target_pairs={{0,2},{2,4},{4,6},{6,8},{8,10},{10,12},{12,14},{14,0},{1,3},{3,5},... | collective-permute-start | bytes 983048 | tf_op jit(solution)/shard_map/ppermute | solution.py:219
  29.2 0.7 copy-start.4
  32.8 36.8 %all-to-all-start.1 = ((bf16[16,432,128]{2,1,0:T(8,128)(2,1)}), bf16[16,432,128]{2,1,0:T(8,128)(2,1)S(1)}, u32[]{:S(2)}, u32[]{:S(2)}) async-start(bf16[16,432,128]{2,1,0:T(8,128)(2,1)} %broadcast_in_dim.7), calls=%async_computation.1 | async-start | bytes 3538944 | tf_op jit(solution)/shard_map/all_to_all | solution.py:32
  39.5 9.7 %collective-permute-start.4 = (bf16[64,2560]{1,0:T(8,128)(2,1)}, bf16[64,2560]{1,0:T(8,128)(2,1)}, u32[]{:S(2)}, u32[]{:S(2)}) collective-permute-start(bf16[64,2560]{1,0:T(8,128)(2,1)} %collective-permute-done.refs_6_.refs_5_), channel_id=1, source_target_pairs={{0,2},{2,4},{4,6},{6,8},{8,10},{10,12},{12,14},{14,0},{1,3},{3,5},... | collective-permute-start | bytes 983048 | tf_op jit(solution)/shard_map/ppermute | solution.py:219
  40.2 11.6 %collective-permute-start.10 = (bf16[64,2560]{1,0:T(8,128)(2,1)}, bf16[64,2560]{1,0:T(8,128)(2,1)}, u32[]{:S(2)}, u32[]{:S(2)}) collective-permute-start(bf16[64,2560]{1,0:T(8,128)(2,1)} %copy-done.4), channel_id=1, source_target_pairs={{0,14},{2,0},{4,2},{6,4},{8,6},{10,8},{12,10},{14,12},{1,15},{3,1}... | collective-permute-start | bytes 983048 | tf_op jit(solution)/shard_map/ppermute | solution.py:223
  49.2 8.7 %collective-permute-start.6 = (bf16[64,2560]{1,0:T(8,128)(2,1)}, bf16[64,2560]{1,0:T(8,128)(2,1)}, u32[]{:S(2)}, u32[]{:S(2)}) collective-permute-start(bf16[64,2560]{1,0:T(8,128)(2,1)} %collective-permute-done.4.refs_8_.refs_7_), channel_id=1, source_target_pairs={{0,2},{2,4},{4,6},{6,8},{8,10},{10,12},{12,14},{14,0},{1,3},{3,5},... | collective-permute-start | bytes 983048 | tf_op jit(solution)/shard_map/ppermute | solution.py:219
  49.2 8.7 %collective-permute-start.2 = (bf16[64,2560]{1,0:T(8,128)(2,1)}, bf16[64,2560]{1,0:T(8,128)(2,1)S(1)}, u32[]{:S(2)}, u32[]{:S(2)}) collective-permute-start(bf16[64,2560]{1,0:T(8,128)(2,1)} %refs_3_.1), channel_id=1, source_target_pairs={{0,1},{1,0},{2,3},{3,2},{4,5},{5,4},{6,7},{7,6},{8,9},{9,8},{10,11... | collective-permute-start | bytes 983048 | tf_op jit(solution)/shard_map/ppermute | solution.py:228
  51.3 10.3 %collective-permute-start.14 = (bf16[64,2560]{1,0:T(8,128)(2,1)}, bf16[64,2560]{1,0:T(8,128)(2,1)S(1)}, u32[]{:S(2)}, u32[]{:S(2)}) collective-permute-start(bf16[64,2560]{1,0:T(8,128)(2,1)} %copy-done.4), channel_id=1, source_target_pairs={{0,1},{1,0},{2,3},{3,2},{4,5},{5,4},{6,7},{7,6},{8,9},{9,8},{10,11... | collective-permute-start | bytes 983048 | tf_op jit(solution)/shard_map/ppermute | solution.py:228
  51.3 11.0 %collective-permute-start.3 = (bf16[64,2560]{1,0:T(8,128)(2,1)}, bf16[64,2560]{1,0:T(8,128)(2,1)S(1)}, u32[]{:S(2)}, u32[]{:S(2)}) collective-permute-start(bf16[64,2560]{1,0:T(8,128)(2,1)} %collective-permute-done.refs_6_.refs_5_), channel_id=1, source_target_pairs={{0,1},{1,0},{2,3},{3,2},{4,5},{5,4},{6,7},{7,6},{8,9},{9,8},{10,11... | collective-permute-start | bytes 983048 | tf_op jit(solution)/shard_map/ppermute | solution.py:228
  51.8 11.8 %collective-permute-start.11 = (bf16[64,2560]{1,0:T(8,128)(2,1)}, bf16[64,2560]{1,0:T(8,128)(2,1)}, u32[]{:S(2)}, u32[]{:S(2)}) collective-permute-start(bf16[64,2560]{1,0:T(8,128)(2,1)} %collective-permute-done.10.refs_16_.refs_15_), channel_id=1, source_target_pairs={{0,14},{2,0},{4,2},{6,4},{8,6},{10,8},{12,10},{14,12},{1,15},{3,1}... | collective-permute-start | bytes 983048 | tf_op jit(solution)/shard_map/ppermute | solution.py:223
  57.8 7.5 %collective-permute-start.8 = (bf16[64,2560]{1,0:T(8,128)(2,1)}, bf16[64,2560]{1,0:T(8,128)(2,1)}, u32[]{:S(2)}, u32[]{:S(2)}) collective-permute-start(bf16[64,2560]{1,0:T(8,128)(2,1)} %collective-permute-done.6.refs_10_.refs_9_), channel_id=1, source_target_pairs={{0,2},{2,4},{4,6},{6,8},{8,10},{10,12},{12,14},{14,0},{1,3},{3,5},... | collective-permute-start | bytes 983048 | tf_op jit(solution)/shard_map/ppermute | solution.py:219
  57.9 0.7 copy-start.7
  58.6 16.4 %collective-permute-start.13 = (bf16[64,2560]{1,0:T(8,128)(2,1)}, bf16[64,2560]{1,0:T(8,128)(2,1)}, u32[]{:S(2)}, u32[]{:S(2)}) collective-permute-start(bf16[64,2560]{1,0:T(8,128)(2,1)} %collective-permute-done.10.refs_16_.refs_15_), channel_id=1, source_target_pairs={{0,1},{1,0},{2,3},{3,2},{4,5},{5,4},{6,7},{7,6},{8,9},{9,8},{10,11... | collective-permute-start | bytes 983048 | tf_op jit(solution)/shard_map/ppermute | solution.py:228
  61.6 0.7 copy-start.10
  62.3 12.7 %collective-permute-start.5 = (bf16[64,2560]{1,0:T(8,128)(2,1)}, bf16[64,2560]{1,0:T(8,128)(2,1)}, u32[]{:S(2)}, u32[]{:S(2)}) collective-permute-start(bf16[64,2560]{1,0:T(8,128)(2,1)} %collective-permute-done.4.refs_8_.refs_7_), channel_id=1, source_target_pairs={{0,1},{1,0},{2,3},{3,2},{4,5},{5,4},{6,7},{7,6},{8,9},{9,8},{10,11... | collective-permute-start | bytes 983048 | tf_op jit(solution)/shard_map/ppermute | solution.py:228
  62.3 0.7 copy-start.13
  63.1 12.0 %collective-permute-start.7 = (bf16[64,2560]{1,0:T(8,128)(2,1)}, bf16[64,2560]{1,0:T(8,128)(2,1)}, u32[]{:S(2)}, u32[]{:S(2)}) collective-permute-start(bf16[64,2560]{1,0:T(8,128)(2,1)} %collective-permute-done.6.refs_10_.refs_9_), channel_id=1, source_target_pairs={{0,1},{1,0},{2,3},{3,2},{4,5},{5,4},{6,7},{7,6},{8,9},{9,8},{10,11... | collective-permute-start | bytes 983048 | tf_op jit(solution)/shard_map/ppermute | solution.py:228
  63.6 11.4 %collective-permute-start.12 = (bf16[64,2560]{1,0:T(8,128)(2,1)}, bf16[64,2560]{1,0:T(8,128)(2,1)}, u32[]{:S(2)}, u32[]{:S(2)}) collective-permute-start(bf16[64,2560]{1,0:T(8,128)(2,1)} %collective-permute-done.11.refs_14_.refs_13_), channel_id=1, source_target_pairs={{0,1},{1,0},{2,3},{3,2},{4,5},{5,4},{6,7},{7,6},{8,9},{9,8},{10,11... | collective-permute-start | bytes 983048 | tf_op jit(solution)/shard_map/ppermute | solution.py:228
  65.3 9.7 %collective-permute-start.9 = (bf16[64,2560]{1,0:T(8,128)(2,1)}, bf16[64,2560]{1,0:T(8,128)(2,1)}, u32[]{:S(2)}, u32[]{:S(2)}) collective-permute-start(bf16[64,2560]{1,0:T(8,128)(2,1)} %collective-permute-done.8.refs_12_.refs_11_), channel_id=1, source_target_pairs={{0,1},{1,0},{2,3},{3,2},{4,5},{5,4},{6,7},{7,6},{8,9},{9,8},{10,11... | collective-permute-start | bytes 983048 | tf_op jit(solution)/shard_map/ppermute | solution.py:228
  69.6 5.5 %copy-start.2 = (bf16[64,2560]{1,0:T(8,128)(2,1)S(1)}, bf16[64,2560]{1,0:T(8,128)(2,1)}, u32[]{:S(2)}) copy-start(bf16[64,2560]{1,0:T(8,128)(2,1)} %refs_3_.1) | copy-start | bytes 983044
  69.6 5.5 %copy-start.5 = (bf16[64,2560]{1,0:T(8,128)(2,1)S(1)}, bf16[64,2560]{1,0:T(8,128)(2,1)}, u32[]{:S(2)}) copy-start(bf16[64,2560]{1,0:T(8,128)(2,1)} %copy-done.4) | copy-start | bytes 983044
  69.6 5.5 %copy-start.8 = (bf16[64,2560]{1,0:T(8,128)(2,1)S(1)}, bf16[64,2560]{1,0:T(8,128)(2,1)}, u32[]{:S(2)}) copy-start(bf16[64,2560]{1,0:T(8,128)(2,1)} %copy-done.7) | copy-start | bytes 983044
  69.6 5.5 %copy-start.11 = (bf16[64,2560]{1,0:T(8,128)(2,1)S(1)}, bf16[64,2560]{1,0:T(8,128)(2,1)}, u32[]{:S(2)}) copy-start(bf16[64,2560]{1,0:T(8,128)(2,1)} %copy-done.10) | copy-start | bytes 983044
  69.6 5.5 %copy-start.14 = (bf16[64,2560]{1,0:T(8,128)(2,1)S(1)}, bf16[64,2560]{1,0:T(8,128)(2,1)}, u32[]{:S(2)}) copy-start(bf16[64,2560]{1,0:T(8,128)(2,1)} %copy-done.13) | copy-start | bytes 983044
  73.5 0.8 copy-start.16
  74.4 0.6 copy-start.17
  94.6 26.8 %copy-start.3 = (bf16[64,2560]{1,0:T(8,128)(2,1)S(1)}, bf16[64,2560]{1,0:T(8,128)(2,1)}, u32[]{:S(2)}) copy-start(bf16[64,2560]{1,0:T(8,128)(2,1)} %refs_3_.1) | copy-start | bytes 983044
  94.6 26.8 %copy-start.6 = (bf16[64,2560]{1,0:T(8,128)(2,1)S(1)}, bf16[64,2560]{1,0:T(8,128)(2,1)}, u32[]{:S(2)}) copy-start(bf16[64,2560]{1,0:T(8,128)(2,1)} %copy-done.4) | copy-start | bytes 983044
  94.6 26.8 %copy-start.9 = (bf16[64,2560]{1,0:T(8,128)(2,1)S(1)}, bf16[64,2560]{1,0:T(8,128)(2,1)}, u32[]{:S(2)}) copy-start(bf16[64,2560]{1,0:T(8,128)(2,1)} %copy-done.7) | copy-start | bytes 983044
  94.6 26.9 %copy-start.12 = (bf16[64,2560]{1,0:T(8,128)(2,1)S(1)}, bf16[64,2560]{1,0:T(8,128)(2,1)}, u32[]{:S(2)}) copy-start(bf16[64,2560]{1,0:T(8,128)(2,1)} %copy-done.10) | copy-start | bytes 983044
  94.6 26.9 %copy-start.15 = (bf16[64,2560]{1,0:T(8,128)(2,1)S(1)}, bf16[64,2560]{1,0:T(8,128)(2,1)}, u32[]{:S(2)}) copy-start(bf16[64,2560]{1,0:T(8,128)(2,1)} %copy-done.13) | copy-start | bytes 983044
  117.9 16.2 %all-to-all-start.4 = ((bf16[16,16,768]{2,1,0:T(8,128)(2,1)}), bf16[16,16,768]{2,1,0:T(8,128)(2,1)S(1)}, u32[]{:S(2)}, u32[]{:S(2)}) async-start(bf16[16,16,768]{2,1,0:T(8,128)(2,1)} %summed.3), calls=%async_computation.4 | async-start | bytes 786432 | tf_op jit(solution)/shard_map/all_to_all | solution.py:32
  121.5 12.6 %copy-start.18 = (bf16[432,128]{1,0:T(8,128)(2,1)S(1)}, bf16[432,128]{1,0:T(8,128)(2,1)}, u32[]{:S(2)}) copy-start(bf16[432,128]{1,0:T(8,128)(2,1)} %copy-done.17) | copy-start | bytes 331780

commit v3 on v2

v3 whole, which is shorter than its diff:
```python
import functools

import jax
import jax.numpy as jnp
from jax import lax
from jax.experimental import pallas as pl
from jax.experimental.pallas import tpu as pltpu
from jax.sharding import Mesh
from jax.sharding import PartitionSpec as P

MP = ("mp_0", "mp_1")
DP = ("dp_0", "dp_1")
DP_MP = ("dp_0", "dp_1", "mp_0", "mp_1")

bf16 = jnp.bfloat16
f32 = jnp.float32
highest = lax.Precision.HIGHEST
VMEM = pltpu.VMEM
whole = pl.BlockSpec(memory_space=pltpu.VMEM)
anywhere = pl.BlockSpec(memory_space=pl.ANY)
in_hbm = pl.BlockSpec(memory_space=pltpu.HBM)
scalars = pl.BlockSpec(memory_space=pltpu.SMEM)
MIB = 1024 * 1024


def product(left, right, left_dim, right_dim):
    return lax.dot_general(
        left, right, (((left_dim,), (right_dim,)), ((), ())), preferred_element_type=f32
    )


def sent(array, axis):
    return lax.all_to_all(array, axis, 0, 0, tiled=True)


def sent_to_all(array, axis):
    devices = lax.axis_size(axis)
    return sent(jnp.broadcast_to(array[None], (devices, *array.shape)), axis)


def halves(array):
    high = lax.reduce_precision(array, 8, 7)
    return high.astype(bf16), (array - high).astype(bf16)


def split(array):
    high = array.astype(bf16)
    return high, (array - high.astype(f32)).astype(bf16)


def call(kernel, out_shape, limit=8, **options):
    return pl.pallas_call(
        kernel,
        out_shape=out_shape,
        compiler_params=pltpu.CompilerParams(vmem_limit_bytes=limit * MIB),
        **options,
    )


def of(shape, kind):
    return jax.ShapeDtypeStruct(shape, kind)


def chunk_copies(place_ref, chunk_refs, half_ref, sems):
    steps = len(chunk_refs)
    tokens = chunk_refs[0].shape[0]
    copies = []
    for k, chunk_ref in enumerate(chunk_refs):
        row = lax.rem(place_ref[0] + (steps - k), steps) * tokens
        copies.append(
            pltpu.make_async_copy(
                chunk_ref, half_ref.at[pl.ds(pl.multiple_of(row, tokens), tokens), :], sems.at[k]
            )
        )
    return copies


def in_terms(array):
    high, low = split(array)
    least = (array - high.astype(f32) - low.astype(f32)).astype(bf16)
    return jnp.concatenate([high, low, least], axis=1)


def left_kernel(
    place_ref, parts_ref, act_hbm, own_hbm, left_ref, gram_ref, keep_ref, give_ref, right_ref,
    act_ref, own_ref, sems,
):
    act_copy = pltpu.make_async_copy(act_hbm, act_ref, sems.at[0])
    own_copy = pltpu.make_async_copy(own_hbm, own_ref, sems.at[1])
    act_copy.start()
    own_copy.start()
    rows, lanes = left_ref.shape
    rank = lanes // 2
    left = total_of(parts_ref).astype(bf16)
    left_ref[...] = left
    turned = left.astype(f32).T.astype(bf16)
    gram = product(left, left, 0, 0)
    gram = gram[:rank, :rank] + gram[rank:, rank:]
    gram_ref[...] = jnp.concatenate([gram[: rank // 2], gram[rank // 2 :]], axis=1)
    upper, lower = turned[:rank], turned[rank:]
    act_copy.wait()
    act_left = product(upper, act_ref[:rows], 1, 0) + product(lower, act_ref[rows:], 1, 0)
    act_left = jnp.concatenate(split(act_left.T), axis=1)
    first = place_ref[1] == 0
    tokens = 64
    for z in range(act_left.shape[0] // (2 * tokens)):
        near = act_left[2 * z * tokens : (2 * z + 1) * tokens]
        far = act_left[(2 * z + 1) * tokens : (2 * z + 2) * tokens]
        keep_ref[z * tokens : (z + 1) * tokens, :] = jnp.where(first, near, far)
        give_ref[z * tokens : (z + 1) * tokens, :] = jnp.where(first, far, near)
    own_copy.wait()
    right_ref[...] = product(upper, own_ref[:rows], 1, 0) + product(lower, own_ref[rows:], 1, 0)


def right_kernel(count, *refs):
    place_ref, keep_ref, other_ref, right_ref = refs[:4]
    chunk_refs = refs[4 : 4 + count]
    out_ref, half_hbm, half_ref, sems = refs[4 + count :]
    copies = chunk_copies(place_ref, chunk_refs, half_ref, sems)
    for copy in copies:
        copy.start()
    rank = right_ref.shape[0]
    both = keep_ref[...].astype(f32) + other_ref[...].astype(f32)
    both = jnp.concatenate(split((both[:, :rank] + both[:, rank:]).T), axis=0)
    for copy in copies:
        copy.wait()
    half_copy = pltpu.make_async_copy(half_ref, half_hbm, sems.at[count])
    half_copy.start()
    both = product(both, half_ref[...], 1, 0)
    right = (right_ref[...] + both[:rank] + both[rank:]).astype(bf16)
    height, width = out_ref.shape[1:]
    for a in range(4):
        for b in range(4):
            out_ref[4 * a + b] = right[a * height : (a + 1) * height, b * width : (b + 1) * width]
    half_copy.wait()


def merged_kernel(place_ref, act_ref, own_ref, half_ref, other_ref, out_ref, full_ref):
    tokens = 64
    for z in range(half_ref.shape[0] // tokens):
        rows = slice(z * tokens, (z + 1) * tokens)
        for ref, near in ((half_ref, place_ref[1]), (other_ref, 1 - place_ref[1])):
            row = pl.multiple_of((2 * z + near) * tokens, tokens)
            full_ref[pl.ds(row, tokens), :] = ref[rows, :]
    out_ref[...] = own_ref[...].astype(f32) + product(act_ref[...], full_ref[...], 1, 0)


def total_of(parts_ref):
    total = parts_ref[0].astype(f32)
    for i in range(1, parts_ref.shape[0]):
        total = total + parts_ref[i].astype(f32)
    return total


def replica_sum_kernel(parts_ref, out_ref):
    out_ref[...] = total_of(parts_ref).astype(bf16)


def core_sum_kernel(place_ref, own_ref, other_ref, gram_ref, other_gram_ref, out_ref):
    right = (own_ref[...].astype(f32) + other_ref[...].astype(f32)).astype(bf16)
    gram = gram_ref[...] + other_gram_ref[...]
    height = gram.shape[0] // 2
    gram = jnp.where(place_ref[1] == 0, gram[:height], gram[height:])
    sent_on = jnp.concatenate([right, in_terms(gram)], axis=1)
    for i in range(out_ref.shape[0]):
        out_ref[i] = sent_on


def chip_sum_kernel(parts_ref, out_ref, gram_ref):
    total = total_of(parts_ref)
    width = out_ref.shape[2]
    right = total[:, :width].astype(bf16)
    for i in range(out_ref.shape[0]):
        out_ref[i] = right
    terms = [total[:, width + 128 * i : width + 128 * (i + 1)] for i in range(3)]
    gram_ref[...] = terms[0] + terms[1] + terms[2]


def inverse_of(gram):
    rank = gram.shape[0]
    row = lax.broadcasted_iota(jnp.int32, (rank, rank), 0)
    column = lax.broadcasted_iota(jnp.int32, (rank, rank), 1)
    diagonal = row == column
    trace = jnp.sum(jnp.where(diagonal, gram, 0.0), keepdims=True)
    gram = gram + jnp.where(diagonal, 0.001 * (trace / rank), 0.0)
    work = jnp.concatenate([gram, jnp.where(diagonal, 1.0, 0.0)], axis=1)
    rows = lax.broadcasted_iota(jnp.int32, (rank, 1), 0)
    group = 4
    for first in range(0, rank, group):
        columns = [
            jnp.broadcast_to(work[:, k : k + 1], work.shape) for k in range(first, first + group)
        ]
        lines = [work[k : k + 1, :] for k in range(first, first + group)]
        for i in range(group):
            k = first + i
            factor = columns[i] * (1.0 / columns[i][k : k + 1, :])
            factor = jnp.where(rows > k, factor, 0.0)
            for j in range(i + 1, group):
                columns[j] = columns[j] - factor * columns[j][k : k + 1, :]
                lines[j] = lines[j] - factor[first + j : first + j + 1, :] * lines[i]
            work = work - factor * lines[i]
    pivots = jnp.sum(jnp.where(diagonal, work[:, :rank], 0.0), axis=1, keepdims=True)
    return work[:, rank:] * lax.rsqrt(pivots)


def inverse_kernel(place_ref, gram_ref, other_ref, out_ref):
    own, other = gram_ref[...], other_ref[...]
    first = place_ref[1] == 0
    upper, lower = jnp.where(first, own, other), jnp.where(first, other, own)
    rank = out_ref.shape[0]
    gram = jnp.concatenate([upper[:, :rank], lower[:, :rank], upper[:, rank:], lower[:, rank:]], axis=0)
    out_ref[...] = inverse_of(gram)


def residual_kernel(
    replicas, inverse_ref, left_ref, right_ref, merged_ref, out_ref, next_ref, ortho_ref
):
    rows = left_ref.shape[0]
    rank = inverse_ref.shape[0]

    @pl.when(pl.program_id(0) == 0)
    def _():
        left = left_ref[...]
        inverse = inverse_ref[...]
        high, low = split(inverse)
        least = (inverse - high.astype(f32) - low.astype(f32)).astype(bf16)
        for i in range(2):
            part = left[:, i * rank : (i + 1) * rank]
            ortho = product(part, high, 1, 1) + product(part, low, 1, 1) + product(part, least, 1, 1)
            high_part, low_part = split(ortho)
            ortho_ref[i * rows : (i + 1) * rows, :] = jnp.concatenate(
                [high_part, low_part, high_part], axis=1
            )

    right = jnp.concatenate([right_ref[a, 0] for a in range(4)], axis=0).astype(f32)
    turned = jnp.dot(
        inverse_ref[...], right, precision=highest, preferred_element_type=f32
    ) * (1.0 / replicas)
    next_ref[...] = turned
    high, low = split(turned)
    low_rank = product(ortho_ref[...], jnp.concatenate([high, high, low], axis=0), 1, 0)
    out_ref[...] = (merged_ref[...] - low_rank).astype(bf16)


def swapped(array):
    return lax.ppermute(array, "mp_1", [(0, 1), (1, 0)])


class Ring:
    def __init__(self, own):
        self.size = lax.axis_size("mp_0")
        self.chunks = {0: own}
        self.done = 0

    def passed(self, array, hop):
        return lax.ppermute(
            array, "mp_0", [(i, (i + hop) % self.size) for i in range(self.size)]
        )

    def step(self, later=None):
        size, k = self.size, self.done + 1
        self.chunks[k] = self.passed(self.chunks[k - 1], 1)
        if k < size // 2:
            self.chunks[size - k] = self.passed(self.chunks[(size - k + 1) % size], -1)
        self.done = k
        if later is not None:
            both = (later, self.chunks[k], self.chunks[size - k])
            later, self.chunks[k], self.chunks[size - k] = lax.optimization_barrier(both)
        return later

    def all(self):
        return tuple(self.chunks[k] for k in range(self.size))


def per_device(grad_out, hidden_act, carried, prior_right):
    own = carried[0]
    act = hidden_act.T
    features = own.shape[1]
    rank = prior_right.shape[1]
    replicas = lax.axis_size(DP)
    rows = own.shape[0] // 2
    tokens = hidden_act.shape[0]
    place = jnp.stack([lax.axis_index("mp_0"), lax.axis_index("mp_1")]).astype(jnp.int32)

    prior = jnp.concatenate(halves(prior_right), axis=1)
    proj = product(grad_out, prior, 1, 0)
    proj = jnp.concatenate(halves(proj[:, :rank] + proj[:, rank:]), axis=1)
    proj = sent_to_all(proj, MP).reshape(-1, 2 * rank)
    ring = Ring(grad_out)
    proj = ring.step(proj)
    left = product(own, prior, 1, 0) + product(hidden_act, proj, 0, 0)
    left = left[:, :rank] + left[:, rank:]
    left = jnp.concatenate([left[:rows], left[rows:]], axis=1).astype(bf16)
    parts = sent_to_all(left, DP)
    for _ in range(3):
        ring.step()
    chunks = ring.all()

    width = features // 4
    half = tokens // 2
    left, gram, keep, give, right = call(
        left_kernel,
        (
            of((rows, 2 * rank), bf16),
            of((rank // 2, 2 * rank), f32),
            of((half, 2 * rank), bf16),
            of((half, 2 * rank), bf16),
            of((rank, features), f32),
        ),
        limit=24,
        in_specs=[scalars, whole, in_hbm, in_hbm],
        out_specs=(whole,) * 5,
        scratch_shapes=[
            VMEM(act.shape, bf16),
            VMEM(own.shape, bf16),
            pltpu.SemaphoreType.DMA((2,)),
        ],
        name="left_sum",
    )(place, parts, act, own)

    right, half_out = call(
        functools.partial(right_kernel, len(chunks)),
        (of((16, rank // 4, width), bf16), of((half, features), bf16)),
        limit=16,
        in_specs=[scalars, whole, whole, whole] + [anywhere] * len(chunks),
        out_specs=(whole, in_hbm),
        scratch_shapes=[VMEM((half, features), bf16), pltpu.SemaphoreType.DMA((len(chunks) + 1,))],
        name="right_product",
    )(place, keep, swapped(give), right, *chunks)

    other_half = swapped(half_out)
    other_gram = swapped(gram)
    right = sent(right, DP)
    right, other_half, other_gram = lax.optimization_barrier((right, other_half, other_gram))
    columns = pl.BlockSpec((half, width), lambda j: (0, j))
    merged = call(
        merged_kernel,
        of(own.shape, f32),
        limit=58,
        grid=(4,),
        in_specs=[
            scalars,
            pl.BlockSpec((2 * rows, tokens), lambda j: (0, 0)),
            pl.BlockSpec((2 * rows, width), lambda j: (0, j)),
            columns,
            columns,
        ],
        out_specs=pl.BlockSpec((2 * rows, width), lambda j: (0, j)),
        scratch_shapes=[VMEM((tokens, width), bf16)],
        name="merged",
    )(place, act, own, half_out, other_half)
    right = call(
        replica_sum_kernel,
        of((rank // 4, width), bf16),
        in_specs=[whole],
        out_specs=whole,
        name="replica_sum",
    )(right)
    right = call(
        core_sum_kernel,
        of((8, rank // 4, width + 384), bf16),
        in_specs=[scalars] + [whole] * 4,
        out_specs=whole,
        name="core_sum",
    )(place, right, swapped(right), gram, other_gram)
    right, merged = lax.optimization_barrier((sent(right, "mp_0"), merged))
    right, gram = call(
        chip_sum_kernel,
        (of((16, rank // 4, width), bf16), of((rank // 4, 2 * rank), f32)),
        in_specs=[whole],
        out_specs=(whole, whole),
        name="chip_sum",
    )(right)
    right = sent(right, DP)
    inverse = call(
        inverse_kernel,
        of((rank, rank), f32),
        in_specs=[scalars, whole, whole],
        out_specs=whole,
        name="inverse",
    )(place, gram, swapped(gram))
    right = right.reshape(4, 4, rank // 4, width)

    residual_out, next_right = call(
        functools.partial(residual_kernel, replicas),
        (of(own.shape, bf16), of((rank, features), f32)),
        limit=58,
        grid=(4,),
        in_specs=[
            pl.BlockSpec((rank, rank), lambda j: (0, 0)),
            pl.BlockSpec((rows, 2 * rank), lambda j: (0, 0)),
            pl.BlockSpec((4, 1, rank // 4, width), lambda j: (0, j, 0, 0)),
            pl.BlockSpec((2 * rows, width), lambda j: (0, j)),
        ],
        out_specs=(
            pl.BlockSpec((2 * rows, width), lambda j: (0, j)),
            pl.BlockSpec((rank, width), lambda j: (0, j)),
        ),
        scratch_shapes=[VMEM((2 * rows, 3 * rank), bf16)],
        name="residual",
    )(inverse, left, right, merged)
    return (residual_out[None], next_right.T)


def solution(mesh):
    parted = Mesh(mesh.devices.reshape(4, 4, 8, 2), DP_MP)
    placed = (P(DP_MP, None), P(DP, MP), P(DP, MP, None), P())
    return jax.shard_map(
        per_device, mesh=parted, in_specs=placed, out_specs=(P(DP, MP, None), P()), check_vma=False
    )
```

time: 148 us -> 134 us (0.905); the launches traced: 148 us -> 132 us
  blocking collectives: 37.5 us -> 0 us
  waiting for transfers between devices: 21.1 us -> 36.8 us
  starting transfers between devices: 39 us -> 46.2 us
  Pallas kernels: 35.3 us -> 32.7 us
    all_to_all x2 -> x0, blocking collectives: 37.5 us -> none  [sent(): return lax.all_to_all(array, axis, 0, 0, tiled=True)]
    all_to_all x3 -> x5, waiting for transfers between devices: 0.01 us -> 11.6 us  [sent(): return lax.all_to_all(array, axis, 0, 0, tiled=True)]
    all_to_all x3 -> x5, starting transfers between devices: 20.3 us -> 28.5 us  [sent(): return lax.all_to_all(array, axis, 0, 0, tiled=True)]
    pallas_call x1, Pallas kernels: 13.6 us -> 8.14 us  [per_device(): call(functools.partial(residual_kernel, replicas), (of(own.shape, bf16),...]
    ppermute x15 -> x12, waiting for transfers between devices: 21.1 us -> 25.2 us  [the longest x7 21.7 us: passed(): lax.ppermute(array, 'mp_0', [(i, (i + hop) % self.size) for i in range(se...]
    pallas_call x4 -> x6, Pallas kernels: 17.8 us -> 20.9 us  [the longest x1 11.4 us: per_device(): call(merged_kernel, of(own.shape, f32), limit=58, grid=(4,), in_specs=[sc...]
    unnamed x38 -> x30, local copies, waits for them, and re-layouts: 4.44 us -> 5.7 us
    ppermute x15 -> x12, starting transfers between devices: 18.7 us -> 17.7 us  [the longest x5 9.48 us: swapped(): return lax.ppermute(array, 'mp_1', [(0, 1), (1, 0)])]
  transfers between devices with their start and end apart: 18 -> 17, of which waited for: 5 -> 10; matrix products, arithmetic and copies ran while one was open for 2% -> 3% of each run, Pallas kernels for 11% -> 14%
where the time goes in v3:
time: 134 us; the launch traced here: 132 us
  starting transfers between devices  46.2 us (34%)
  waiting for transfers between devices  36.8 us (27%)
  Pallas kernels  32.7 us (24%)
  local copies, waits for them, and re-layouts  7.91 us (6%)
  matrix products  5.47 us (4%)
  other arithmetic  2.28 us (2%)
    all_to_all x5, starting transfers between devices, sent(): return lax.all_to_all(array, axis, 0, 0, tiled=True)  28.5 us
    ppermute x7, waiting for transfers between devices, passed(): lax.ppermute(array, 'mp_0', [(i, (i + hop) % self.size) for i in range(se...  21.7 us
    all_to_all x5, waiting for transfers between devices, sent(): return lax.all_to_all(array, axis, 0, 0, tiled=True)  11.6 us
    pallas_call x1, Pallas kernels, per_device(): call(merged_kernel, of(own.shape, f32), limit=58, grid=(4,), in_specs=[sc...  11.4 us
    ppermute x5, starting transfers between devices, swapped(): return lax.ppermute(array, 'mp_1', [(0, 1), (1, 0)])  9.48 us
    ppermute x7, starting transfers between devices, passed(): lax.ppermute(array, 'mp_0', [(i, (i + hop) % self.size) for i in range(se...  8.2 us
    pallas_call x1, Pallas kernels, per_device(): call(functools.partial(residual_kernel, replicas), (of(own.shape, bf16),...  8.14 us
    unnamed x30, local copies, waits for them, and re-layouts  5.7 us
  transfers between devices with their start and end apart: 17, of which 10 were waited for; matrix products, arithmetic and copies ran while one was open for 3% of the time, Pallas kernels for 14%

profile of v3, /device:TPU:1, one launch (start us, length us, event | category | flops | bytes accessed | tf_op | source)
XLA Modules:
  0.0 132.2 jit_solution(8138878378466717726)
XLA Ops:
  0.6 0.0 copy-start.3
  0.6 1.2 reduce-precision_convert_fusion
  1.9 1.3 convolution_bitcast_fusion
  3.2 0.1 reduce-precision_convert_fusion.1
  3.3 0.1 pad_maximum_fusion.4
  3.3 0.8 broadcast_in_dim.6
  4.1 10.0 %all-to-all-start = ((bf16[16,64,128]{2,1,0:T(8,128)(2,1)}), bf16[16,64,128]{2,1,0:T(8,128)(2,1)S(1)}, u32[]{:S(2)}, u32[]{:S(2)}) async-start(bf16[16,64,128]{2,1,0:T(8,128)(2,1)} %broadcast_in_dim.6), calls=%async_computation | async-start | bytes 524288 | tf_op jit(solution)/shard_map/all_to_all | solution.py:33
  14.1 0.0 copy-start.1
  14.1 1.5 %collective-permute-start = (bf16[64,2560]{1,0:T(8,128)(2,1)S(1)}, bf16[64,2560]{1,0:T(8,128)(2,1)S(1)}, u32[]{:S(2)}, u32[]{:S(2)}) collective-permute-start(bf16[64,2560]{1,0:T(8,128)(2,1)S(1)} %copy-done.3), channel_id=1, source_target_pairs={{0,2},{2,4},{4,6},{6,8},{8,10},{10,12},{12,14},{14,0},{1,3},{3,5},... | collective-permute-start | bytes 983048 | tf_op jit(solution)/shard_map/ppermute | solution.py:256
  15.6 1.3 collective-permute-start.1
  16.9 3.5 %fusion.3 = f32[128,864]{0,1:T(8,128)S(1)} fusion(bf16[2560,64]{0,1:T(8,128)(2,1)S(1)} %get-tuple-element.41, bf16[2560,64]{0,1:T(8,128)(2,1)S(1)} %get-tuple-element.40, bf16[1,864,2560]{2,1,0:T(8,128)(2,1)} %param.6), kind=kOutput, calls=%fused_computation.9 | convolution fusion | flops 567541760 | bytes 5521408 | tf_op jit(solution)/shard_map/dot_general | solution.py:27
  20.4 9.9 %collective-permute-done.refs_5_ = bf16[64,2560]{1,0:T(8,128)(2,1)S(1)} collective-permute-done((bf16[64,2560]{1,0:T(8,128)(2,1)S(1)}, bf16[64,2560]{1,0:T(8,128)(2,1)S(1)}, u32[]{:S(2)}, u32[]{:S(2)}) %collective-permute-start) | collective-permute-done | bytes 327712 | tf_op jit(solution)/shard_map/ppermute | solution.py:256
  30.3 0.7 copy-done.5
  31.0 0.0 collective-permute-done.1.refs_11_
  31.0 0.0 all-to-all-done
  31.0 0.6 fusion
  31.7 0.2 fusion.2
  31.9 0.1 pad_maximum_fusion.3
  32.0 1.4 %broadcast_in_dim.7 = bf16[16,432,128]{2,1,0:T(8,128)(2,1)} broadcast(bf16[432,128]{1,0:T(8,128)(2,1)S(1)} %pad_maximum_fusion.3), dimensions={1,2} | broadcast | bytes 1880064 | tf_op jit(solution)/shard_map/broadcast_in_dim | solution.py:38
  33.4 6.8 %all-to-all-start.1 = ((bf16[16,432,128]{2,1,0:T(8,128)(2,1)}), bf16[16,432,128]{2,1,0:T(8,128)(2,1)S(1)}, u32[]{:S(2)}, u32[]{:S(2)}) async-start(bf16[16,432,128]{2,1,0:T(8,128)(2,1)} %broadcast_in_dim.7), calls=%async_computation.1 | async-start | bytes 3538944 | tf_op jit(solution)/shard_map/all_to_all | solution.py:33
  40.2 0.1 collective-permute-start.3
  40.3 2.7 %collective-permute-start.6 = (bf16[64,2560]{1,0:T(8,128)(2,1)}, bf16[64,2560]{1,0:T(8,128)(2,1)}, u32[]{:S(2)}, u32[]{:S(2)}) collective-permute-start(bf16[64,2560]{1,0:T(8,128)(2,1)} %collective-permute-done.1.refs_11_), channel_id=1, source_target_pairs={{0,14},{2,0},{4,2},{6,4},{8,6},{10,8},{12,10},{14,12},{1,15},{3,1}... | collective-permute-start | bytes 983048 | tf_op jit(solution)/shard_map/ppermute | solution.py:256
  42.9 6.8 %collective-permute-done.3.refs_6_ = bf16[64,2560]{1,0:T(8,128)(2,1)S(1)} collective-permute-done((bf16[64,2560]{1,0:T(8,128)(2,1)}, bf16[64,2560]{1,0:T(8,128)(2,1)S(1)}, u32[]{:S(2)}, u32[]{:S(2)}) %collective-permute-start.3) | collective-permute-done | bytes 327712 | tf_op jit(solution)/shard_map/ppermute | solution.py:256
  49.7 0.0 collective-permute-start.4
  49.7 0.7 copy-done.7
  50.4 0.0 collective-permute-done.6.refs_10_
  50.5 2.7 %collective-permute-start.7 = (bf16[64,2560]{1,0:T(8,128)(2,1)}, bf16[64,2560]{1,0:T(8,128)(2,1)}, u32[]{:S(2)}, u32[]{:S(2)}) collective-permute-start(bf16[64,2560]{1,0:T(8,128)(2,1)} %collective-permute-done.6.refs_10_), channel_id=1, source_target_pairs={{0,14},{2,0},{4,2},{6,4},{8,6},{10,8},{12,10},{14,12},{1,15},{3,1}... | collective-permute-start | bytes 983048 | tf_op jit(solution)/shard_map/ppermute | solution.py:256
  53.1 5.0 %collective-permute-done.4.refs_7_ = bf16[64,2560]{1,0:T(8,128)(2,1)} collective-permute-done((bf16[64,2560]{1,0:T(8,128)(2,1)S(1)}, bf16[64,2560]{1,0:T(8,128)(2,1)}, u32[]{:S(2)}, u32[]{:S(2)}) %collective-permute-start.4) | collective-permute-done | bytes 327712 | tf_op jit(solution)/shard_map/ppermute | solution.py:256
  58.2 0.0 collective-permute-start.5
  58.2 0.6 pad_add_fusion.place_ref.refs_0_
  58.8 3.8 %all-to-all-done.1.parts_ref = bf16[16,432,128]{2,1,0:T(8,128)(2,1)S(1)} async-done(((bf16[16,432,128]{2,1,0:T(8,128)(2,1)}), bf16[16,432,128]{2,1,0:T(8,128)(2,1)S(1)}, u32[]{:S(2)}, u32[]{:S(2)}) %all-to-all-start.1) | async-done | bytes 1769504 | tf_op jit(solution)/shard_map/all_to_all | solution.py:33
  62.5 2.3 %copy-done = bf16[1,864,2560]{2,1,0:T(8,128)(2,1)S(1)} copy-done((bf16[1,864,2560]{2,1,0:T(8,128)(2,1)S(1)}, bf16[1,864,2560]{2,1,0:T(8,128)(2,1)}, u32[]{:S(2)}) %copy-start) | copy-done | bytes 4423704
  64.8 0.6 copy-done.11
  65.4 3.7 %left_sum.1 = (bf16[432,128]{1,0:T(8,128)(2,1)S(1)}, f32[32,128]{1,0:T(8,128)S(1)}, bf16[512,128]{1,0:T(8,128)(2,1)S(1)}, bf16[512,128]{1,0:T(8,128)(2,1)S(1)}, f32[64,2560]{1,0:T(8,128)S(1)}) custom-call(s32[2]{0:T(128)S(1)} %copy-done.11, bf16[16,432,128]{2,1,0:T(8,128)(2,1)S(1)} %all-to-all-done.1.parts_ref, bf16[864,1024]{1,0:T(8,128)(2,1)S(1)} %bitcast.20, ...), custom_call_target="tpu_custom_call" | custom-call | tf_op jit(solution)/shard_map/left_sum/pallas_call | solution.py:301
  69.2 4.7 %collective-permute-start.2 = (bf16[512,128]{1,0:T(8,128)(2,1)S(1)}, bf16[512,128]{1,0:T(8,128)(2,1)S(1)}, u32[]{:S(2)}, u32[]{:S(2)}) collective-permute-start(bf16[512,128]{1,0:T(8,128)(2,1)S(1)} %get-tuple-element.23), channel_id=1, source_target_pairs={{0,1},{1,0},{2,3},{3,2},{4,5},{5,4},{6,7},{7,6},{8,9},{9,8},{10,11... | collective-permute-start | bytes 393224 | tf_op jit(solution)/shard_map/ppermute | solution.py:246
  73.9 0.0 collective-permute-done.7.refs_9_
  73.9 0.0 collective-permute-done.5.refs_8_
  73.9 1.0 collective-permute-done.2.refs_2_
  74.9 0.0 copy-done.8
  74.9 3.8 %right_product.1 = (bf16[16,16,640]{2,1,0:T(8,128)(2,1)}, bf16[512,2560]{1,0:T(8,128)(2,1)S(1)}) custom-call(s32[2]{0:T(128)S(1)} %copy-done.11, bf16[512,128]{1,0:T(8,128)(2,1)S(1)} %get-tuple-element.22.refs_1_, bf16[512,128]{1,0:T(8,128)(2,1)S(1)} %collective-permute-done.2.refs_2_, f32[64,2560]{1,0:T(8,128)S(1)} %get-tuple-element.24.refs_3_, ...), custom_call_target="tpu_custom_call" | custom-call | tf_op jit(solution)/shard_map/right_product/pallas_call | solution.py:321
  78.7 0.0 copy-start.2
  78.7 0.4 collective-permute-start.8
  79.2 3.7 %all-to-all-start.2 = ((bf16[16,16,640]{2,1,0:T(8,128)(2,1)}), bf16[16,16,640]{2,1,0:T(8,128)(2,1)S(1)}, u32[]{:S(2)}, u32[]{:S(2)}) async-start(bf16[16,16,640]{2,1,0:T(8,128)(2,1)} %get-tuple-element.27), calls=%async_computation.2 | async-start | bytes 655360 | tf_op jit(solution)/shard_map/all_to_all | solution.py:33
  82.8 0.5 collective-permute-start.9
  83.3 0.8 collective-permute-done.9.other_gram_ref
  84.2 6.8 %all-to-all-done.2.parts_ref = bf16[16,16,640]{2,1,0:T(8,128)(2,1)S(1)} async-done(((bf16[16,16,640]{2,1,0:T(8,128)(2,1)}), bf16[16,16,640]{2,1,0:T(8,128)(2,1)S(1)}, u32[]{:S(2)}, u32[]{:S(2)}) %all-to-all-start.2) | async-done | bytes 327712 | tf_op jit(solution)/shard_map/all_to_all | solution.py:33
  91.0 0.0 collective-permute-done.8.other_ref
  91.0 0.1 replica_sum.1.own_ref
  91.1 2.2 %collective-permute-start.10 = (bf16[16,640]{1,0:T(8,128)(2,1)S(1)}, bf16[16,640]{1,0:T(8,128)(2,1)S(1)}, u32[]{:S(2)}, u32[]{:S(2)}) collective-permute-start(bf16[16,640]{1,0:T(8,128)(2,1)S(1)} %replica_sum.1.own_ref), channel_id=1, source_target_pairs={{0,1},{1,0},{2,3},{3,2},{4,5},{5,4},{6,7},{7,6},{8,9},{9,8},{10,11... | collective-permute-start | bytes 61448 | tf_op jit(solution)/shard_map/ppermute | solution.py:246
  93.3 0.8 collective-permute-done.10.other_ref
  94.1 1.3 core_sum.1
  95.4 4.6 %all-to-all-start.3 = ((bf16[8,16,1024]{2,1,0:T(8,128)(2,1)}), bf16[8,16,1024]{2,1,0:T(8,128)(2,1)S(1)}, u32[]{:S(2)}, u32[]{:S(2)}) async-start(bf16[8,16,1024]{2,1,0:T(8,128)(2,1)} %core_sum.1), calls=%async_computation.3 | async-start | bytes 524288 | tf_op jit(solution)/shard_map/all_to_all | solution.py:33
  99.9 0.0 copy-done.2
  100.0 11.4 %merged.1.merged_ref = f32[864,2560]{1,0:T(8,128)} custom-call(s32[2]{0:T(128)} %pad_add_fusion.place_ref.refs_0_, bf16[864,1024]{1,0:T(8,128)(2,1)} %bitcast.19, bf16[864,2560]{1,0:T(8,128)(2,1)} %bitcast.17, bf16[512,2560]{1,0:T(8,128)(2,1)} %copy-done.2, bf16[512,2560]{1,0:T(8,128)(2,1)} %collective-permute-done.8.other_ref), custom_call_target="tpu_custom_call" | custom-call | tf_op jit(solution)/shard_map/merged/pallas_call | solution.py:336
  111.4 0.0 all-to-all-done.3.parts_ref
  111.4 0.8 chip_sum.1
  112.1 3.5 %all-to-all-start.4 = ((bf16[16,16,640]{2,1,0:T(8,128)(2,1)}), bf16[16,16,640]{2,1,0:T(8,128)(2,1)S(1)}, u32[]{:S(2)}, u32[]{:S(2)}) async-start(bf16[16,16,640]{2,1,0:T(8,128)(2,1)} %get-tuple-element.36), calls=%async_computation.4 | async-start | bytes 655360 | tf_op jit(solution)/shard_map/all_to_all | solution.py:33
  115.7 1.6 %collective-permute-start.11 = (f32[16,128]{1,0:T(8,128)S(1)}, f32[16,128]{1,0:T(8,128)S(1)}, u32[]{:S(2)}, u32[]{:S(2)}) collective-permute-start(f32[16,128]{1,0:T(8,128)S(1)} %get-tuple-element.34.gram_ref), channel_id=1, source_target_pairs={{0,1},{1,0},{2,3},{3,2},{4,5},{5,4},{6,7},{7,6},{8,9},{9,8},{10,11... | collective-permute-start | bytes 24584 | tf_op jit(solution)/shard_map/ppermute | solution.py:246
  117.3 0.8 collective-permute-done.11.other_ref
  118.1 3.6 %inverse.1.inverse_ref = f32[64,64]{1,0:T(8,128)S(1)} custom-call(s32[2]{0:T(128)S(1)} %copy-done.13, f32[16,128]{1,0:T(8,128)S(1)} %get-tuple-element.34.gram_ref, f32[16,128]{1,0:T(8,128)S(1)} %collective-permute-done.11.other_ref), custom_call_target="tpu_custom_call" | custom-call | tf_op jit(solution)/shard_map/inverse/pallas_call | solution.py:375
  121.7 0.6 copy-done.9
  122.3 1.0 all-to-all-done.4
  123.3 0.7 copy-done.14
  124.1 8.1 %residual.1 = (bf16[864,2560]{1,0:T(8,128)(2,1)}, f32[64,2560]{1,0:T(8,128)}) custom-call(f32[64,64]{1,0:T(8,128)} %copy-done.9, bf16[432,128]{1,0:T(8,128)(2,1)} %copy-done.10, bf16[4,4,16,640]{3,2,1,0:T(8,128)(2,1)} %bitcast.21, f32[864,2560]{1,0:T(8,128)} %merged.1.merged_ref), custom_call_target="tpu_custom_call" | custom-call | tf_op jit(solution)/shard_map/residual/pallas_call | solution.py:384
  (20 shorter events, 0.1 us)
Async XLA Ops:
  0.6 13.5 %copy-start.3 = (bf16[64,2560]{1,0:T(8,128)(2,1)S(1)}, bf16[64,2560]{1,0:T(8,128)(2,1)}, u32[]{:S(2)}) copy-start(bf16[64,2560]{1,0:T(8,128)(2,1)} %refs_4_.1) | copy-start | bytes 983044
  4.1 26.9 %all-to-all-start = ((bf16[16,64,128]{2,1,0:T(8,128)(2,1)}), bf16[16,64,128]{2,1,0:T(8,128)(2,1)S(1)}, u32[]{:S(2)}, u32[]{:S(2)}) async-start(bf16[16,64,128]{2,1,0:T(8,128)(2,1)} %broadcast_in_dim.6), calls=%async_computation | async-start | bytes 524288 | tf_op jit(solution)/shard_map/all_to_all | solution.py:33
  14.1 16.9 %copy-start.1 = (bf16[1024,864]{0,1:T(8,128)(2,1)S(1)}, bf16[1024,864]{0,1:T(8,128)(2,1)}, u32[]{:S(2)}) copy-start(bf16[1024,864]{0,1:T(8,128)(2,1)} %param.5) | copy-start | bytes 5308420
  14.1 16.2 %collective-permute-start = (bf16[64,2560]{1,0:T(8,128)(2,1)S(1)}, bf16[64,2560]{1,0:T(8,128)(2,1)S(1)}, u32[]{:S(2)}, u32[]{:S(2)}) collective-permute-start(bf16[64,2560]{1,0:T(8,128)(2,1)S(1)} %copy-done.3), channel_id=1, source_target_pairs={{0,2},{2,4},{4,6},{6,8},{8,10},{10,12},{12,14},{14,0},{1,3},{3,5},... | collective-permute-start | bytes 983048 | tf_op jit(solution)/shard_map/ppermute | solution.py:256
  15.6 15.5 %collective-permute-start.1 = (bf16[64,2560]{1,0:T(8,128)(2,1)S(1)}, bf16[64,2560]{1,0:T(8,128)(2,1)}, u32[]{:S(2)}, u32[]{:S(2)}) collective-permute-start(bf16[64,2560]{1,0:T(8,128)(2,1)S(1)} %copy-done.3), channel_id=1, source_target_pairs={{0,14},{2,0},{4,2},{6,4},{8,6},{10,8},{12,10},{14,12},{1,15},{3,1}... | collective-permute-start | bytes 983048 | tf_op jit(solution)/shard_map/ppermute | solution.py:256
  30.3 0.7 copy-start.5
  33.4 29.1 %all-to-all-start.1 = ((bf16[16,432,128]{2,1,0:T(8,128)(2,1)}), bf16[16,432,128]{2,1,0:T(8,128)(2,1)S(1)}, u32[]{:S(2)}, u32[]{:S(2)}) async-start(bf16[16,432,128]{2,1,0:T(8,128)(2,1)} %broadcast_in_dim.7), calls=%async_computation.1 | async-start | bytes 3538944 | tf_op jit(solution)/shard_map/all_to_all | solution.py:33
  40.2 9.6 %collective-permute-start.3 = (bf16[64,2560]{1,0:T(8,128)(2,1)}, bf16[64,2560]{1,0:T(8,128)(2,1)S(1)}, u32[]{:S(2)}, u32[]{:S(2)}) collective-permute-start(bf16[64,2560]{1,0:T(8,128)(2,1)} %copy-done.5), channel_id=1, source_target_pairs={{0,2},{2,4},{4,6},{6,8},{8,10},{10,12},{12,14},{14,0},{1,3},{3,5},... | collective-permute-start | bytes 983048 | tf_op jit(solution)/shard_map/ppermute | solution.py:256
  40.3 10.2 %collective-permute-start.6 = (bf16[64,2560]{1,0:T(8,128)(2,1)}, bf16[64,2560]{1,0:T(8,128)(2,1)}, u32[]{:S(2)}, u32[]{:S(2)}) collective-permute-start(bf16[64,2560]{1,0:T(8,128)(2,1)} %collective-permute-done.1.refs_11_), channel_id=1, source_target_pairs={{0,14},{2,0},{4,2},{6,4},{8,6},{10,8},{12,10},{14,12},{1,15},{3,1}... | collective-permute-start | bytes 983048 | tf_op jit(solution)/shard_map/ppermute | solution.py:256
  49.7 8.4 %collective-permute-start.4 = (bf16[64,2560]{1,0:T(8,128)(2,1)S(1)}, bf16[64,2560]{1,0:T(8,128)(2,1)}, u32[]{:S(2)}, u32[]{:S(2)}) collective-permute-start(bf16[64,2560]{1,0:T(8,128)(2,1)S(1)} %collective-permute-done.3.refs_6_), channel_id=1, source_target_pairs={{0,2},{2,4},{4,6},{6,8},{8,10},{10,12},{12,14},{14,0},{1,3},{3,5},... | collective-permute-start | bytes 983048 | tf_op jit(solution)/shard_map/ppermute | solution.py:256
  49.7 0.7 copy-start.7
  50.5 23.4 %collective-permute-start.7 = (bf16[64,2560]{1,0:T(8,128)(2,1)}, bf16[64,2560]{1,0:T(8,128)(2,1)}, u32[]{:S(2)}, u32[]{:S(2)}) collective-permute-start(bf16[64,2560]{1,0:T(8,128)(2,1)} %collective-permute-done.6.refs_10_), channel_id=1, source_target_pairs={{0,14},{2,0},{4,2},{6,4},{8,6},{10,8},{12,10},{14,12},{1,15},{3,1}... | collective-permute-start | bytes 983048 | tf_op jit(solution)/shard_map/ppermute | solution.py:256
  58.2 15.7 %collective-permute-start.5 = (bf16[64,2560]{1,0:T(8,128)(2,1)}, bf16[64,2560]{1,0:T(8,128)(2,1)}, u32[]{:S(2)}, u32[]{:S(2)}) collective-permute-start(bf16[64,2560]{1,0:T(8,128)(2,1)} %collective-permute-done.4.refs_7_), channel_id=1, source_target_pairs={{0,2},{2,4},{4,6},{6,8},{8,10},{10,12},{12,14},{14,0},{1,3},{3,5},... | collective-permute-start | bytes 983048 | tf_op jit(solution)/shard_map/ppermute | solution.py:256
  62.5 2.3 %copy-start = (bf16[1,864,2560]{2,1,0:T(8,128)(2,1)S(1)}, bf16[1,864,2560]{2,1,0:T(8,128)(2,1)}, u32[]{:S(2)}) copy-start(bf16[1,864,2560]{2,1,0:T(8,128)(2,1)} %param.6) | copy-start | bytes 13271044
  64.8 0.6 copy-start.11
  65.4 9.4 %copy-start.4 = (bf16[64,2560]{1,0:T(8,128)(2,1)S(1)}, bf16[64,2560]{1,0:T(8,128)(2,1)}, u32[]{:S(2)}) copy-start(bf16[64,2560]{1,0:T(8,128)(2,1)} %refs_4_.1) | copy-start | bytes 983044
  65.4 9.4 %copy-start.6 = (bf16[64,2560]{1,0:T(8,128)(2,1)S(1)}, bf16[64,2560]{1,0:T(8,128)(2,1)}, u32[]{:S(2)}) copy-start(bf16[64,2560]{1,0:T(8,128)(2,1)} %copy-done.5) | copy-start | bytes 983044
  65.4 9.4 %copy-start.8 = (bf16[64,2560]{1,0:T(8,128)(2,1)S(1)}, bf16[64,2560]{1,0:T(8,128)(2,1)}, u32[]{:S(2)}) copy-start(bf16[64,2560]{1,0:T(8,128)(2,1)} %copy-done.7) | copy-start | bytes 983044
  69.2 9.5 %copy-start.10 = (bf16[432,128]{1,0:T(8,128)(2,1)}, bf16[432,128]{1,0:T(8,128)(2,1)S(1)}, u32[]{:S(2)}) copy-start(bf16[432,128]{1,0:T(8,128)(2,1)S(1)} %get-tuple-element.35.left_ref) | copy-start | bytes 331780
  69.2 5.7 %collective-permute-start.2 = (bf16[512,128]{1,0:T(8,128)(2,1)S(1)}, bf16[512,128]{1,0:T(8,128)(2,1)S(1)}, u32[]{:S(2)}, u32[]{:S(2)}) collective-permute-start(bf16[512,128]{1,0:T(8,128)(2,1)S(1)} %get-tuple-element.23), channel_id=1, source_target_pairs={{0,1},{1,0},{2,3},{3,2},{4,5},{5,4},{6,7},{7,6},{8,9},{9,8},{10,11... | collective-permute-start | bytes 393224 | tf_op jit(solution)/shard_map/ppermute | solution.py:246
  74.9 19.3 %copy-start.12 = (s32[2]{0:T(128)S(1)}, s32[2]{0:T(128)}, u32[]{:S(2)}) copy-start(s32[2]{0:T(128)} %pad_add_fusion.place_ref.refs_0_) | copy-start | bytes 28
  78.7 21.3 %copy-start.2 = (bf16[512,2560]{1,0:T(8,128)(2,1)}, bf16[512,2560]{1,0:T(8,128)(2,1)S(1)}, u32[]{:S(2)}) copy-start(bf16[512,2560]{1,0:T(8,128)(2,1)S(1)} %get-tuple-element.28.half_ref) | copy-start | bytes 7864324
  78.7 12.3 %collective-permute-start.8 = (bf16[512,2560]{1,0:T(8,128)(2,1)S(1)}, bf16[512,2560]{1,0:T(8,128)(2,1)}, u32[]{:S(2)}, u32[]{:S(2)}) collective-permute-start(bf16[512,2560]{1,0:T(8,128)(2,1)S(1)} %get-tuple-element.28.half_ref), channel_id=1, source_target_pairs={{0,1},{1,0},{2,3},{3,2},{4,5},{5,4},{6,7},{7,6},{8,9},{9,8},{10,11... | collective-permute-start | bytes 7864328 | tf_op jit(solution)/shard_map/ppermute | solution.py:246
  79.2 11.9 %all-to-all-start.2 = ((bf16[16,16,640]{2,1,0:T(8,128)(2,1)}), bf16[16,16,640]{2,1,0:T(8,128)(2,1)S(1)}, u32[]{:S(2)}, u32[]{:S(2)}) async-start(bf16[16,16,640]{2,1,0:T(8,128)(2,1)} %get-tuple-element.27), calls=%async_computation.2 | async-start | bytes 655360 | tf_op jit(solution)/shard_map/all_to_all | solution.py:33
  82.8 1.4 %collective-permute-start.9 = (f32[32,128]{1,0:T(8,128)S(1)}, f32[32,128]{1,0:T(8,128)S(1)}, u32[]{:S(2)}, u32[]{:S(2)}) collective-permute-start(f32[32,128]{1,0:T(8,128)S(1)} %get-tuple-element.29.gram_ref), channel_id=1, source_target_pairs={{0,1},{1,0},{2,3},{3,2},{4,5},{5,4},{6,7},{7,6},{8,9},{9,8},{10,11... | collective-permute-start | bytes 49160 | tf_op jit(solution)/shard_map/ppermute | solution.py:246
  91.1 3.0 %collective-permute-start.10 = (bf16[16,640]{1,0:T(8,128)(2,1)S(1)}, bf16[16,640]{1,0:T(8,128)(2,1)S(1)}, u32[]{:S(2)}, u32[]{:S(2)}) collective-permute-start(bf16[16,640]{1,0:T(8,128)(2,1)S(1)} %replica_sum.1.own_ref), channel_id=1, source_target_pairs={{0,1},{1,0},{2,3},{3,2},{4,5},{5,4},{6,7},{7,6},{8,9},{9,8},{10,11... | collective-permute-start | bytes 61448 | tf_op jit(solution)/shard_map/ppermute | solution.py:246
  95.4 16.0 %all-to-all-start.3 = ((bf16[8,16,1024]{2,1,0:T(8,128)(2,1)}), bf16[8,16,1024]{2,1,0:T(8,128)(2,1)S(1)}, u32[]{:S(2)}, u32[]{:S(2)}) async-start(bf16[8,16,1024]{2,1,0:T(8,128)(2,1)} %core_sum.1), calls=%async_computation.3 | async-start | bytes 524288 | tf_op jit(solution)/shard_map/all_to_all | solution.py:33
  100.0 18.2 %copy-start.13 = (s32[2]{0:T(128)S(1)}, s32[2]{0:T(128)}, u32[]{:S(2)}) copy-start(s32[2]{0:T(128)} %pad_add_fusion.place_ref.refs_0_) | copy-start | bytes 28
  112.1 11.2 %all-to-all-start.4 = ((bf16[16,16,640]{2,1,0:T(8,128)(2,1)}), bf16[16,16,640]{2,1,0:T(8,128)(2,1)S(1)}, u32[]{:S(2)}, u32[]{:S(2)}) async-start(bf16[16,16,640]{2,1,0:T(8,128)(2,1)} %get-tuple-element.36), calls=%async_computation.4 | async-start | bytes 655360 | tf_op jit(solution)/shard_map/all_to_all | solution.py:33
  115.7 2.5 %collective-permute-start.11 = (f32[16,128]{1,0:T(8,128)S(1)}, f32[16,128]{1,0:T(8,128)S(1)}, u32[]{:S(2)}, u32[]{:S(2)}) collective-permute-start(f32[16,128]{1,0:T(8,128)S(1)} %get-tuple-element.34.gram_ref), channel_id=1, source_target_pairs={{0,1},{1,0},{2,3},{3,2},{4,5},{5,4},{6,7},{7,6},{8,9},{9,8},{10,11... | collective-permute-start | bytes 24584 | tf_op jit(solution)/shard_map/ppermute | solution.py:246
  121.7 0.6 copy-start.9
  123.3 0.7 copy-start.14

commit v4 on v3

--- a/solution.py
+++ b/solution.py
@@ -19,7 +19,6 @@
 whole = pl.BlockSpec(memory_space=pltpu.VMEM)
 anywhere = pl.BlockSpec(memory_space=pl.ANY)
 in_hbm = pl.BlockSpec(memory_space=pltpu.HBM)
-scalars = pl.BlockSpec(memory_space=pltpu.SMEM)
 MIB = 1024 * 1024
 
 
@@ -61,12 +60,20 @@
     return jax.ShapeDtypeStruct(shape, kind)
 
 
-def chunk_copies(place_ref, chunk_refs, half_ref, sems):
+def proj_kernel(grad_ref, prior_ref, out_ref):
+    grad = grad_ref[...]
+    high, low = split(prior_ref[...])
+    proj = jnp.concatenate(split(product(grad, high, 1, 1) + product(grad, low, 1, 1)), axis=1)
+    for i in range(out_ref.shape[0]):
+        out_ref[i] = proj
+
+
+def chunk_copies(chunk_refs, half_ref, sems):
     steps = len(chunk_refs)
     tokens = chunk_refs[0].shape[0]
     copies = []
     for k, chunk_ref in enumerate(chunk_refs):
-        row = lax.rem(place_ref[0] + (steps - k), steps) * tokens
+        row = lax.rem(lax.axis_index("mp_0") + (steps - k), steps) * tokens
         copies.append(
             pltpu.make_async_copy(
                 chunk_ref, half_ref.at[pl.ds(pl.multiple_of(row, tokens), tokens), :], sems.at[k]
@@ -82,13 +89,10 @@
 
 
 def left_kernel(
-    place_ref, parts_ref, act_hbm, own_hbm, left_ref, gram_ref, keep_ref, give_ref, right_ref,
-    act_ref, own_ref, sems,
+    parts_ref, act_hbm, left_ref, turned_ref, gram_ref, keep_ref, give_ref, act_ref, sem
 ):
-    act_copy = pltpu.make_async_copy(act_hbm, act_ref, sems.at[0])
-    own_copy = pltpu.make_async_copy(own_hbm, own_ref, sems.at[1])
+    act_copy = pltpu.make_async_copy(act_hbm, act_ref, sem)
     act_copy.start()
-    own_copy.start()
     rows, lanes = left_ref.shape
     rank = lanes // 2
     left = total_of(parts_ref).astype(bf16)
@@ -101,22 +105,42 @@
     act_copy.wait()
     act_left = product(upper, act_ref[:rows], 1, 0) + product(lower, act_ref[rows:], 1, 0)
     act_left = jnp.concatenate(split(act_left.T), axis=1)
-    first = place_ref[1] == 0
+    first = lax.axis_index("mp_1") == 0
     tokens = 64
     for z in range(act_left.shape[0] // (2 * tokens)):
         near = act_left[2 * z * tokens : (2 * z + 1) * tokens]
         far = act_left[(2 * z + 1) * tokens : (2 * z + 2) * tokens]
         keep_ref[z * tokens : (z + 1) * tokens, :] = jnp.where(first, near, far)
         give_ref[z * tokens : (z + 1) * tokens, :] = jnp.where(first, far, near)
-    own_copy.wait()
-    right_ref[...] = product(upper, own_ref[:rows], 1, 0) + product(lower, own_ref[rows:], 1, 0)
+    turned_ref[...] = turned
+
+
+def own_kernel(turned_ref, own_hbm, right_ref, own_ref, sems):
+    features = own_ref.shape[1]
+    rows = turned_ref.shape[1]
+    rank = turned_ref.shape[0] // 2
+    width = features // 4
+    copies = []
+    for b in range(4):
+        columns = pl.ds(b * width, width)
+        copies.append(
+            pltpu.make_async_copy(own_hbm.at[:, columns], own_ref.at[:, columns], sems.at[b])
+        )
+        copies[b].start()
+    turned = turned_ref[...]
+    for b in range(4):
+        columns = slice(b * width, (b + 1) * width)
+        copies[b].wait()
+        right_ref[:, columns] = product(turned[:rank], own_ref[:rows, columns], 1, 0) + product(
+            turned[rank:], own_ref[rows:, columns], 1, 0
+        )
 
 
 def right_kernel(count, *refs):
-    place_ref, keep_ref, other_ref, right_ref = refs[:4]
-    chunk_refs = refs[4 : 4 + count]
-    out_ref, half_hbm, half_ref, sems = refs[4 + count :]
-    copies = chunk_copies(place_ref, chunk_refs, half_ref, sems)
+    keep_ref, other_ref, right_ref = refs[:3]
+    chunk_refs = refs[3 : 3 + count]
+    out_ref, half_hbm, half_ref, sems = refs[3 + count :]
+    copies = chunk_copies(chunk_refs, half_ref, sems)
     for copy in copies:
         copy.start()
     rank = right_ref.shape[0]
@@ -135,14 +159,15 @@
     half_copy.wait()
 
 
-def merged_kernel(place_ref, act_ref, own_ref, half_ref, other_ref, out_ref, full_ref):
+def merged_kernel(act_ref, own_ref, half_ref, other_ref, out_ref, full_ref):
     tokens = 64
     for z in range(half_ref.shape[0] // tokens):
         rows = slice(z * tokens, (z + 1) * tokens)
-        for ref, near in ((half_ref, place_ref[1]), (other_ref, 1 - place_ref[1])):
+        for ref, near in ((half_ref, lax.axis_index("mp_1")), (other_ref, 1 - lax.axis_index("mp_1"))):
             row = pl.multiple_of((2 * z + near) * tokens, tokens)
             full_ref[pl.ds(row, tokens), :] = ref[rows, :]
-    out_ref[...] = own_ref[...].astype(f32) + product(act_ref[...], full_ref[...], 1, 0)
+    merged = own_ref[...].astype(f32) + product(act_ref[...], full_ref[...], 1, 0)
+    out_ref[...] = merged.astype(bf16)
 
 
 def total_of(parts_ref):
@@ -156,11 +181,11 @@
     out_ref[...] = total_of(parts_ref).astype(bf16)
 
 
-def core_sum_kernel(place_ref, own_ref, other_ref, gram_ref, other_gram_ref, out_ref):
+def core_sum_kernel(own_ref, other_ref, gram_ref, other_gram_ref, out_ref):
     right = (own_ref[...].astype(f32) + other_ref[...].astype(f32)).astype(bf16)
     gram = gram_ref[...] + other_gram_ref[...]
     height = gram.shape[0] // 2
-    gram = jnp.where(place_ref[1] == 0, gram[:height], gram[height:])
+    gram = jnp.where(lax.axis_index("mp_1") == 0, gram[:height], gram[height:])
     sent_on = jnp.concatenate([right, in_terms(gram)], axis=1)
     for i in range(out_ref.shape[0]):
         out_ref[i] = sent_on
@@ -203,35 +228,28 @@
     return work[:, rank:] * lax.rsqrt(pivots)
 
 
-def inverse_kernel(place_ref, gram_ref, other_ref, out_ref):
+def inverse_kernel(gram_ref, other_ref, left_ref, out_ref, ortho_ref):
     own, other = gram_ref[...], other_ref[...]
-    first = place_ref[1] == 0
+    first = lax.axis_index("mp_1") == 0
     upper, lower = jnp.where(first, own, other), jnp.where(first, other, own)
     rank = out_ref.shape[0]
     gram = jnp.concatenate([upper[:, :rank], lower[:, :rank], upper[:, rank:], lower[:, rank:]], axis=0)
-    out_ref[...] = inverse_of(gram)
-
-
-def residual_kernel(
-    replicas, inverse_ref, left_ref, right_ref, merged_ref, out_ref, next_ref, ortho_ref
-):
+    inverse = inverse_of(gram)
+    out_ref[...] = inverse
     rows = left_ref.shape[0]
-    rank = inverse_ref.shape[0]
-
-    @pl.when(pl.program_id(0) == 0)
-    def _():
-        left = left_ref[...]
-        inverse = inverse_ref[...]
-        high, low = split(inverse)
-        least = (inverse - high.astype(f32) - low.astype(f32)).astype(bf16)
-        for i in range(2):
-            part = left[:, i * rank : (i + 1) * rank]
-            ortho = product(part, high, 1, 1) + product(part, low, 1, 1) + product(part, least, 1, 1)
-            high_part, low_part = split(ortho)
-            ortho_ref[i * rows : (i + 1) * rows, :] = jnp.concatenate(
-                [high_part, low_part, high_part], axis=1
-            )
-
+    left = left_ref[...]
+    high, low = split(inverse)
+    least = (inverse - high.astype(f32) - low.astype(f32)).astype(bf16)
+    for i in range(2):
+        part = left[:, i * rank : (i + 1) * rank]
+        ortho = product(part, high, 1, 1) + product(part, low, 1, 1) + product(part, least, 1, 1)
+        high_part, low_part = split(ortho)
+        ortho_ref[i * rows : (i + 1) * rows, :] = jnp.concatenate(
+            [high_part, low_part, high_part], axis=1
+        )
+
+
+def residual_kernel(replicas, inverse_ref, ortho_ref, right_ref, merged_ref, out_ref, next_ref):
     right = jnp.concatenate([right_ref[a, 0] for a in range(4)], axis=0).astype(f32)
     turned = jnp.dot(
         inverse_ref[...], right, precision=highest, preferred_element_type=f32
@@ -239,7 +257,7 @@
     next_ref[...] = turned
     high, low = split(turned)
     low_rank = product(ortho_ref[...], jnp.concatenate([high, high, low], axis=0), 1, 0)
-    out_ref[...] = (merged_ref[...] - low_rank).astype(bf16)
+    out_ref[...] = (merged_ref[...].astype(f32) - low_rank).astype(bf16)
 
 
 def swapped(array):
@@ -280,15 +298,23 @@
     replicas = lax.axis_size(DP)
     rows = own.shape[0] // 2
     tokens = hidden_act.shape[0]
-    place = jnp.stack([lax.axis_index("mp_0"), lax.axis_index("mp_1")]).astype(jnp.int32)
-
-    prior = jnp.concatenate(halves(prior_right), axis=1)
-    proj = product(grad_out, prior, 1, 0)
-    proj = jnp.concatenate(halves(proj[:, :rank] + proj[:, rank:]), axis=1)
-    proj = sent_to_all(proj, MP).reshape(-1, 2 * rank)
+
+    proj = call(
+        proj_kernel,
+        of((lax.axis_size("mp_0"), grad_out.shape[0], 2 * rank), bf16),
+        in_specs=[whole, whole],
+        out_specs=whole,
+        name="proj",
+    )(grad_out, prior_right.T)
+    left = product(own, jnp.concatenate(halves(prior_right), axis=1), 1, 0)
+    proj, left = lax.optimization_barrier((sent(proj, "mp_0"), left))
     ring = Ring(grad_out)
     proj = ring.step(proj)
-    left = product(own, prior, 1, 0) + product(hidden_act, proj, 0, 0)
+    other = swapped(proj)
+    first = lax.axis_index("mp_1") == 0
+    proj = jnp.stack([jnp.where(first, proj, other), jnp.where(first, other, proj)], axis=1)
+    proj = proj.reshape(-1, 2 * rank)
+    left = left + product(hidden_act, proj, 0, 0)
     left = left[:, :rank] + left[:, rank:]
     left = jnp.concatenate([left[:rows], left[rows:]], axis=1).astype(bf16)
     parts = sent_to_all(left, DP)
@@ -298,35 +324,40 @@
 
     width = features // 4
     half = tokens // 2
-    left, gram, keep, give, right = call(
+    left, turned, gram, keep, give = call(
         left_kernel,
         (
             of((rows, 2 * rank), bf16),
+            of((2 * rank, rows), bf16),
             of((rank // 2, 2 * rank), f32),
             of((half, 2 * rank), bf16),
             of((half, 2 * rank), bf16),
-            of((rank, features), f32),
         ),
-        limit=24,
-        in_specs=[scalars, whole, in_hbm, in_hbm],
+        limit=50,
+        in_specs=[whole, in_hbm],
         out_specs=(whole,) * 5,
-        scratch_shapes=[
-            VMEM(act.shape, bf16),
-            VMEM(own.shape, bf16),
-            pltpu.SemaphoreType.DMA((2,)),
-        ],
+        scratch_shapes=[VMEM(act.shape, bf16), pltpu.SemaphoreType.DMA],
         name="left_sum",
-    )(place, parts, act, own)
+    )(parts, act)
+    right = call(
+        own_kernel,
+        of((rank, features), f32),
+        limit=50,
+        in_specs=[whole, in_hbm],
+        out_specs=whole,
+        scratch_shapes=[VMEM(own.shape, bf16), pltpu.SemaphoreType.DMA((4,))],
+        name="own_product",
+    )(turned, own)
 
     right, half_out = call(
         functools.partial(right_kernel, len(chunks)),
         (of((16, rank // 4, width), bf16), of((half, features), bf16)),
-        limit=16,
-        in_specs=[scalars, whole, whole, whole] + [anywhere] * len(chunks),
+        limit=50,
+        in_specs=[whole, whole, whole] + [anywhere] * len(chunks),
         out_specs=(whole, in_hbm),
         scratch_shapes=[VMEM((half, features), bf16), pltpu.SemaphoreType.DMA((len(chunks) + 1,))],
         name="right_product",
-    )(place, keep, swapped(give), right, *chunks)
+    )(keep, swapped(give), right, *chunks)
 
     other_half = swapped(half_out)
     other_gram = swapped(gram)
@@ -335,11 +366,10 @@
     columns = pl.BlockSpec((half, width), lambda j: (0, j))
     merged = call(
         merged_kernel,
-        of(own.shape, f32),
+        of(own.shape, bf16),
         limit=58,
         grid=(4,),
         in_specs=[
-            scalars,
             pl.BlockSpec((2 * rows, tokens), lambda j: (0, 0)),
             pl.BlockSpec((2 * rows, width), lambda j: (0, j)),
             columns,
@@ -348,7 +378,7 @@
         out_specs=pl.BlockSpec((2 * rows, width), lambda j: (0, j)),
         scratch_shapes=[VMEM((tokens, width), bf16)],
         name="merged",
-    )(place, act, own, half_out, other_half)
+    )(act, own, half_out, other_half)
     right = call(
         replica_sum_kernel,
         of((rank // 4, width), bf16),
@@ -359,10 +389,10 @@
     right = call(
         core_sum_kernel,
         of((8, rank // 4, width + 384), bf16),
-        in_specs=[scalars] + [whole] * 4,
+        in_specs=[whole] * 4,
         out_specs=whole,
         name="core_sum",
-    )(place, right, swapped(right), gram, other_gram)
+    )(right, swapped(right), gram, other_gram)
     right, merged = lax.optimization_barrier((sent(right, "mp_0"), merged))
     right, gram = call(
         chip_sum_kernel,
@@ -372,13 +402,13 @@
         name="chip_sum",
     )(right)
     right = sent(right, DP)
-    inverse = call(
+    inverse, ortho = call(
         inverse_kernel,
-        of((rank, rank), f32),
-        in_specs=[scalars, whole, whole],
-        out_specs=whole,
+        (of((rank, rank), f32), of((2 * rows, 3 * rank), bf16)),
+        in_specs=[whole] * 3,
+        out_specs=(whole, whole),
         name="inverse",
-    )(place, gram, swapped(gram))
+    )(gram, swapped(gram), left)
     right = right.reshape(4, 4, rank // 4, width)
 
     residual_out, next_right = call(
@@ -388,7 +418,7 @@
         grid=(4,),
         in_specs=[
             pl.BlockSpec((rank, rank), lambda j: (0, 0)),
-            pl.BlockSpec((rows, 2 * rank), lambda j: (0, 0)),
+            pl.BlockSpec((2 * rows, 3 * rank), lambda j: (0, 0)),
             pl.BlockSpec((4, 1, rank // 4, width), lambda j: (0, j, 0, 0)),
             pl.BlockSpec((2 * rows, width), lambda j: (0, j)),
         ],
@@ -396,9 +426,8 @@
             pl.BlockSpec((2 * rows, width), lambda j: (0, j)),
             pl.BlockSpec((rank, width), lambda j: (0, j)),
         ),
-        scratch_shapes=[VMEM((2 * rows, 3 * rank), bf16)],
         name="residual",
-    )(inverse, left, right, merged)
+    )(inverse, ortho, right, merged)
     return (residual_out[None], next_right.T)
 
 

time: 134 us -> 125 us (0.933)
  starting transfers between devices: 46.2 us -> 43.2 us
  other arithmetic: 2.28 us -> 0.41 us
    ppermute x7, waiting for transfers between devices: 21.7 us -> 13 us  [passed(): lax.ppermute(array, 'mp_0', [(i, (i + hop) % self.size) for i in range(se...]
    all_to_all x5, waiting for transfers between devices: 11.6 us -> 20.4 us  [sent(): return lax.all_to_all(array, axis, 0, 0, tiled=True)]
    all_to_all x5, starting transfers between devices: 28.5 us -> 23 us  [sent(): return lax.all_to_all(array, axis, 0, 0, tiled=True)]
    ppermute x7, starting transfers between devices: 8.2 us -> 12 us  [passed(): lax.ppermute(array, 'mp_0', [(i, (i + hop) % self.size) for i in range(se...]
    pallas_call x1, Pallas kernels: 8.14 us -> 6.6 us  [per_device(): call(functools.partial(residual_kernel, replicas), (of(own.shape, bf16),...]
    ppermute x5 -> x6, starting transfers between devices: 9.48 us -> 8.24 us  [swapped(): return lax.ppermute(array, 'mp_1', [(0, 1), (1, 0)])]
    dot_general x3 -> x2, matrix products: 5.47 us -> 4.31 us  [product(): lax.dot_general(left, right, (((left_dim,), (right_dim,)), ((), ())), pre...]
    pallas_call x4 -> x6, Pallas kernels: 20 us -> 20.3 us  [the longest x1 10.5 us: per_device(): call(merged_kernel, of(own.shape, bf16), limit=58, grid=(4,), in_specs=[p...]
  transfers between devices with their start and end apart: 17 -> 18, of which waited for: 10 -> 11; matrix products, arithmetic and copies ran while one was open for 3% -> 3% of each run, Pallas kernels for 14% -> 16%
where the time goes in v4:
time: 125 us; the launch traced here: 124 us
  starting transfers between devices  43.2 us (35%)
  waiting for transfers between devices  36.9 us (30%)
  Pallas kernels  31.7 us (25%)
  local copies, waits for them, and re-layouts  7.03 us (6%)
  matrix products  4.31 us (3%)
    all_to_all x5, starting transfers between devices, sent(): return lax.all_to_all(array, axis, 0, 0, tiled=True)  23 us
    all_to_all x5, waiting for transfers between devices, sent(): return lax.all_to_all(array, axis, 0, 0, tiled=True)  20.4 us
    ppermute x7, waiting for transfers between devices, passed(): lax.ppermute(array, 'mp_0', [(i, (i + hop) % self.size) for i in range(se...  13 us
    ppermute x7, starting transfers between devices, passed(): lax.ppermute(array, 'mp_0', [(i, (i + hop) % self.size) for i in range(se...  12 us
    pallas_call x1, Pallas kernels, per_device(): call(merged_kernel, of(own.shape, bf16), limit=58, grid=(4,), in_specs=[p...  10.5 us
    ppermute x6, starting transfers between devices, swapped(): return lax.ppermute(array, 'mp_1', [(0, 1), (1, 0)])  8.24 us
    pallas_call x1, Pallas kernels, per_device(): call(functools.partial(residual_kernel, replicas), (of(own.shape, bf16),...  6.6 us
    unnamed x32, local copies, waits for them, and re-layouts  5.56 us
  transfers between devices with their start and end apart: 18, of which 11 were waited for; matrix products, arithmetic and copies ran while one was open for 3% of the time, Pallas kernels for 16%

profile of v4, /device:TPU:1, one launch (start us, length us, event | category | flops | bytes accessed | tf_op | source)
XLA Modules:
  0.0 124.4 jit_solution(18141839131069241593)
XLA Ops:
  0.6 2.5 %collective-permute-start = (bf16[64,2560]{1,0:T(8,128)(2,1)}, bf16[64,2560]{1,0:T(8,128)(2,1)S(1)}, u32[]{:S(2)}, u32[]{:S(2)}) collective-permute-start(bf16[64,2560]{1,0:T(8,128)(2,1)} %refs_3_.1), channel_id=1, source_target_pairs={{0,2},{2,4},{4,6},{6,8},{8,10},{10,12},{12,14},{14,0},{1,3},{3,5},... | collective-permute-start | bytes 983048 | tf_op jit(solution)/shard_map/ppermute | solution.py:274
  3.2 4.0 %collective-permute-start.1 = (bf16[64,2560]{1,0:T(8,128)(2,1)}, bf16[64,2560]{1,0:T(8,128)(2,1)S(1)}, u32[]{:S(2)}, u32[]{:S(2)}) collective-permute-start(bf16[64,2560]{1,0:T(8,128)(2,1)} %refs_3_.1), channel_id=1, source_target_pairs={{0,14},{2,0},{4,2},{6,4},{8,6},{10,8},{12,10},{14,12},{1,15},{3,1}... | collective-permute-start | bytes 983048 | tf_op jit(solution)/shard_map/ppermute | solution.py:274
  7.2 1.1 copy-done.1
  8.3 1.0 copy-done.3
  9.3 1.1 proj.1
  10.3 5.2 %all-to-all-start = ((bf16[8,64,128]{2,1,0:T(8,128)(2,1)}), bf16[8,64,128]{2,1,0:T(8,128)(2,1)S(1)}, u32[]{:S(2)}, u32[]{:S(2)}) async-start(bf16[8,64,128]{2,1,0:T(8,128)(2,1)} %proj.1), calls=%async_computation | async-start | bytes 262144 | tf_op jit(solution)/shard_map/all_to_all | solution.py:32
  15.5 0.0 copy-done.2
  15.5 0.1 reduce-precision_convert_fusion
  15.6 0.0 copy-start
  15.6 3.7 %convolution_bitcast_fusion.1 = f32[864,128]{1,0:T(8,128)S(1)} fusion(bf16[2560,64]{0,1:T(8,128)(2,1)S(1)} %get-tuple-element.49, bf16[2560,64]{0,1:T(8,128)(2,1)S(1)} %get-tuple-element.48, bf16[1,864,2560]{2,1,0:T(8,128)(2,1)} %param.6), kind=kOutput, calls=%fused_computation.2 | convolution fusion | flops 567541760 | bytes 5521408 | tf_op jit(solution)/shard_map/dot_general | solution.py:26
  19.3 4.2 %all-to-all-done = bf16[8,64,128]{2,1,0:T(8,128)(2,1)S(1)} async-done(((bf16[8,64,128]{2,1,0:T(8,128)(2,1)}), bf16[8,64,128]{2,1,0:T(8,128)(2,1)S(1)}, u32[]{:S(2)}, u32[]{:S(2)}) %all-to-all-start) | async-done | bytes 131104 | tf_op jit(solution)/shard_map/all_to_all | solution.py:32
  23.5 0.0 collective-permute-done.refs_4_
  23.5 0.0 collective-permute-done.1.refs_10_
  23.5 0.0 copy-start.8
  23.5 2.7 %collective-permute-start.2 = (bf16[8,64,128]{2,1,0:T(8,128)(2,1)S(1)}, bf16[8,64,128]{2,1,0:T(8,128)(2,1)S(1)}, u32[]{:S(2)}, u32[]{:S(2)}) collective-permute-start(bf16[8,64,128]{2,1,0:T(8,128)(2,1)S(1)} %all-to-all-done), channel_id=1, source_target_pairs={{0,1},{1,0},{2,3},{3,2},{4,5},{5,4},{6,7},{7,6},{8,9},{9,8},{10,11... | collective-permute-start | bytes 393224 | tf_op jit(solution)/shard_map/ppermute | solution.py:264
  26.2 1.0 collective-permute-done.2
  27.3 0.0 copy-done
  27.3 0.6 fusion
  28.0 0.2 fusion.5
  28.2 0.1 pad_maximum_fusion.1
  28.3 1.4 %broadcast_in_dim.4 = bf16[16,432,128]{2,1,0:T(8,128)(2,1)} broadcast(bf16[432,128]{1,0:T(8,128)(2,1)S(1)} %pad_maximum_fusion.1), dimensions={1,2} | broadcast | bytes 1880064 | tf_op jit(solution)/shard_map/broadcast_in_dim | solution.py:37
  29.7 6.8 %all-to-all-start.1 = ((bf16[16,432,128]{2,1,0:T(8,128)(2,1)}), bf16[16,432,128]{2,1,0:T(8,128)(2,1)S(1)}, u32[]{:S(2)}, u32[]{:S(2)}) async-start(bf16[16,432,128]{2,1,0:T(8,128)(2,1)} %broadcast_in_dim.4), calls=%async_computation.1 | async-start | bytes 3538944 | tf_op jit(solution)/shard_map/all_to_all | solution.py:32
  36.5 0.4 collective-permute-start.4
  36.8 2.4 %collective-permute-start.7 = (bf16[64,2560]{1,0:T(8,128)(2,1)}, bf16[64,2560]{1,0:T(8,128)(2,1)}, u32[]{:S(2)}, u32[]{:S(2)}) collective-permute-start(bf16[64,2560]{1,0:T(8,128)(2,1)} %copy-done.8), channel_id=1, source_target_pairs={{0,14},{2,0},{4,2},{6,4},{8,6},{10,8},{12,10},{14,12},{1,15},{3,1}... | collective-permute-start | bytes 983048 | tf_op jit(solution)/shard_map/ppermute | solution.py:274
  39.2 7.4 %collective-permute-done.4.refs_5_ = bf16[64,2560]{1,0:T(8,128)(2,1)S(1)} collective-permute-done((bf16[64,2560]{1,0:T(8,128)(2,1)}, bf16[64,2560]{1,0:T(8,128)(2,1)S(1)}, u32[]{:S(2)}, u32[]{:S(2)}) %collective-permute-start.4) | collective-permute-done | bytes 327712 | tf_op jit(solution)/shard_map/ppermute | solution.py:274
  46.6 0.0 collective-permute-start.5
  46.6 0.7 copy-done.10
  47.3 0.0 collective-permute-done.7.refs_9_
  47.3 2.7 %collective-permute-start.8 = (bf16[64,2560]{1,0:T(8,128)(2,1)}, bf16[64,2560]{1,0:T(8,128)(2,1)}, u32[]{:S(2)}, u32[]{:S(2)}) collective-permute-start(bf16[64,2560]{1,0:T(8,128)(2,1)} %collective-permute-done.7.refs_9_), channel_id=1, source_target_pairs={{0,14},{2,0},{4,2},{6,4},{8,6},{10,8},{12,10},{14,12},{1,15},{3,1}... | collective-permute-start | bytes 983048 | tf_op jit(solution)/shard_map/ppermute | solution.py:274
  50.0 5.6 %collective-permute-done.5.refs_6_ = bf16[64,2560]{1,0:T(8,128)(2,1)} collective-permute-done((bf16[64,2560]{1,0:T(8,128)(2,1)S(1)}, bf16[64,2560]{1,0:T(8,128)(2,1)}, u32[]{:S(2)}, u32[]{:S(2)}) %collective-permute-start.5) | collective-permute-done | bytes 327712 | tf_op jit(solution)/shard_map/ppermute | solution.py:274
  55.6 0.0 collective-permute-start.6
  55.6 5.9 %all-to-all-done.1.parts_ref = bf16[16,432,128]{2,1,0:T(8,128)(2,1)S(1)} async-done(((bf16[16,432,128]{2,1,0:T(8,128)(2,1)}), bf16[16,432,128]{2,1,0:T(8,128)(2,1)S(1)}, u32[]{:S(2)}, u32[]{:S(2)}) %all-to-all-start.1) | async-done | bytes 1769504 | tf_op jit(solution)/shard_map/all_to_all | solution.py:32
  61.5 1.7 %left_sum.1 = (bf16[432,128]{1,0:T(8,128)(2,1)S(1)}, bf16[128,432]{1,0:T(8,128)(2,1)S(1)}, f32[32,128]{1,0:T(8,128)S(1)}, bf16[512,128]{1,0:T(8,128)(2,1)S(1)}, bf16[512,128]{1,0:T(8,128)(2,1)S(1)}) custom-call(bf16[16,432,128]{2,1,0:T(8,128)(2,1)S(1)} %all-to-all-done.1.parts_ref, bf16[864,1024]{1,0:T(8,128)(2,1)S(1)} %bitcast.22), custom_call_target="tpu_custom_call" | custom-call | tf_op jit(solution)/shard_map/left_sum/pallas_call | solution.py:327
  63.2 0.0 copy-start.12
  63.2 0.6 copy-done.12
  63.8 2.5 %collective-permute-start.3 = (bf16[512,128]{1,0:T(8,128)(2,1)S(1)}, bf16[512,128]{1,0:T(8,128)(2,1)S(1)}, u32[]{:S(2)}, u32[]{:S(2)}) collective-permute-start(bf16[512,128]{1,0:T(8,128)(2,1)S(1)} %get-tuple-element.29), channel_id=1, source_target_pairs={{0,1},{1,0},{2,3},{3,2},{4,5},{5,4},{6,7},{7,6},{8,9},{9,8},{10,11... | collective-permute-start | bytes 393224 | tf_op jit(solution)/shard_map/ppermute | solution.py:264
  66.3 2.7 %own_product.1.refs_2_ = f32[64,2560]{1,0:T(8,128)S(1)} custom-call(bf16[128,432]{1,0:T(8,128)(2,1)S(1)} %get-tuple-element.30.turned_ref, bf16[864,2560]{1,0:T(8,128)(2,1)} %bitcast.24), custom_call_target="tpu_custom_call" | custom-call | tf_op jit(solution)/shard_map/own_product/pallas_call | solution.py:342
  69.1 0.0 collective-permute-done.8.refs_8_
  69.1 0.0 collective-permute-done.6.refs_7_
  69.1 0.0 collective-permute-done.3.refs_1_
  69.1 3.9 %right_product.1 = (bf16[16,16,640]{2,1,0:T(8,128)(2,1)}, bf16[512,2560]{1,0:T(8,128)(2,1)}) custom-call(bf16[512,128]{1,0:T(8,128)(2,1)S(1)} %get-tuple-element.28.refs_0_, bf16[512,128]{1,0:T(8,128)(2,1)S(1)} %collective-permute-done.3.refs_1_, f32[64,2560]{1,0:T(8,128)S(1)} %own_product.1.refs_2_, bf16[64,2560]{1,0:T(8,128)(2,1)S(1)} %copy-done.4, ...), custom_call_target="tpu_custom_call" | custom-call | tf_op jit(solution)/shard_map/right_product/pallas_call | solution.py:352
  73.1 0.1 collective-permute-start.9
  73.2 4.1 %all-to-all-start.2 = ((bf16[16,16,640]{2,1,0:T(8,128)(2,1)}), bf16[16,16,640]{2,1,0:T(8,128)(2,1)S(1)}, u32[]{:S(2)}, u32[]{:S(2)}) async-start(bf16[16,16,640]{2,1,0:T(8,128)(2,1)} %get-tuple-element.33), calls=%async_computation.2 | async-start | bytes 655360 | tf_op jit(solution)/shard_map/all_to_all | solution.py:32
  77.3 0.4 collective-permute-start.10
  77.7 0.9 collective-permute-done.10.other_gram_ref
  78.5 7.1 %all-to-all-done.2.parts_ref = bf16[16,16,640]{2,1,0:T(8,128)(2,1)S(1)} async-done(((bf16[16,16,640]{2,1,0:T(8,128)(2,1)}), bf16[16,16,640]{2,1,0:T(8,128)(2,1)S(1)}, u32[]{:S(2)}, u32[]{:S(2)}) %all-to-all-start.2) | async-done | bytes 327712 | tf_op jit(solution)/shard_map/all_to_all | solution.py:32
  85.6 0.0 collective-permute-done.9.other_ref
  85.6 0.1 replica_sum.1.own_ref
  85.7 1.9 %collective-permute-start.11 = (bf16[16,640]{1,0:T(8,128)(2,1)S(1)}, bf16[16,640]{1,0:T(8,128)(2,1)S(1)}, u32[]{:S(2)}, u32[]{:S(2)}) collective-permute-start(bf16[16,640]{1,0:T(8,128)(2,1)S(1)} %replica_sum.1.own_ref), channel_id=1, source_target_pairs={{0,1},{1,0},{2,3},{3,2},{4,5},{5,4},{6,7},{7,6},{8,9},{9,8},{10,11... | collective-permute-start | bytes 61448 | tf_op jit(solution)/shard_map/ppermute | solution.py:264
  87.5 0.8 collective-permute-done.11.other_ref
  88.4 0.7 core_sum.1
  89.1 3.4 %all-to-all-start.3 = ((bf16[8,16,1024]{2,1,0:T(8,128)(2,1)}), bf16[8,16,1024]{2,1,0:T(8,128)(2,1)S(1)}, u32[]{:S(2)}, u32[]{:S(2)}) async-start(bf16[8,16,1024]{2,1,0:T(8,128)(2,1)} %core_sum.1), calls=%async_computation.3 | async-start | bytes 524288 | tf_op jit(solution)/shard_map/all_to_all | solution.py:32
  92.5 10.5 %merged.1.merged_ref = bf16[864,2560]{1,0:T(8,128)(2,1)} custom-call(bf16[864,1024]{1,0:T(8,128)(2,1)} %bitcast.21, bf16[864,2560]{1,0:T(8,128)(2,1)} %bitcast.25, bf16[512,2560]{1,0:T(8,128)(2,1)} %get-tuple-element.34.half_ref, bf16[512,2560]{1,0:T(8,128)(2,1)} %collective-permute-done.9.other_ref), custom_call_target="tpu_custom_call" | custom-call | tf_op jit(solution)/shard_map/merged/pallas_call | solution.py:367
  103.1 1.7 %all-to-all-done.3.parts_ref = bf16[8,16,1024]{2,1,0:T(8,128)(2,1)S(1)} async-done(((bf16[8,16,1024]{2,1,0:T(8,128)(2,1)}), bf16[8,16,1024]{2,1,0:T(8,128)(2,1)S(1)}, u32[]{:S(2)}, u32[]{:S(2)}) %all-to-all-start.3) | async-done | bytes 262176 | tf_op jit(solution)/shard_map/all_to_all | solution.py:32
  104.8 0.8 chip_sum.1
  105.6 3.5 %all-to-all-start.4 = ((bf16[16,16,640]{2,1,0:T(8,128)(2,1)}), bf16[16,16,640]{2,1,0:T(8,128)(2,1)S(1)}, u32[]{:S(2)}, u32[]{:S(2)}) async-start(bf16[16,16,640]{2,1,0:T(8,128)(2,1)} %get-tuple-element.44), calls=%async_computation.4 | async-start | bytes 655360 | tf_op jit(solution)/shard_map/all_to_all | solution.py:32
  109.1 0.7 collective-permute-start.12
  109.8 0.8 collective-permute-done.12.other_ref
  110.6 3.6 %inverse.1 = (f32[64,64]{1,0:T(8,128)S(1)}, bf16[864,192]{1,0:T(8,128)(2,1)S(1)}) custom-call(f32[16,128]{1,0:T(8,128)S(1)} %get-tuple-element.40.gram_ref, f32[16,128]{1,0:T(8,128)S(1)} %collective-permute-done.12.other_ref, bf16[432,128]{1,0:T(8,128)(2,1)S(1)} %copy-done.13), custom_call_target="tpu_custom_call" | custom-call | tf_op jit(solution)/shard_map/inverse/pallas_call | solution.py:405
  114.2 0.8 copy-done.5
  115.0 0.6 copy-done.14
  115.6 1.5 %all-to-all-done.4 = bf16[16,16,640]{2,1,0:T(8,128)(2,1)S(1)} async-done(((bf16[16,16,640]{2,1,0:T(8,128)(2,1)}), bf16[16,16,640]{2,1,0:T(8,128)(2,1)S(1)}, u32[]{:S(2)}, u32[]{:S(2)}) %all-to-all-start.4) | async-done | bytes 327712 | tf_op jit(solution)/shard_map/all_to_all | solution.py:32
  117.1 0.7 copy-done.15
  117.8 6.6 %residual.1 = (bf16[864,2560]{1,0:T(8,128)(2,1)}, f32[64,2560]{1,0:T(8,128)}) custom-call(f32[64,64]{1,0:T(8,128)} %copy-done.14, bf16[864,192]{1,0:T(8,128)(2,1)} %copy-done.5, bf16[4,4,16,640]{3,2,1,0:T(8,128)(2,1)} %bitcast.26, bf16[864,2560]{1,0:T(8,128)(2,1)} %merged.1.merged_ref), custom_call_target="tpu_custom_call" | custom-call | tf_op jit(solution)/shard_map/residual/pallas_call | solution.py:414
  (24 shorter events, 0.1 us)
Async XLA Ops:
  0.6 22.9 %collective-permute-start = (bf16[64,2560]{1,0:T(8,128)(2,1)}, bf16[64,2560]{1,0:T(8,128)(2,1)S(1)}, u32[]{:S(2)}, u32[]{:S(2)}) collective-permute-start(bf16[64,2560]{1,0:T(8,128)(2,1)} %refs_3_.1), channel_id=1, source_target_pairs={{0,2},{2,4},{4,6},{6,8},{8,10},{10,12},{12,14},{14,0},{1,3},{3,5},... | collective-permute-start | bytes 983048 | tf_op jit(solution)/shard_map/ppermute | solution.py:274
  3.2 20.3 %collective-permute-start.1 = (bf16[64,2560]{1,0:T(8,128)(2,1)}, bf16[64,2560]{1,0:T(8,128)(2,1)S(1)}, u32[]{:S(2)}, u32[]{:S(2)}) collective-permute-start(bf16[64,2560]{1,0:T(8,128)(2,1)} %refs_3_.1), channel_id=1, source_target_pairs={{0,14},{2,0},{4,2},{6,4},{8,6},{10,8},{12,10},{14,12},{1,15},{3,1}... | collective-permute-start | bytes 983048 | tf_op jit(solution)/shard_map/ppermute | solution.py:274
  7.2 1.1 copy-start.1
  8.3 1.0 copy-start.3
  9.3 6.3 %copy-start.2 = (f32[2560,64]{0,1:T(8,128)S(1)}, f32[2560,64]{0,1:T(8,128)}, u32[]{:S(2)}) copy-start(f32[2560,64]{0,1:T(8,128)} %param.7) | copy-start | bytes 1966084
  10.3 13.2 %all-to-all-start = ((bf16[8,64,128]{2,1,0:T(8,128)(2,1)}), bf16[8,64,128]{2,1,0:T(8,128)(2,1)S(1)}, u32[]{:S(2)}, u32[]{:S(2)}) async-start(bf16[8,64,128]{2,1,0:T(8,128)(2,1)} %proj.1), calls=%async_computation | async-start | bytes 262144 | tf_op jit(solution)/shard_map/all_to_all | solution.py:32
  15.6 11.7 %copy-start = (bf16[1024,864]{0,1:T(8,128)(2,1)S(1)}, bf16[1024,864]{0,1:T(8,128)(2,1)}, u32[]{:S(2)}) copy-start(bf16[1024,864]{0,1:T(8,128)(2,1)} %param.5) | copy-start | bytes 5308420
  23.5 4.5 %copy-start.6 = (bf16[64,2560]{1,0:T(8,128)(2,1)}, bf16[64,2560]{1,0:T(8,128)(2,1)S(1)}, u32[]{:S(2)}) copy-start(bf16[64,2560]{1,0:T(8,128)(2,1)S(1)} %collective-permute-done.refs_4_) | copy-start | bytes 983044
  23.5 4.5 %copy-start.8 = (bf16[64,2560]{1,0:T(8,128)(2,1)}, bf16[64,2560]{1,0:T(8,128)(2,1)S(1)}, u32[]{:S(2)}) copy-start(bf16[64,2560]{1,0:T(8,128)(2,1)S(1)} %collective-permute-done.1.refs_10_) | copy-start | bytes 983044
  23.5 3.7 %collective-permute-start.2 = (bf16[8,64,128]{2,1,0:T(8,128)(2,1)S(1)}, bf16[8,64,128]{2,1,0:T(8,128)(2,1)S(1)}, u32[]{:S(2)}, u32[]{:S(2)}) collective-permute-start(bf16[8,64,128]{2,1,0:T(8,128)(2,1)S(1)} %all-to-all-done), channel_id=1, source_target_pairs={{0,1},{1,0},{2,3},{3,2},{4,5},{5,4},{6,7},{7,6},{8,9},{9,8},{10,11... | collective-permute-start | bytes 393224 | tf_op jit(solution)/shard_map/ppermute | solution.py:264
  29.7 31.8 %all-to-all-start.1 = ((bf16[16,432,128]{2,1,0:T(8,128)(2,1)}), bf16[16,432,128]{2,1,0:T(8,128)(2,1)S(1)}, u32[]{:S(2)}, u32[]{:S(2)}) async-start(bf16[16,432,128]{2,1,0:T(8,128)(2,1)} %broadcast_in_dim.4), calls=%async_computation.1 | async-start | bytes 3538944 | tf_op jit(solution)/shard_map/all_to_all | solution.py:32
  36.5 10.1 %collective-permute-start.4 = (bf16[64,2560]{1,0:T(8,128)(2,1)}, bf16[64,2560]{1,0:T(8,128)(2,1)S(1)}, u32[]{:S(2)}, u32[]{:S(2)}) collective-permute-start(bf16[64,2560]{1,0:T(8,128)(2,1)} %copy-done.6), channel_id=1, source_target_pairs={{0,2},{2,4},{4,6},{6,8},{8,10},{10,12},{12,14},{14,0},{1,3},{3,5},... | collective-permute-start | bytes 983048 | tf_op jit(solution)/shard_map/ppermute | solution.py:274
  36.8 10.5 %collective-permute-start.7 = (bf16[64,2560]{1,0:T(8,128)(2,1)}, bf16[64,2560]{1,0:T(8,128)(2,1)}, u32[]{:S(2)}, u32[]{:S(2)}) collective-permute-start(bf16[64,2560]{1,0:T(8,128)(2,1)} %copy-done.8), channel_id=1, source_target_pairs={{0,14},{2,0},{4,2},{6,4},{8,6},{10,8},{12,10},{14,12},{1,15},{3,1}... | collective-permute-start | bytes 983048 | tf_op jit(solution)/shard_map/ppermute | solution.py:274
  46.6 9.0 %collective-permute-start.5 = (bf16[64,2560]{1,0:T(8,128)(2,1)S(1)}, bf16[64,2560]{1,0:T(8,128)(2,1)}, u32[]{:S(2)}, u32[]{:S(2)}) collective-permute-start(bf16[64,2560]{1,0:T(8,128)(2,1)S(1)} %collective-permute-done.4.refs_5_), channel_id=1, source_target_pairs={{0,2},{2,4},{4,6},{6,8},{8,10},{10,12},{12,14},{14,0},{1,3},{3,5},... | collective-permute-start | bytes 983048 | tf_op jit(solution)/shard_map/ppermute | solution.py:274
  46.6 0.7 copy-start.10
  47.3 21.7 %collective-permute-start.8 = (bf16[64,2560]{1,0:T(8,128)(2,1)}, bf16[64,2560]{1,0:T(8,128)(2,1)}, u32[]{:S(2)}, u32[]{:S(2)}) collective-permute-start(bf16[64,2560]{1,0:T(8,128)(2,1)} %collective-permute-done.7.refs_9_), channel_id=1, source_target_pairs={{0,14},{2,0},{4,2},{6,4},{8,6},{10,8},{12,10},{14,12},{1,15},{3,1}... | collective-permute-start | bytes 983048 | tf_op jit(solution)/shard_map/ppermute | solution.py:274
  55.6 13.5 %collective-permute-start.6 = (bf16[64,2560]{1,0:T(8,128)(2,1)}, bf16[64,2560]{1,0:T(8,128)(2,1)}, u32[]{:S(2)}, u32[]{:S(2)}) collective-permute-start(bf16[64,2560]{1,0:T(8,128)(2,1)} %collective-permute-done.5.refs_6_), channel_id=1, source_target_pairs={{0,2},{2,4},{4,6},{6,8},{8,10},{10,12},{12,14},{14,0},{1,3},{3,5},... | collective-permute-start | bytes 983048 | tf_op jit(solution)/shard_map/ppermute | solution.py:274
  63.2 0.7 copy-start.12
  63.8 5.2 %collective-permute-start.3 = (bf16[512,128]{1,0:T(8,128)(2,1)S(1)}, bf16[512,128]{1,0:T(8,128)(2,1)S(1)}, u32[]{:S(2)}, u32[]{:S(2)}) collective-permute-start(bf16[512,128]{1,0:T(8,128)(2,1)S(1)} %get-tuple-element.29), channel_id=1, source_target_pairs={{0,1},{1,0},{2,3},{3,2},{4,5},{5,4},{6,7},{7,6},{8,9},{9,8},{10,11... | collective-permute-start | bytes 393224 | tf_op jit(solution)/shard_map/ppermute | solution.py:264
  66.3 2.8 %copy-start.4 = (bf16[64,2560]{1,0:T(8,128)(2,1)S(1)}, bf16[64,2560]{1,0:T(8,128)(2,1)}, u32[]{:S(2)}) copy-start(bf16[64,2560]{1,0:T(8,128)(2,1)} %refs_3_.1) | copy-start | bytes 983044
  66.3 2.8 %copy-start.7 = (bf16[64,2560]{1,0:T(8,128)(2,1)S(1)}, bf16[64,2560]{1,0:T(8,128)(2,1)}, u32[]{:S(2)}) copy-start(bf16[64,2560]{1,0:T(8,128)(2,1)} %copy-done.6) | copy-start | bytes 983044
  66.3 2.8 %copy-start.9 = (bf16[64,2560]{1,0:T(8,128)(2,1)S(1)}, bf16[64,2560]{1,0:T(8,128)(2,1)}, u32[]{:S(2)}) copy-start(bf16[64,2560]{1,0:T(8,128)(2,1)} %copy-done.8) | copy-start | bytes 983044
  66.3 2.8 %copy-start.11 = (bf16[64,2560]{1,0:T(8,128)(2,1)S(1)}, bf16[64,2560]{1,0:T(8,128)(2,1)}, u32[]{:S(2)}) copy-start(bf16[64,2560]{1,0:T(8,128)(2,1)} %copy-done.10) | copy-start | bytes 983044
  73.1 12.5 %collective-permute-start.9 = (bf16[512,2560]{1,0:T(8,128)(2,1)}, bf16[512,2560]{1,0:T(8,128)(2,1)}, u32[]{:S(2)}, u32[]{:S(2)}) collective-permute-start(bf16[512,2560]{1,0:T(8,128)(2,1)} %get-tuple-element.34.half_ref), channel_id=1, source_target_pairs={{0,1},{1,0},{2,3},{3,2},{4,5},{5,4},{6,7},{7,6},{8,9},{9,8},{10,11... | collective-permute-start | bytes 7864328 | tf_op jit(solution)/shard_map/ppermute | solution.py:264
  73.2 12.4 %all-to-all-start.2 = ((bf16[16,16,640]{2,1,0:T(8,128)(2,1)}), bf16[16,16,640]{2,1,0:T(8,128)(2,1)S(1)}, u32[]{:S(2)}, u32[]{:S(2)}) async-start(bf16[16,16,640]{2,1,0:T(8,128)(2,1)} %get-tuple-element.33), calls=%async_computation.2 | async-start | bytes 655360 | tf_op jit(solution)/shard_map/all_to_all | solution.py:32
  77.3 1.3 %collective-permute-start.10 = (f32[32,128]{1,0:T(8,128)S(1)}, f32[32,128]{1,0:T(8,128)S(1)}, u32[]{:S(2)}, u32[]{:S(2)}) collective-permute-start(f32[32,128]{1,0:T(8,128)S(1)} %get-tuple-element.35.gram_ref), channel_id=1, source_target_pairs={{0,1},{1,0},{2,3},{3,2},{4,5},{5,4},{6,7},{7,6},{8,9},{9,8},{10,11... | collective-permute-start | bytes 49160 | tf_op jit(solution)/shard_map/ppermute | solution.py:264
  85.7 2.7 %collective-permute-start.11 = (bf16[16,640]{1,0:T(8,128)(2,1)S(1)}, bf16[16,640]{1,0:T(8,128)(2,1)S(1)}, u32[]{:S(2)}, u32[]{:S(2)}) collective-permute-start(bf16[16,640]{1,0:T(8,128)(2,1)S(1)} %replica_sum.1.own_ref), channel_id=1, source_target_pairs={{0,1},{1,0},{2,3},{3,2},{4,5},{5,4},{6,7},{7,6},{8,9},{9,8},{10,11... | collective-permute-start | bytes 61448 | tf_op jit(solution)/shard_map/ppermute | solution.py:264
  89.1 15.7 %all-to-all-start.3 = ((bf16[8,16,1024]{2,1,0:T(8,128)(2,1)}), bf16[8,16,1024]{2,1,0:T(8,128)(2,1)S(1)}, u32[]{:S(2)}, u32[]{:S(2)}) async-start(bf16[8,16,1024]{2,1,0:T(8,128)(2,1)} %core_sum.1), calls=%async_computation.3 | async-start | bytes 524288 | tf_op jit(solution)/shard_map/all_to_all | solution.py:32
  92.5 18.1 %copy-start.13 = (bf16[432,128]{1,0:T(8,128)(2,1)S(1)}, bf16[432,128]{1,0:T(8,128)(2,1)}, u32[]{:S(2)}) copy-start(bf16[432,128]{1,0:T(8,128)(2,1)} %copy-done.12) | copy-start | bytes 331780
  105.6 11.5 %all-to-all-start.4 = ((bf16[16,16,640]{2,1,0:T(8,128)(2,1)}), bf16[16,16,640]{2,1,0:T(8,128)(2,1)S(1)}, u32[]{:S(2)}, u32[]{:S(2)}) async-start(bf16[16,16,640]{2,1,0:T(8,128)(2,1)} %get-tuple-element.44), calls=%async_computation.4 | async-start | bytes 655360 | tf_op jit(solution)/shard_map/all_to_all | solution.py:32
  109.1 1.5 %collective-permute-start.12 = (f32[16,128]{1,0:T(8,128)S(1)}, f32[16,128]{1,0:T(8,128)S(1)}, u32[]{:S(2)}, u32[]{:S(2)}) collective-permute-start(f32[16,128]{1,0:T(8,128)S(1)} %get-tuple-element.40.gram_ref), channel_id=1, source_target_pairs={{0,1},{1,0},{2,3},{3,2},{4,5},{5,4},{6,7},{7,6},{8,9},{9,8},{10,11... | collective-permute-start | bytes 24584 | tf_op jit(solution)/shard_map/ppermute | solution.py:264
  114.2 0.8 copy-start.5
  115.0 0.6 copy-start.14
  117.1 0.7 copy-start.15

commit v5 on v4

--- a/solution.py
+++ b/solution.py
@@ -89,14 +89,16 @@
 
 
 def left_kernel(
-    parts_ref, act_hbm, left_ref, turned_ref, gram_ref, keep_ref, give_ref, act_ref, sem
+    parts_ref, act_hbm, left_hbm, turned_ref, gram_ref, keep_ref, give_ref, act_ref, left_ref, sems
 ):
-    act_copy = pltpu.make_async_copy(act_hbm, act_ref, sem)
+    act_copy = pltpu.make_async_copy(act_hbm, act_ref, sems.at[0])
     act_copy.start()
     rows, lanes = left_ref.shape
     rank = lanes // 2
     left = total_of(parts_ref).astype(bf16)
     left_ref[...] = left
+    left_copy = pltpu.make_async_copy(left_ref, left_hbm, sems.at[1])
+    left_copy.start()
     turned = left.astype(f32).T.astype(bf16)
     gram = product(left, left, 0, 0)
     gram = gram[:rank, :rank] + gram[rank:, rank:]
@@ -113,6 +115,7 @@
         keep_ref[z * tokens : (z + 1) * tokens, :] = jnp.where(first, near, far)
         give_ref[z * tokens : (z + 1) * tokens, :] = jnp.where(first, far, near)
     turned_ref[...] = turned
+    left_copy.wait()
 
 
 def own_kernel(turned_ref, own_hbm, right_ref, own_ref, sems):
@@ -175,6 +178,12 @@
     for i in range(1, parts_ref.shape[0]):
         total = total + parts_ref[i].astype(f32)
     return total
+
+
+def row_sum_kernel(parts_ref, out_ref):
+    total = total_of(parts_ref).astype(bf16)
+    for i in range(out_ref.shape[0]):
+        out_ref[i] = total
 
 
 def replica_sum_kernel(parts_ref, out_ref):
@@ -250,7 +259,8 @@
 
 
 def residual_kernel(replicas, inverse_ref, ortho_ref, right_ref, merged_ref, out_ref, next_ref):
-    right = jnp.concatenate([right_ref[a, 0] for a in range(4)], axis=0).astype(f32)
+    step = pl.program_id(0)
+    right = jnp.concatenate([right_ref[a, step] for a in range(4)], axis=0).astype(f32)
     turned = jnp.dot(
         inverse_ref[...], right, precision=highest, preferred_element_type=f32
     ) * (1.0 / replicas)
@@ -302,6 +312,7 @@
     proj = call(
         proj_kernel,
         of((lax.axis_size("mp_0"), grad_out.shape[0], 2 * rank), bf16),
+        limit=63,
         in_specs=[whole, whole],
         out_specs=whole,
         name="proj",
@@ -317,7 +328,14 @@
     left = left + product(hidden_act, proj, 0, 0)
     left = left[:, :rank] + left[:, rank:]
     left = jnp.concatenate([left[:rows], left[rows:]], axis=1).astype(bf16)
-    parts = sent_to_all(left, DP)
+    left = call(
+        row_sum_kernel,
+        of((lax.axis_size("dp_1"), *left.shape), bf16),
+        in_specs=[whole],
+        out_specs=whole,
+        name="row_sum",
+    )(sent_to_all(left, "dp_0"))
+    parts = sent(left, "dp_1")
     for _ in range(3):
         ring.step()
     chunks = ring.all()
@@ -335,8 +353,12 @@
         ),
         limit=50,
         in_specs=[whole, in_hbm],
-        out_specs=(whole,) * 5,
-        scratch_shapes=[VMEM(act.shape, bf16), pltpu.SemaphoreType.DMA],
+        out_specs=(in_hbm,) + (whole,) * 4,
+        scratch_shapes=[
+            VMEM(act.shape, bf16),
+            VMEM((rows, 2 * rank), bf16),
+            pltpu.SemaphoreType.DMA((2,)),
+        ],
         name="left_sum",
     )(parts, act)
     right = call(
@@ -417,9 +439,9 @@
         limit=58,
         grid=(4,),
         in_specs=[
-            pl.BlockSpec((rank, rank), lambda j: (0, 0)),
-            pl.BlockSpec((2 * rows, 3 * rank), lambda j: (0, 0)),
-            pl.BlockSpec((4, 1, rank // 4, width), lambda j: (0, j, 0, 0)),
+            whole,
+            whole,
+            whole,
             pl.BlockSpec((2 * rows, width), lambda j: (0, j)),
         ],
         out_specs=(

time: 125 us -> 116 us (0.928)
  waiting for transfers between devices: 36.9 us -> 27.6 us
  local copies, waits for them, and re-layouts: 7.03 us -> 3 us
  Pallas kernels: 31.7 us -> 33.4 us
    ppermute x7, waiting for transfers between devices: 13 us -> 1.92 us  [passed(): lax.ppermute(array, 'mp_0', [(i, (i + hop) % self.size) for i in range(se...]
    unnamed x32 -> x14, local copies, waits for them, and re-layouts: 5.56 us -> 2.15 us
    all_to_all x5 -> x6, waiting for transfers between devices: 20.4 us -> 22.5 us  [sent(): return lax.all_to_all(array, axis, 0, 0, tiled=True)]
    all_to_all x5 -> x6, starting transfers between devices: 23 us -> 24.8 us  [sent(): return lax.all_to_all(array, axis, 0, 0, tiled=True)]
    ppermute x7, starting transfers between devices: 12 us -> 10.3 us  [passed(): lax.ppermute(array, 'mp_0', [(i, (i + hop) % self.size) for i in range(se...]
  transfers between devices with their start and end apart: 18 -> 19, of which waited for: 11 -> 11; matrix products, arithmetic and copies ran while one was open for 3% -> 6% of each run, Pallas kernels for 16% -> 19%
where the time goes in v5:
time: 116 us; the launch traced here: 115 us
  starting transfers between devices  44.1 us (38%)
  Pallas kernels  33.4 us (29%)
  waiting for transfers between devices  27.6 us (24%)
  matrix products  4.3 us (4%)
  local copies, waits for them, and re-layouts  3 us (3%)
  other arithmetic  1.5 us (1%)
    all_to_all x6, starting transfers between devices, sent(): return lax.all_to_all(array, axis, 0, 0, tiled=True)  24.8 us
    all_to_all x6, waiting for transfers between devices, sent(): return lax.all_to_all(array, axis, 0, 0, tiled=True)  22.5 us
    pallas_call x1, Pallas kernels, per_device(): call(merged_kernel, of(own.shape, bf16), limit=58, grid=(4,), in_specs=[p...  10.5 us
    ppermute x7, starting transfers between devices, passed(): lax.ppermute(array, 'mp_0', [(i, (i + hop) % self.size) for i in range(se...  10.3 us
    ppermute x6, starting transfers between devices, swapped(): return lax.ppermute(array, 'mp_1', [(0, 1), (1, 0)])  9 us
    pallas_call x1, Pallas kernels, per_device(): call(functools.partial(residual_kernel, replicas), (of(own.shape, bf16),...  6.54 us
    dot_general x2, matrix products, product(): lax.dot_general(left, right, (((left_dim,), (right_dim,)), ((), ())), pre...  4.3 us
    pallas_call x1, Pallas kernels, per_device(): call(functools.partial(right_kernel, len(chunks)), (of((16, rank // 4, wi...  3.82 us
  transfers between devices with their start and end apart: 19, of which 11 were waited for; matrix products, arithmetic and copies ran while one was open for 6% of the time, Pallas kernels for 19%

profile of v5, /device:TPU:1, one launch (start us, length us, event | category | flops | bytes accessed | tf_op | source)
XLA Modules:
  0.0 114.8 jit_solution(16808843387334525642)
XLA Ops:
  0.6 2.5 %collective-permute-start = (bf16[64,2560]{1,0:T(8,128)(2,1)}, bf16[64,2560]{1,0:T(8,128)(2,1)S(1)}, u32[]{:S(2)}, u32[]{:S(2)}) collective-permute-start(bf16[64,2560]{1,0:T(8,128)(2,1)} %refs_3_.1), channel_id=1, source_target_pairs={{0,2},{2,4},{4,6},{6,8},{8,10},{10,12},{12,14},{14,0},{1,3},{3,5},... | collective-permute-start | bytes 983048 | tf_op jit(solution)/shard_map/ppermute | solution.py:284
  3.2 4.0 %collective-permute-start.1 = (bf16[64,2560]{1,0:T(8,128)(2,1)}, bf16[64,2560]{1,0:T(8,128)(2,1)S(1)}, u32[]{:S(2)}, u32[]{:S(2)}) collective-permute-start(bf16[64,2560]{1,0:T(8,128)(2,1)} %refs_3_.1), channel_id=1, source_target_pairs={{0,14},{2,0},{4,2},{6,4},{8,6},{10,8},{12,10},{14,12},{1,15},{3,1}... | collective-permute-start | bytes 983048 | tf_op jit(solution)/shard_map/ppermute | solution.py:284
  7.2 2.2 %proj.1 = bf16[8,64,128]{2,1,0:T(8,128)(2,1)} custom-call(bf16[64,2560]{1,0:T(8,128)(2,1)} %refs_3_.1, f32[64,2560]{1,0:T(8,128)} %bitcast.25), custom_call_target="tpu_custom_call" | custom-call | tf_op jit(solution)/shard_map/proj/pallas_call | solution.py:312
  9.5 5.2 %all-to-all-start = ((bf16[8,64,128]{2,1,0:T(8,128)(2,1)}), bf16[8,64,128]{2,1,0:T(8,128)(2,1)S(1)}, u32[]{:S(2)}, u32[]{:S(2)}) async-start(bf16[8,64,128]{2,1,0:T(8,128)(2,1)} %proj.1), calls=%async_computation | async-start | bytes 262144 | tf_op jit(solution)/shard_map/all_to_all | solution.py:32
  14.6 1.2 %reduce-precision_convert_fusion = (bf16[2560,64]{0,1:T(8,128)(2,1)S(1)}, bf16[2560,64]{0,1:T(8,128)(2,1)S(1)}) fusion(f32[2560,64]{0,1:T(8,128)} %param.7), kind=kLoop, calls=%fused_computation.4 | loop fusion | flops 655360 | bytes 1310720 | tf_op jit(solution)/shard_map/convert_element_type | solution.py:42
  15.8 0.0 copy-start
  15.8 3.7 %convolution_bitcast_fusion.1 = f32[864,128]{1,0:T(8,128)S(1)} fusion(bf16[2560,64]{0,1:T(8,128)(2,1)S(1)} %get-tuple-element.49, bf16[2560,64]{0,1:T(8,128)(2,1)S(1)} %get-tuple-element.48, bf16[1,864,2560]{2,1,0:T(8,128)(2,1)} %param.6), kind=kOutput, calls=%fused_computation.2 | convolution fusion | flops 567541760 | bytes 5521408 | tf_op jit(solution)/shard_map/dot_general | solution.py:26
  19.5 3.1 %all-to-all-done = bf16[8,64,128]{2,1,0:T(8,128)(2,1)S(1)} async-done(((bf16[8,64,128]{2,1,0:T(8,128)(2,1)}), bf16[8,64,128]{2,1,0:T(8,128)(2,1)S(1)}, u32[]{:S(2)}, u32[]{:S(2)}) %all-to-all-start) | async-done | bytes 131104 | tf_op jit(solution)/shard_map/all_to_all | solution.py:32
  22.6 0.0 collective-permute-done.refs_4_
  22.6 0.0 collective-permute-done.1.refs_10_
  22.6 2.6 %collective-permute-start.2 = (bf16[8,64,128]{2,1,0:T(8,128)(2,1)S(1)}, bf16[8,64,128]{2,1,0:T(8,128)(2,1)S(1)}, u32[]{:S(2)}, u32[]{:S(2)}) collective-permute-start(bf16[8,64,128]{2,1,0:T(8,128)(2,1)S(1)} %all-to-all-done), channel_id=1, source_target_pairs={{0,1},{1,0},{2,3},{3,2},{4,5},{5,4},{6,7},{7,6},{8,9},{9,8},{10,11... | collective-permute-start | bytes 393224 | tf_op jit(solution)/shard_map/ppermute | solution.py:274
  25.3 0.3 collective-permute-start.4
  25.5 0.7 collective-permute-done.2
  26.3 0.0 copy-done
  26.3 0.6 fusion
  27.0 0.2 fusion.5
  27.2 0.1 pad_maximum_fusion.1
  27.3 0.8 broadcast_in_dim.4
  28.1 4.0 %all-to-all-start.1 = ((bf16[4,432,128]{2,1,0:T(8,128)(2,1)}), bf16[4,432,128]{2,1,0:T(8,128)(2,1)S(1)}, u32[]{:S(2)}, u32[]{:S(2)}) async-start(bf16[4,432,128]{2,1,0:T(8,128)(2,1)} %broadcast_in_dim.4), calls=%async_computation.1 | async-start | bytes 884736 | tf_op jit(solution)/shard_map/all_to_all | solution.py:32
  32.1 1.7 %collective-permute-start.7 = (bf16[64,2560]{1,0:T(8,128)(2,1)S(1)}, bf16[64,2560]{1,0:T(8,128)(2,1)S(1)}, u32[]{:S(2)}, u32[]{:S(2)}) collective-permute-start(bf16[64,2560]{1,0:T(8,128)(2,1)S(1)} %collective-permute-done.1.refs_10_), channel_id=1, source_target_pairs={{0,14},{2,0},{4,2},{6,4},{8,6},{10,8},{12,10},{14,12},{1,15},{3,1}... | collective-permute-start | bytes 983048 | tf_op jit(solution)/shard_map/ppermute | solution.py:284
  33.8 1.9 %collective-permute-done.4.refs_5_ = bf16[64,2560]{1,0:T(8,128)(2,1)S(1)} collective-permute-done((bf16[64,2560]{1,0:T(8,128)(2,1)S(1)}, bf16[64,2560]{1,0:T(8,128)(2,1)S(1)}, u32[]{:S(2)}, u32[]{:S(2)}) %collective-permute-start.4) | collective-permute-done | bytes 327712 | tf_op jit(solution)/shard_map/ppermute | solution.py:284
  35.7 0.0 collective-permute-start.5
  35.7 4.4 %all-to-all-done.1.parts_ref = bf16[4,432,128]{2,1,0:T(8,128)(2,1)S(1)} async-done(((bf16[4,432,128]{2,1,0:T(8,128)(2,1)}), bf16[4,432,128]{2,1,0:T(8,128)(2,1)S(1)}, u32[]{:S(2)}, u32[]{:S(2)}) %all-to-all-start.1) | async-done | bytes 442400 | tf_op jit(solution)/shard_map/all_to_all | solution.py:32
  40.2 0.8 row_sum.1
  41.0 4.2 %all-to-all-start.2 = ((bf16[4,432,128]{2,1,0:T(8,128)(2,1)}), bf16[4,432,128]{2,1,0:T(8,128)(2,1)S(1)}, u32[]{:S(2)}, u32[]{:S(2)}) async-start(bf16[4,432,128]{2,1,0:T(8,128)(2,1)} %row_sum.1), calls=%async_computation.2 | async-start | bytes 884736 | tf_op jit(solution)/shard_map/all_to_all | solution.py:32
  45.2 0.0 collective-permute-done.7.refs_9_
  45.2 1.7 %collective-permute-start.8 = (bf16[64,2560]{1,0:T(8,128)(2,1)S(1)}, bf16[64,2560]{1,0:T(8,128)(2,1)}, u32[]{:S(2)}, u32[]{:S(2)}) collective-permute-start(bf16[64,2560]{1,0:T(8,128)(2,1)S(1)} %collective-permute-done.7.refs_9_), channel_id=1, source_target_pairs={{0,14},{2,0},{4,2},{6,4},{8,6},{10,8},{12,10},{14,12},{1,15},{3,1}... | collective-permute-start | bytes 983048 | tf_op jit(solution)/shard_map/ppermute | solution.py:284
  46.9 0.0 collective-permute-done.5.refs_6_
  46.9 0.0 collective-permute-start.6
  46.9 4.8 %all-to-all-done.2.parts_ref = bf16[4,432,128]{2,1,0:T(8,128)(2,1)S(1)} async-done(((bf16[4,432,128]{2,1,0:T(8,128)(2,1)}), bf16[4,432,128]{2,1,0:T(8,128)(2,1)S(1)}, u32[]{:S(2)}, u32[]{:S(2)}) %all-to-all-start.2) | async-done | bytes 442400 | tf_op jit(solution)/shard_map/all_to_all | solution.py:32
  51.7 1.7 %left_sum.1 = (bf16[432,128]{1,0:T(8,128)(2,1)S(1)}, bf16[128,432]{1,0:T(8,128)(2,1)S(1)}, f32[32,128]{1,0:T(8,128)S(1)}, bf16[512,128]{1,0:T(8,128)(2,1)S(1)}, bf16[512,128]{1,0:T(8,128)(2,1)S(1)}) custom-call(bf16[4,432,128]{2,1,0:T(8,128)(2,1)S(1)} %all-to-all-done.2.parts_ref, bf16[864,1024]{1,0:T(8,128)(2,1)S(1)} %bitcast.22), custom_call_target="tpu_custom_call" | custom-call | tf_op jit(solution)/shard_map/left_sum/pallas_call | solution.py:345
  53.4 0.0 copy-start.3
  53.5 0.0 copy-start.1
  53.5 3.1 %collective-permute-start.3 = (bf16[512,128]{1,0:T(8,128)(2,1)S(1)}, bf16[512,128]{1,0:T(8,128)(2,1)S(1)}, u32[]{:S(2)}, u32[]{:S(2)}) collective-permute-start(bf16[512,128]{1,0:T(8,128)(2,1)S(1)} %get-tuple-element.29), channel_id=1, source_target_pairs={{0,1},{1,0},{2,3},{3,2},{4,5},{5,4},{6,7},{7,6},{8,9},{9,8},{10,11... | collective-permute-start | bytes 393224 | tf_op jit(solution)/shard_map/ppermute | solution.py:274
  56.6 2.6 %own_product.1.refs_2_ = f32[64,2560]{1,0:T(8,128)S(1)} custom-call(bf16[128,432]{1,0:T(8,128)(2,1)S(1)} %get-tuple-element.30.turned_ref, bf16[864,2560]{1,0:T(8,128)(2,1)} %bitcast.23), custom_call_target="tpu_custom_call" | custom-call | tf_op jit(solution)/shard_map/own_product/pallas_call | solution.py:364
  59.2 0.0 collective-permute-done.8.refs_8_
  59.2 0.0 collective-permute-done.3.refs_1_
  59.2 0.0 copy-done.3
  59.2 0.0 collective-permute-done.6.refs_7_
  59.2 0.0 copy-done.1
  59.3 3.8 %right_product.1 = (bf16[16,16,640]{2,1,0:T(8,128)(2,1)}, bf16[512,2560]{1,0:T(8,128)(2,1)}) custom-call(bf16[512,128]{1,0:T(8,128)(2,1)S(1)} %get-tuple-element.28.refs_0_, bf16[512,128]{1,0:T(8,128)(2,1)S(1)} %collective-permute-done.3.refs_1_, f32[64,2560]{1,0:T(8,128)S(1)} %own_product.1.refs_2_, bf16[64,2560]{1,0:T(8,128)(2,1)S(1)} %copy-done.1, ...), custom_call_target="tpu_custom_call" | custom-call | tf_op jit(solution)/shard_map/right_product/pallas_call | solution.py:374
  63.1 0.1 collective-permute-start.9
  63.2 4.5 %all-to-all-start.3 = ((bf16[16,16,640]{2,1,0:T(8,128)(2,1)}), bf16[16,16,640]{2,1,0:T(8,128)(2,1)S(1)}, u32[]{:S(2)}, u32[]{:S(2)}) async-start(bf16[16,16,640]{2,1,0:T(8,128)(2,1)} %get-tuple-element.33), calls=%async_computation.3 | async-start | bytes 655360 | tf_op jit(solution)/shard_map/all_to_all | solution.py:32
  67.7 0.6 collective-permute-start.10
  68.3 0.9 collective-permute-done.10.other_gram_ref
  69.2 6.9 %all-to-all-done.3.parts_ref = bf16[16,16,640]{2,1,0:T(8,128)(2,1)S(1)} async-done(((bf16[16,16,640]{2,1,0:T(8,128)(2,1)}), bf16[16,16,640]{2,1,0:T(8,128)(2,1)S(1)}, u32[]{:S(2)}, u32[]{:S(2)}) %all-to-all-start.3) | async-done | bytes 327712 | tf_op jit(solution)/shard_map/all_to_all | solution.py:32
  76.0 0.0 collective-permute-done.9.other_ref
  76.0 0.1 replica_sum.1.own_ref
  76.1 1.9 %collective-permute-start.11 = (bf16[16,640]{1,0:T(8,128)(2,1)S(1)}, bf16[16,640]{1,0:T(8,128)(2,1)S(1)}, u32[]{:S(2)}, u32[]{:S(2)}) collective-permute-start(bf16[16,640]{1,0:T(8,128)(2,1)S(1)} %replica_sum.1.own_ref), channel_id=1, source_target_pairs={{0,1},{1,0},{2,3},{3,2},{4,5},{5,4},{6,7},{7,6},{8,9},{9,8},{10,11... | collective-permute-start | bytes 61448 | tf_op jit(solution)/shard_map/ppermute | solution.py:274
  78.0 0.8 collective-permute-done.11.other_ref
  78.8 0.7 core_sum.1
  79.5 3.4 %all-to-all-start.4 = ((bf16[8,16,1024]{2,1,0:T(8,128)(2,1)}), bf16[8,16,1024]{2,1,0:T(8,128)(2,1)S(1)}, u32[]{:S(2)}, u32[]{:S(2)}) async-start(bf16[8,16,1024]{2,1,0:T(8,128)(2,1)} %core_sum.1), calls=%async_computation.4 | async-start | bytes 524288 | tf_op jit(solution)/shard_map/all_to_all | solution.py:32
  83.0 10.5 %merged.1.merged_ref = bf16[864,2560]{1,0:T(8,128)(2,1)} custom-call(bf16[864,1024]{1,0:T(8,128)(2,1)} %bitcast.21, bf16[864,2560]{1,0:T(8,128)(2,1)} %bitcast.24, bf16[512,2560]{1,0:T(8,128)(2,1)} %get-tuple-element.34.half_ref, bf16[512,2560]{1,0:T(8,128)(2,1)} %collective-permute-done.9.other_ref), custom_call_target="tpu_custom_call" | custom-call | tf_op jit(solution)/shard_map/merged/pallas_call | solution.py:389
  93.5 1.8 %all-to-all-done.4.parts_ref = bf16[8,16,1024]{2,1,0:T(8,128)(2,1)S(1)} async-done(((bf16[8,16,1024]{2,1,0:T(8,128)(2,1)}), bf16[8,16,1024]{2,1,0:T(8,128)(2,1)S(1)}, u32[]{:S(2)}, u32[]{:S(2)}) %all-to-all-start.4) | async-done | bytes 262176 | tf_op jit(solution)/shard_map/all_to_all | solution.py:32
  95.2 0.8 chip_sum.1
  96.0 3.5 %all-to-all-start.5 = ((bf16[16,16,640]{2,1,0:T(8,128)(2,1)}), bf16[16,16,640]{2,1,0:T(8,128)(2,1)S(1)}, u32[]{:S(2)}, u32[]{:S(2)}) async-start(bf16[16,16,640]{2,1,0:T(8,128)(2,1)} %get-tuple-element.44), calls=%async_computation.5 | async-start | bytes 655360 | tf_op jit(solution)/shard_map/all_to_all | solution.py:32
  99.6 0.7 collective-permute-start.12
  100.2 0.8 collective-permute-done.12.other_ref
  101.1 3.6 %inverse.1 = (f32[64,64]{1,0:T(8,128)S(1)}, bf16[864,192]{1,0:T(8,128)(2,1)S(1)}) custom-call(f32[16,128]{1,0:T(8,128)S(1)} %get-tuple-element.40.gram_ref, f32[16,128]{1,0:T(8,128)S(1)} %collective-permute-done.12.other_ref, bf16[432,128]{1,0:T(8,128)(2,1)S(1)} %copy-done.4), custom_call_target="tpu_custom_call" | custom-call | tf_op jit(solution)/shard_map/inverse/pallas_call | solution.py:427
  104.7 0.8 copy-done.2
  105.4 0.6 copy-done.5
  106.1 1.5 %all-to-all-done.5 = bf16[16,16,640]{2,1,0:T(8,128)(2,1)S(1)} async-done(((bf16[16,16,640]{2,1,0:T(8,128)(2,1)}), bf16[16,16,640]{2,1,0:T(8,128)(2,1)S(1)}, u32[]{:S(2)}, u32[]{:S(2)}) %all-to-all-start.5) | async-done | bytes 327712 | tf_op jit(solution)/shard_map/all_to_all | solution.py:32
  107.5 0.7 copy-done.6
  108.3 6.5 %residual.1 = (bf16[864,2560]{1,0:T(8,128)(2,1)}, f32[64,2560]{1,0:T(8,128)}) custom-call(f32[64,64]{1,0:T(8,128)} %copy-done.5, bf16[864,192]{1,0:T(8,128)(2,1)} %copy-done.2, bf16[4,4,16,640]{3,2,1,0:T(8,128)(2,1)} %bitcast.26, bf16[864,2560]{1,0:T(8,128)(2,1)} %merged.1.merged_ref), custom_call_target="tpu_custom_call" | custom-call | tf_op jit(solution)/shard_map/residual/pallas_call | solution.py:436
  (9 shorter events, 0.1 us)
Async XLA Ops:
  0.6 22.0 %collective-permute-start = (bf16[64,2560]{1,0:T(8,128)(2,1)}, bf16[64,2560]{1,0:T(8,128)(2,1)S(1)}, u32[]{:S(2)}, u32[]{:S(2)}) collective-permute-start(bf16[64,2560]{1,0:T(8,128)(2,1)} %refs_3_.1), channel_id=1, source_target_pairs={{0,2},{2,4},{4,6},{6,8},{8,10},{10,12},{12,14},{14,0},{1,3},{3,5},... | collective-permute-start | bytes 983048 | tf_op jit(solution)/shard_map/ppermute | solution.py:284
  3.2 19.4 %collective-permute-start.1 = (bf16[64,2560]{1,0:T(8,128)(2,1)}, bf16[64,2560]{1,0:T(8,128)(2,1)S(1)}, u32[]{:S(2)}, u32[]{:S(2)}) collective-permute-start(bf16[64,2560]{1,0:T(8,128)(2,1)} %refs_3_.1), channel_id=1, source_target_pairs={{0,14},{2,0},{4,2},{6,4},{8,6},{10,8},{12,10},{14,12},{1,15},{3,1}... | collective-permute-start | bytes 983048 | tf_op jit(solution)/shard_map/ppermute | solution.py:284
  9.5 13.2 %all-to-all-start = ((bf16[8,64,128]{2,1,0:T(8,128)(2,1)}), bf16[8,64,128]{2,1,0:T(8,128)(2,1)S(1)}, u32[]{:S(2)}, u32[]{:S(2)}) async-start(bf16[8,64,128]{2,1,0:T(8,128)(2,1)} %proj.1), calls=%async_computation | async-start | bytes 262144 | tf_op jit(solution)/shard_map/all_to_all | solution.py:32
  15.8 10.5 %copy-start = (bf16[1024,864]{0,1:T(8,128)(2,1)S(1)}, bf16[1024,864]{0,1:T(8,128)(2,1)}, u32[]{:S(2)}) copy-start(bf16[1024,864]{0,1:T(8,128)(2,1)} %param.5) | copy-start | bytes 5308420
  22.6 3.6 %collective-permute-start.2 = (bf16[8,64,128]{2,1,0:T(8,128)(2,1)S(1)}, bf16[8,64,128]{2,1,0:T(8,128)(2,1)S(1)}, u32[]{:S(2)}, u32[]{:S(2)}) collective-permute-start(bf16[8,64,128]{2,1,0:T(8,128)(2,1)S(1)} %all-to-all-done), channel_id=1, source_target_pairs={{0,1},{1,0},{2,3},{3,2},{4,5},{5,4},{6,7},{7,6},{8,9},{9,8},{10,11... | collective-permute-start | bytes 393224 | tf_op jit(solution)/shard_map/ppermute | solution.py:274
  25.3 10.5 %collective-permute-start.4 = (bf16[64,2560]{1,0:T(8,128)(2,1)S(1)}, bf16[64,2560]{1,0:T(8,128)(2,1)S(1)}, u32[]{:S(2)}, u32[]{:S(2)}) collective-permute-start(bf16[64,2560]{1,0:T(8,128)(2,1)S(1)} %collective-permute-done.refs_4_), channel_id=1, source_target_pairs={{0,2},{2,4},{4,6},{6,8},{8,10},{10,12},{12,14},{14,0},{1,3},{3,5},... | collective-permute-start | bytes 983048 | tf_op jit(solution)/shard_map/ppermute | solution.py:284
  28.1 12.1 %all-to-all-start.1 = ((bf16[4,432,128]{2,1,0:T(8,128)(2,1)}), bf16[4,432,128]{2,1,0:T(8,128)(2,1)S(1)}, u32[]{:S(2)}, u32[]{:S(2)}) async-start(bf16[4,432,128]{2,1,0:T(8,128)(2,1)} %broadcast_in_dim.4), calls=%async_computation.1 | async-start | bytes 884736 | tf_op jit(solution)/shard_map/all_to_all | solution.py:32
  32.1 13.1 %collective-permute-start.7 = (bf16[64,2560]{1,0:T(8,128)(2,1)S(1)}, bf16[64,2560]{1,0:T(8,128)(2,1)S(1)}, u32[]{:S(2)}, u32[]{:S(2)}) collective-permute-start(bf16[64,2560]{1,0:T(8,128)(2,1)S(1)} %collective-permute-done.1.refs_10_), channel_id=1, source_target_pairs={{0,14},{2,0},{4,2},{6,4},{8,6},{10,8},{12,10},{14,12},{1,15},{3,1}... | collective-permute-start | bytes 983048 | tf_op jit(solution)/shard_map/ppermute | solution.py:284
  35.7 11.2 %collective-permute-start.5 = (bf16[64,2560]{1,0:T(8,128)(2,1)S(1)}, bf16[64,2560]{1,0:T(8,128)(2,1)}, u32[]{:S(2)}, u32[]{:S(2)}) collective-permute-start(bf16[64,2560]{1,0:T(8,128)(2,1)S(1)} %collective-permute-done.4.refs_5_), channel_id=1, source_target_pairs={{0,2},{2,4},{4,6},{6,8},{8,10},{10,12},{12,14},{14,0},{1,3},{3,5},... | collective-permute-start | bytes 983048 | tf_op jit(solution)/shard_map/ppermute | solution.py:284
  41.0 10.7 %all-to-all-start.2 = ((bf16[4,432,128]{2,1,0:T(8,128)(2,1)}), bf16[4,432,128]{2,1,0:T(8,128)(2,1)S(1)}, u32[]{:S(2)}, u32[]{:S(2)}) async-start(bf16[4,432,128]{2,1,0:T(8,128)(2,1)} %row_sum.1), calls=%async_computation.2 | async-start | bytes 884736 | tf_op jit(solution)/shard_map/all_to_all | solution.py:32
  45.2 14.0 %collective-permute-start.8 = (bf16[64,2560]{1,0:T(8,128)(2,1)S(1)}, bf16[64,2560]{1,0:T(8,128)(2,1)}, u32[]{:S(2)}, u32[]{:S(2)}) collective-permute-start(bf16[64,2560]{1,0:T(8,128)(2,1)S(1)} %collective-permute-done.7.refs_9_), channel_id=1, source_target_pairs={{0,14},{2,0},{4,2},{6,4},{8,6},{10,8},{12,10},{14,12},{1,15},{3,1}... | collective-permute-start | bytes 983048 | tf_op jit(solution)/shard_map/ppermute | solution.py:284
  46.9 12.3 %collective-permute-start.6 = (bf16[64,2560]{1,0:T(8,128)(2,1)}, bf16[64,2560]{1,0:T(8,128)(2,1)}, u32[]{:S(2)}, u32[]{:S(2)}) collective-permute-start(bf16[64,2560]{1,0:T(8,128)(2,1)} %collective-permute-done.5.refs_6_), channel_id=1, source_target_pairs={{0,2},{2,4},{4,6},{6,8},{8,10},{10,12},{12,14},{14,0},{1,3},{3,5},... | collective-permute-start | bytes 983048 | tf_op jit(solution)/shard_map/ppermute | solution.py:284
  53.4 5.8 %copy-start.3 = (bf16[432,128]{1,0:T(8,128)(2,1)}, bf16[432,128]{1,0:T(8,128)(2,1)S(1)}, u32[]{:S(2)}) copy-start(bf16[432,128]{1,0:T(8,128)(2,1)S(1)} %get-tuple-element.41.left_ref) | copy-start | bytes 331780
  53.5 5.8 %copy-start.1 = (bf16[64,2560]{1,0:T(8,128)(2,1)S(1)}, bf16[64,2560]{1,0:T(8,128)(2,1)}, u32[]{:S(2)}) copy-start(bf16[64,2560]{1,0:T(8,128)(2,1)} %refs_3_.1) | copy-start | bytes 983044
  53.5 5.7 %collective-permute-start.3 = (bf16[512,128]{1,0:T(8,128)(2,1)S(1)}, bf16[512,128]{1,0:T(8,128)(2,1)S(1)}, u32[]{:S(2)}, u32[]{:S(2)}) collective-permute-start(bf16[512,128]{1,0:T(8,128)(2,1)S(1)} %get-tuple-element.29), channel_id=1, source_target_pairs={{0,1},{1,0},{2,3},{3,2},{4,5},{5,4},{6,7},{7,6},{8,9},{9,8},{10,11... | collective-permute-start | bytes 393224 | tf_op jit(solution)/shard_map/ppermute | solution.py:274
  63.1 13.0 %collective-permute-start.9 = (bf16[512,2560]{1,0:T(8,128)(2,1)}, bf16[512,2560]{1,0:T(8,128)(2,1)}, u32[]{:S(2)}, u32[]{:S(2)}) collective-permute-start(bf16[512,2560]{1,0:T(8,128)(2,1)} %get-tuple-element.34.half_ref), channel_id=1, source_target_pairs={{0,1},{1,0},{2,3},{3,2},{4,5},{5,4},{6,7},{7,6},{8,9},{9,8},{10,11... | collective-permute-start | bytes 7864328 | tf_op jit(solution)/shard_map/ppermute | solution.py:274
  63.2 12.8 %all-to-all-start.3 = ((bf16[16,16,640]{2,1,0:T(8,128)(2,1)}), bf16[16,16,640]{2,1,0:T(8,128)(2,1)S(1)}, u32[]{:S(2)}, u32[]{:S(2)}) async-start(bf16[16,16,640]{2,1,0:T(8,128)(2,1)} %get-tuple-element.33), calls=%async_computation.3 | async-start | bytes 655360 | tf_op jit(solution)/shard_map/all_to_all | solution.py:32
  67.7 1.5 %collective-permute-start.10 = (f32[32,128]{1,0:T(8,128)S(1)}, f32[32,128]{1,0:T(8,128)S(1)}, u32[]{:S(2)}, u32[]{:S(2)}) collective-permute-start(f32[32,128]{1,0:T(8,128)S(1)} %get-tuple-element.35.gram_ref), channel_id=1, source_target_pairs={{0,1},{1,0},{2,3},{3,2},{4,5},{5,4},{6,7},{7,6},{8,9},{9,8},{10,11... | collective-permute-start | bytes 49160 | tf_op jit(solution)/shard_map/ppermute | solution.py:274
  76.1 2.7 %collective-permute-start.11 = (bf16[16,640]{1,0:T(8,128)(2,1)S(1)}, bf16[16,640]{1,0:T(8,128)(2,1)S(1)}, u32[]{:S(2)}, u32[]{:S(2)}) collective-permute-start(bf16[16,640]{1,0:T(8,128)(2,1)S(1)} %replica_sum.1.own_ref), channel_id=1, source_target_pairs={{0,1},{1,0},{2,3},{3,2},{4,5},{5,4},{6,7},{7,6},{8,9},{9,8},{10,11... | collective-permute-start | bytes 61448 | tf_op jit(solution)/shard_map/ppermute | solution.py:274
  79.5 15.7 %all-to-all-start.4 = ((bf16[8,16,1024]{2,1,0:T(8,128)(2,1)}), bf16[8,16,1024]{2,1,0:T(8,128)(2,1)S(1)}, u32[]{:S(2)}, u32[]{:S(2)}) async-start(bf16[8,16,1024]{2,1,0:T(8,128)(2,1)} %core_sum.1), calls=%async_computation.4 | async-start | bytes 524288 | tf_op jit(solution)/shard_map/all_to_all | solution.py:32
  83.0 18.1 %copy-start.4 = (bf16[432,128]{1,0:T(8,128)(2,1)S(1)}, bf16[432,128]{1,0:T(8,128)(2,1)}, u32[]{:S(2)}) copy-start(bf16[432,128]{1,0:T(8,128)(2,1)} %copy-done.3) | copy-start | bytes 331780
  96.0 11.5 %all-to-all-start.5 = ((bf16[16,16,640]{2,1,0:T(8,128)(2,1)}), bf16[16,16,640]{2,1,0:T(8,128)(2,1)S(1)}, u32[]{:S(2)}, u32[]{:S(2)}) async-start(bf16[16,16,640]{2,1,0:T(8,128)(2,1)} %get-tuple-element.44), calls=%async_computation.5 | async-start | bytes 655360 | tf_op jit(solution)/shard_map/all_to_all | solution.py:32
  99.6 1.5 %collective-permute-start.12 = (f32[16,128]{1,0:T(8,128)S(1)}, f32[16,128]{1,0:T(8,128)S(1)}, u32[]{:S(2)}, u32[]{:S(2)}) collective-permute-start(f32[16,128]{1,0:T(8,128)S(1)} %get-tuple-element.40.gram_ref), channel_id=1, source_target_pairs={{0,1},{1,0},{2,3},{3,2},{4,5},{5,4},{6,7},{7,6},{8,9},{9,8},{10,11... | collective-permute-start | bytes 24584 | tf_op jit(solution)/shard_map/ppermute | solution.py:274
  104.7 0.8 copy-start.2
  105.4 0.6 copy-start.5
  107.5 0.7 copy-start.6

commit v6 on v5

--- a/solution.py
+++ b/solution.py
@@ -14,7 +14,6 @@
 
 bf16 = jnp.bfloat16
 f32 = jnp.float32
-highest = lax.Precision.HIGHEST
 VMEM = pltpu.VMEM
 whole = pl.BlockSpec(memory_space=pltpu.VMEM)
 anywhere = pl.BlockSpec(memory_space=pl.ANY)
@@ -30,11 +29,6 @@
 
 def sent(array, axis):
     return lax.all_to_all(array, axis, 0, 0, tiled=True)
-
-
-def sent_to_all(array, axis):
-    devices = lax.axis_size(axis)
-    return sent(jnp.broadcast_to(array[None], (devices, *array.shape)), axis)
 
 
 def halves(array):
@@ -66,6 +60,20 @@
     proj = jnp.concatenate(split(product(grad, high, 1, 1) + product(grad, low, 1, 1)), axis=1)
     for i in range(out_ref.shape[0]):
         out_ref[i] = proj
+
+
+def local_left_kernel(own_ref, other_ref, carried_ref, act_ref, out_ref):
+    first = lax.axis_index("mp_1") == 0
+    parts = []
+    for z in range(own_ref.shape[0]):
+        own, other = own_ref[z], other_ref[z]
+        parts += [jnp.where(first, own, other), jnp.where(first, other, own)]
+    left = carried_ref[...] + product(act_ref[...], jnp.concatenate(parts, axis=0), 1, 0)
+    rows, lanes = out_ref.shape[1:]
+    left = left[:, : lanes // 2] + left[:, lanes // 2 :]
+    left = jnp.concatenate([left[:rows], left[rows:]], axis=1).astype(bf16)
+    for i in range(out_ref.shape[0]):
+        out_ref[i] = left
 
 
 def chunk_copies(chunk_refs, half_ref, sems):
@@ -237,18 +245,18 @@
     return work[:, rank:] * lax.rsqrt(pivots)
 
 
-def inverse_kernel(gram_ref, other_ref, left_ref, out_ref, ortho_ref):
+def inverse_kernel(gram_ref, other_ref, left_ref, terms_ref, ortho_ref):
     own, other = gram_ref[...], other_ref[...]
     first = lax.axis_index("mp_1") == 0
     upper, lower = jnp.where(first, own, other), jnp.where(first, other, own)
-    rank = out_ref.shape[0]
+    rank = terms_ref.shape[0]
     gram = jnp.concatenate([upper[:, :rank], lower[:, :rank], upper[:, rank:], lower[:, rank:]], axis=0)
     inverse = inverse_of(gram)
-    out_ref[...] = inverse
     rows = left_ref.shape[0]
     left = left_ref[...]
     high, low = split(inverse)
     least = (inverse - high.astype(f32) - low.astype(f32)).astype(bf16)
+    terms_ref[...] = jnp.concatenate([high, low, least], axis=1)
     for i in range(2):
         part = left[:, i * rank : (i + 1) * rank]
         ortho = product(part, high, 1, 1) + product(part, low, 1, 1) + product(part, least, 1, 1)
@@ -258,12 +266,10 @@
         )
 
 
-def residual_kernel(replicas, inverse_ref, ortho_ref, right_ref, merged_ref, out_ref, next_ref):
+def residual_kernel(replicas, terms_ref, ortho_ref, right_ref, merged_ref, out_ref, next_ref):
     step = pl.program_id(0)
-    right = jnp.concatenate([right_ref[a, step] for a in range(4)], axis=0).astype(f32)
-    turned = jnp.dot(
-        inverse_ref[...], right, precision=highest, preferred_element_type=f32
-    ) * (1.0 / replicas)
+    right = jnp.concatenate([right_ref[a, step] for a in range(4)] * 3, axis=0)
+    turned = product(terms_ref[...], right, 1, 0) * (1.0 / replicas)
     next_ref[...] = turned
     high, low = split(turned)
     low_rank = product(ortho_ref[...], jnp.concatenate([high, high, low], axis=0), 1, 0)
@@ -317,24 +323,27 @@
         out_specs=whole,
         name="proj",
     )(grad_out, prior_right.T)
+    proj, passed_on = lax.optimization_barrier((proj, grad_out))
     left = product(own, jnp.concatenate(halves(prior_right), axis=1), 1, 0)
     proj, left = lax.optimization_barrier((sent(proj, "mp_0"), left))
-    ring = Ring(grad_out)
+    ring = Ring(passed_on)
     proj = ring.step(proj)
     other = swapped(proj)
-    first = lax.axis_index("mp_1") == 0
-    proj = jnp.stack([jnp.where(first, proj, other), jnp.where(first, other, proj)], axis=1)
-    proj = proj.reshape(-1, 2 * rank)
-    left = left + product(hidden_act, proj, 0, 0)
-    left = left[:, :rank] + left[:, rank:]
-    left = jnp.concatenate([left[:rows], left[rows:]], axis=1).astype(bf16)
+    left = call(
+        local_left_kernel,
+        of((lax.axis_size("dp_0"), rows, 2 * rank), bf16),
+        limit=24,
+        in_specs=[whole] * 4,
+        out_specs=whole,
+        name="local_left",
+    )(proj, other, left, act)
     left = call(
         row_sum_kernel,
-        of((lax.axis_size("dp_1"), *left.shape), bf16),
+        of((lax.axis_size("dp_1"), rows, 2 * rank), bf16),
         in_specs=[whole],
         out_specs=whole,
         name="row_sum",
-    )(sent_to_all(left, "dp_0"))
+    )(sent(left, "dp_0"))
     parts = sent(left, "dp_1")
     for _ in range(3):
         ring.step()
@@ -426,7 +435,7 @@
     right = sent(right, DP)
     inverse, ortho = call(
         inverse_kernel,
-        (of((rank, rank), f32), of((2 * rows, 3 * rank), bf16)),
+        (of((rank, 3 * rank), bf16), of((2 * rows, 3 * rank), bf16)),
         in_specs=[whole] * 3,
         out_specs=(whole, whole),
         name="inverse",
@@ -436,7 +445,7 @@
     residual_out, next_right = call(
         functools.partial(residual_kernel, replicas),
         (of(own.shape, bf16), of((rank, features), f32)),
-        limit=58,
+        limit=52,
         grid=(4,),
         in_specs=[
             whole,

time: 116 us -> 114 us (0.983)
  local copies, waits for them, and re-layouts: 3 us -> 0.02 us
  waiting for transfers between devices: 27.6 us -> 29.9 us
  starting transfers between devices: 44.1 us -> 42.7 us
  Pallas kernels: 33.4 us -> 34.7 us
    all_to_all x6, waiting for transfers between devices: 22.5 us -> 26.4 us  [sent(): return lax.all_to_all(array, axis, 0, 0, tiled=True)]
    unnamed x14 -> x8, local copies, waits for them, and re-layouts: 2.15 us -> 0.02 us
    ppermute x7, waiting for transfers between devices: 1.92 us -> 0.02 us  [passed(): lax.ppermute(array, 'mp_0', [(i, (i + hop) % self.size) for i in range(se...]
    pallas_call x2 -> x3, Pallas kernels: 4.41 us -> 5.94 us  [the longest x1 3.58 us: per_device(): call(inverse_kernel, (of((rank, 3 * rank), bf16), of((2 * rows, 3 * rank)...]
    all_to_all x6, starting transfers between devices: 24.8 us -> 23.4 us  [sent(): return lax.all_to_all(array, axis, 0, 0, tiled=True)]
    dot_general x2 -> x1, matrix products: 4.3 us -> 3.56 us  [product(): lax.dot_general(left, right, (((left_dim,), (right_dim,)), ((), ())), pre...]
  transfers between devices with their start and end apart: 19 -> 19, of which waited for: 11 -> 10; matrix products, arithmetic and copies ran while one was open for 6% -> 4% of each run, Pallas kernels for 19% -> 18%
where the time goes in v6:
time: 114 us; the launch traced here: 113 us
  starting transfers between devices  42.7 us (37%)
  Pallas kernels  34.7 us (30%)
  waiting for transfers between devices  29.9 us (26%)
  matrix products  3.56 us (3%)
  other arithmetic  1.16 us (1%)
    all_to_all x6, waiting for transfers between devices, sent(): return lax.all_to_all(array, axis, 0, 0, tiled=True)  26.4 us
    all_to_all x6, starting transfers between devices, sent(): return lax.all_to_all(array, axis, 0, 0, tiled=True)  23.4 us
    pallas_call x1, Pallas kernels, per_device(): call(merged_kernel, of(own.shape, bf16), limit=58, grid=(4,), in_specs=[p...  10.5 us
    ppermute x7, starting transfers between devices, passed(): lax.ppermute(array, 'mp_0', [(i, (i + hop) % self.size) for i in range(se...  9.76 us
    ppermute x6, starting transfers between devices, swapped(): return lax.ppermute(array, 'mp_1', [(0, 1), (1, 0)])  9.53 us
    pallas_call x1, Pallas kernels, per_device(): call(functools.partial(residual_kernel, replicas), (of(own.shape, bf16),...  6.22 us
    pallas_call x1, Pallas kernels, per_device(): call(functools.partial(right_kernel, len(chunks)), (of((16, rank // 4, wi...  3.92 us
    pallas_call x1, Pallas kernels, per_device(): call(inverse_kernel, (of((rank, 3 * rank), bf16), of((2 * rows, 3 * rank)...  3.58 us
  transfers between devices with their start and end apart: 19, of which 10 were waited for; matrix products, arithmetic and copies ran while one was open for 4% of the time, Pallas kernels for 18%

profile of v6, /device:TPU:1, one launch (start us, length us, event | category | flops | bytes accessed | tf_op | source)
XLA Modules:
  0.0 112.9 jit_solution(14592371674621234876)
XLA Ops:
  0.6 2.3 %proj.1 = bf16[8,64,128]{2,1,0:T(8,128)(2,1)} custom-call(bf16[64,2560]{1,0:T(8,128)(2,1)} %refs_3_, f32[64,2560]{1,0:T(8,128)} %bitcast.16), custom_call_target="tpu_custom_call" | custom-call | tf_op jit(solution)/shard_map/proj/pallas_call | solution.py:318
  2.9 0.0 copy-start
  2.9 6.4 %collective-permute-start.1 = (bf16[64,2560]{1,0:T(8,128)(2,1)}, bf16[64,2560]{1,0:T(8,128)(2,1)S(1)}, u32[]{:S(2)}, u32[]{:S(2)}) collective-permute-start(bf16[64,2560]{1,0:T(8,128)(2,1)} %refs_3_), channel_id=1, source_target_pairs={{0,14},{2,0},{4,2},{6,4},{8,6},{10,8},{12,10},{14,12},{1,15},{3,1}... | collective-permute-start | bytes 983048 | tf_op jit(solution)/shard_map/ppermute | solution.py:290
  9.3 0.0 collective-permute-start
  9.3 4.1 %all-to-all-start = ((bf16[8,64,128]{2,1,0:T(8,128)(2,1)}), bf16[8,64,128]{2,1,0:T(8,128)(2,1)S(1)}, u32[]{:S(2)}, u32[]{:S(2)}) async-start(bf16[8,64,128]{2,1,0:T(8,128)(2,1)} %proj.1), calls=%async_computation | async-start | bytes 262144 | tf_op jit(solution)/shard_map/all_to_all | solution.py:31
  13.4 1.2 %reduce-precision_convert_fusion = (bf16[2560,64]{0,1:T(8,128)(2,1)S(1)}, bf16[2560,64]{0,1:T(8,128)(2,1)S(1)}) fusion(f32[2560,64]{0,1:T(8,128)} %param.7), kind=kLoop, calls=%fused_computation.2 | loop fusion | flops 655360 | bytes 1310720 | tf_op jit(solution)/shard_map/convert_element_type | solution.py:36
  14.5 3.6 %convolution_bitcast_fusion.carried_ref = f32[864,128]{1,0:T(8,128)S(1)} fusion(bf16[2560,64]{0,1:T(8,128)(2,1)S(1)} %get-tuple-element.53, bf16[2560,64]{0,1:T(8,128)(2,1)S(1)} %get-tuple-element.52, bf16[1,864,2560]{2,1,0:T(8,128)(2,1)} %param.6), kind=kOutput, calls=%fused_computation | convolution fusion | flops 567541760 | bytes 5521408 | tf_op jit(solution)/shard_map/dot_general | solution.py:25
  18.1 3.6 %all-to-all-done.own_ref = bf16[8,64,128]{2,1,0:T(8,128)(2,1)S(1)} async-done(((bf16[8,64,128]{2,1,0:T(8,128)(2,1)}), bf16[8,64,128]{2,1,0:T(8,128)(2,1)S(1)}, u32[]{:S(2)}, u32[]{:S(2)}) %all-to-all-start) | async-done | bytes 131104 | tf_op jit(solution)/shard_map/all_to_all | solution.py:31
  21.7 0.0 collective-permute-done.1.refs_10_
  21.7 0.0 collective-permute-done.refs_4_
  21.7 0.0 collective-permute-start.4
  21.7 3.2 %collective-permute-start.2 = (bf16[8,64,128]{2,1,0:T(8,128)(2,1)S(1)}, bf16[8,64,128]{2,1,0:T(8,128)(2,1)S(1)}, u32[]{:S(2)}, u32[]{:S(2)}) collective-permute-start(bf16[8,64,128]{2,1,0:T(8,128)(2,1)S(1)} %all-to-all-done.own_ref), channel_id=1, source_target_pairs={{0,1},{1,0},{2,3},{3,2},{4,5},{5,4},{6,7},{7,6},{8,9},{9,8},{10,11... | collective-permute-start | bytes 393224 | tf_op jit(solution)/shard_map/ppermute | solution.py:280
  24.9 1.0 collective-permute-done.2.other_ref
  25.9 0.0 copy-done
  25.9 1.5 %local_left.1 = bf16[4,432,128]{2,1,0:T(8,128)(2,1)} custom-call(bf16[8,64,128]{2,1,0:T(8,128)(2,1)S(1)} %all-to-all-done.own_ref, bf16[8,64,128]{2,1,0:T(8,128)(2,1)S(1)} %collective-permute-done.2.other_ref, f32[864,128]{1,0:T(8,128)S(1)} %convolution_bitcast_fusion.carried_ref, bf16[864,1024]{1,0:T(8,128)(2,1)S(1)} %bitcast.11), custom_call_target="tpu_custom_call" | custom-call | tf_op jit(solution)/shard_map/local_left/pallas_call | solution.py:332
  27.5 4.0 %all-to-all-start.1 = ((bf16[4,432,128]{2,1,0:T(8,128)(2,1)}), bf16[4,432,128]{2,1,0:T(8,128)(2,1)S(1)}, u32[]{:S(2)}, u32[]{:S(2)}) async-start(bf16[4,432,128]{2,1,0:T(8,128)(2,1)} %local_left.1), calls=%async_computation.1 | async-start | bytes 884736 | tf_op jit(solution)/shard_map/all_to_all | solution.py:31
  31.5 0.0 copy-start.1
  31.5 1.7 %collective-permute-start.7 = (bf16[64,2560]{1,0:T(8,128)(2,1)S(1)}, bf16[64,2560]{1,0:T(8,128)(2,1)}, u32[]{:S(2)}, u32[]{:S(2)}) collective-permute-start(bf16[64,2560]{1,0:T(8,128)(2,1)S(1)} %collective-permute-done.1.refs_10_), channel_id=1, source_target_pairs={{0,14},{2,0},{4,2},{6,4},{8,6},{10,8},{12,10},{14,12},{1,15},{3,1}... | collective-permute-start | bytes 983048 | tf_op jit(solution)/shard_map/ppermute | solution.py:290
  33.2 0.0 collective-permute-done.4.refs_5_
  33.2 0.0 collective-permute-start.5
  33.2 6.4 %all-to-all-done.1.parts_ref = bf16[4,432,128]{2,1,0:T(8,128)(2,1)S(1)} async-done(((bf16[4,432,128]{2,1,0:T(8,128)(2,1)}), bf16[4,432,128]{2,1,0:T(8,128)(2,1)S(1)}, u32[]{:S(2)}, u32[]{:S(2)}) %all-to-all-start.1) | async-done | bytes 442400 | tf_op jit(solution)/shard_map/all_to_all | solution.py:31
  39.5 0.8 row_sum.1
  40.3 4.2 %all-to-all-start.2 = ((bf16[4,432,128]{2,1,0:T(8,128)(2,1)}), bf16[4,432,128]{2,1,0:T(8,128)(2,1)S(1)}, u32[]{:S(2)}, u32[]{:S(2)}) async-start(bf16[4,432,128]{2,1,0:T(8,128)(2,1)} %row_sum.1), calls=%async_computation.2 | async-start | bytes 884736 | tf_op jit(solution)/shard_map/all_to_all | solution.py:31
  44.5 0.0 collective-permute-done.7.refs_9_
  44.5 1.7 %collective-permute-start.8 = (bf16[64,2560]{1,0:T(8,128)(2,1)}, bf16[64,2560]{1,0:T(8,128)(2,1)}, u32[]{:S(2)}, u32[]{:S(2)}) collective-permute-start(bf16[64,2560]{1,0:T(8,128)(2,1)} %collective-permute-done.7.refs_9_), channel_id=1, source_target_pairs={{0,14},{2,0},{4,2},{6,4},{8,6},{10,8},{12,10},{14,12},{1,15},{3,1}... | collective-permute-start | bytes 983048 | tf_op jit(solution)/shard_map/ppermute | solution.py:290
  46.2 0.0 collective-permute-done.5.refs_6_
  46.2 0.0 collective-permute-start.6
  46.2 4.9 %all-to-all-done.2.parts_ref = bf16[4,432,128]{2,1,0:T(8,128)(2,1)S(1)} async-done(((bf16[4,432,128]{2,1,0:T(8,128)(2,1)}), bf16[4,432,128]{2,1,0:T(8,128)(2,1)S(1)}, u32[]{:S(2)}, u32[]{:S(2)}) %all-to-all-start.2) | async-done | bytes 442400 | tf_op jit(solution)/shard_map/all_to_all | solution.py:31
  51.1 1.7 %left_sum.1 = (bf16[432,128]{1,0:T(8,128)(2,1)S(1)}, bf16[128,432]{1,0:T(8,128)(2,1)S(1)}, f32[32,128]{1,0:T(8,128)S(1)}, bf16[512,128]{1,0:T(8,128)(2,1)S(1)}, bf16[512,128]{1,0:T(8,128)(2,1)S(1)}) custom-call(bf16[4,432,128]{2,1,0:T(8,128)(2,1)S(1)} %all-to-all-done.2.parts_ref, bf16[864,1024]{1,0:T(8,128)(2,1)S(1)} %bitcast.12), custom_call_target="tpu_custom_call" | custom-call | tf_op jit(solution)/shard_map/left_sum/pallas_call | solution.py:354
  52.8 0.0 copy-start.2
  52.8 3.1 %collective-permute-start.3 = (bf16[512,128]{1,0:T(8,128)(2,1)S(1)}, bf16[512,128]{1,0:T(8,128)(2,1)S(1)}, u32[]{:S(2)}, u32[]{:S(2)}) collective-permute-start(bf16[512,128]{1,0:T(8,128)(2,1)S(1)} %get-tuple-element.33), channel_id=1, source_target_pairs={{0,1},{1,0},{2,3},{3,2},{4,5},{5,4},{6,7},{7,6},{8,9},{9,8},{10,11... | collective-permute-start | bytes 393224 | tf_op jit(solution)/shard_map/ppermute | solution.py:280
  55.9 2.6 %own_product.1.refs_2_ = f32[64,2560]{1,0:T(8,128)S(1)} custom-call(bf16[128,432]{1,0:T(8,128)(2,1)S(1)} %get-tuple-element.34.turned_ref, bf16[864,2560]{1,0:T(8,128)(2,1)} %bitcast.14), custom_call_target="tpu_custom_call" | custom-call | tf_op jit(solution)/shard_map/own_product/pallas_call | solution.py:373
  58.6 0.0 collective-permute-done.8.refs_8_
  58.6 0.0 collective-permute-done.3.refs_1_
  58.6 0.0 copy-done.2
  58.6 0.0 collective-permute-done.6.refs_7_
  58.6 0.0 copy-done.1
  58.6 3.9 %right_product.1 = (bf16[16,16,640]{2,1,0:T(8,128)(2,1)}, bf16[512,2560]{1,0:T(8,128)(2,1)}) custom-call(bf16[512,128]{1,0:T(8,128)(2,1)S(1)} %get-tuple-element.32.refs_0_, bf16[512,128]{1,0:T(8,128)(2,1)S(1)} %collective-permute-done.3.refs_1_, f32[64,2560]{1,0:T(8,128)S(1)} %own_product.1.refs_2_, bf16[64,2560]{1,0:T(8,128)(2,1)S(1)} %copy-done.1, ...), custom_call_target="tpu_custom_call" | custom-call | tf_op jit(solution)/shard_map/right_product/pallas_call | solution.py:383
  62.5 0.1 collective-permute-start.9
  62.6 4.2 %all-to-all-start.3 = ((bf16[16,16,640]{2,1,0:T(8,128)(2,1)}), bf16[16,16,640]{2,1,0:T(8,128)(2,1)S(1)}, u32[]{:S(2)}, u32[]{:S(2)}) async-start(bf16[16,16,640]{2,1,0:T(8,128)(2,1)} %get-tuple-element.37), calls=%async_computation.3 | async-start | bytes 655360 | tf_op jit(solution)/shard_map/all_to_all | solution.py:31
  66.8 0.6 collective-permute-start.10
  67.4 0.9 collective-permute-done.10.other_gram_ref
  68.3 6.9 %all-to-all-done.3.parts_ref = bf16[16,16,640]{2,1,0:T(8,128)(2,1)S(1)} async-done(((bf16[16,16,640]{2,1,0:T(8,128)(2,1)}), bf16[16,16,640]{2,1,0:T(8,128)(2,1)S(1)}, u32[]{:S(2)}, u32[]{:S(2)}) %all-to-all-start.3) | async-done | bytes 327712 | tf_op jit(solution)/shard_map/all_to_all | solution.py:31
  75.1 0.0 collective-permute-done.9.other_ref
  75.1 0.1 replica_sum.1.own_ref
  75.2 1.9 %collective-permute-start.11 = (bf16[16,640]{1,0:T(8,128)(2,1)S(1)}, bf16[16,640]{1,0:T(8,128)(2,1)S(1)}, u32[]{:S(2)}, u32[]{:S(2)}) collective-permute-start(bf16[16,640]{1,0:T(8,128)(2,1)S(1)} %replica_sum.1.own_ref), channel_id=1, source_target_pairs={{0,1},{1,0},{2,3},{3,2},{4,5},{5,4},{6,7},{7,6},{8,9},{9,8},{10,11... | collective-permute-start | bytes 61448 | tf_op jit(solution)/shard_map/ppermute | solution.py:280
  77.1 0.8 collective-permute-done.11.other_ref
  77.9 0.7 core_sum.1
  78.6 3.4 %all-to-all-start.4 = ((bf16[8,16,1024]{2,1,0:T(8,128)(2,1)}), bf16[8,16,1024]{2,1,0:T(8,128)(2,1)S(1)}, u32[]{:S(2)}, u32[]{:S(2)}) async-start(bf16[8,16,1024]{2,1,0:T(8,128)(2,1)} %core_sum.1), calls=%async_computation.4 | async-start | bytes 524288 | tf_op jit(solution)/shard_map/all_to_all | solution.py:31
  82.1 0.0 copy-start.3
  82.1 10.5 %merged.1.merged_ref = bf16[864,2560]{1,0:T(8,128)(2,1)} custom-call(bf16[864,1024]{1,0:T(8,128)(2,1)} %bitcast.10, bf16[864,2560]{1,0:T(8,128)(2,1)} %bitcast.15, bf16[512,2560]{1,0:T(8,128)(2,1)} %get-tuple-element.38.half_ref, bf16[512,2560]{1,0:T(8,128)(2,1)} %collective-permute-done.9.other_ref), custom_call_target="tpu_custom_call" | custom-call | tf_op jit(solution)/shard_map/merged/pallas_call | solution.py:398
  92.6 1.8 %all-to-all-done.4.parts_ref = bf16[8,16,1024]{2,1,0:T(8,128)(2,1)S(1)} async-done(((bf16[8,16,1024]{2,1,0:T(8,128)(2,1)}), bf16[8,16,1024]{2,1,0:T(8,128)(2,1)S(1)}, u32[]{:S(2)}, u32[]{:S(2)}) %all-to-all-start.4) | async-done | bytes 262176 | tf_op jit(solution)/shard_map/all_to_all | solution.py:31
  94.3 0.8 chip_sum.1
  95.1 3.5 %all-to-all-start.5 = ((bf16[16,16,640]{2,1,0:T(8,128)(2,1)}), bf16[16,16,640]{2,1,0:T(8,128)(2,1)S(1)}, u32[]{:S(2)}, u32[]{:S(2)}) async-start(bf16[16,16,640]{2,1,0:T(8,128)(2,1)} %get-tuple-element.48), calls=%async_computation.5 | async-start | bytes 655360 | tf_op jit(solution)/shard_map/all_to_all | solution.py:31
  98.7 0.7 collective-permute-start.12
  99.3 0.8 collective-permute-done.12.other_ref
  100.2 0.0 copy-done.3
  100.2 3.6 %inverse.1 = (bf16[64,192]{1,0:T(8,128)(2,1)S(1)}, bf16[864,192]{1,0:T(8,128)(2,1)S(1)}) custom-call(f32[16,128]{1,0:T(8,128)S(1)} %get-tuple-element.44.gram_ref, f32[16,128]{1,0:T(8,128)S(1)} %collective-permute-done.12.other_ref, bf16[432,128]{1,0:T(8,128)(2,1)S(1)} %copy-done.3), custom_call_target="tpu_custom_call" | custom-call | tf_op jit(solution)/shard_map/inverse/pallas_call | solution.py:436
  103.8 2.9 %all-to-all-done.5 = bf16[16,16,640]{2,1,0:T(8,128)(2,1)S(1)} async-done(((bf16[16,16,640]{2,1,0:T(8,128)(2,1)}), bf16[16,16,640]{2,1,0:T(8,128)(2,1)S(1)}, u32[]{:S(2)}, u32[]{:S(2)}) %all-to-all-start.5) | async-done | bytes 327712 | tf_op jit(solution)/shard_map/all_to_all | solution.py:31
  106.6 6.2 %residual.1 = (bf16[864,2560]{1,0:T(8,128)(2,1)}, f32[64,2560]{1,0:T(8,128)}) custom-call(bf16[64,192]{1,0:T(8,128)(2,1)S(1)} %get-tuple-element.46.terms_ref, bf16[864,192]{1,0:T(8,128)(2,1)S(1)} %get-tuple-element.47.ortho_ref, bf16[4,4,16,640]{3,2,1,0:T(8,128)(2,1)S(1)} %bitcast.13, bf16[864,2560]{1,0:T(8,128)(2,1)} %merged.1.merged_ref), custom_call_target="tpu_custom_call" | custom-call | tf_op jit(solution)/shard_map/residual/pallas_call | solution.py:445
Async XLA Ops:
  2.9 23.0 %copy-start = (bf16[1024,864]{0,1:T(8,128)(2,1)S(1)}, bf16[1024,864]{0,1:T(8,128)(2,1)}, u32[]{:S(2)}) copy-start(bf16[1024,864]{0,1:T(8,128)(2,1)} %param.5) | copy-start | bytes 5308420
  2.9 18.8 %collective-permute-start.1 = (bf16[64,2560]{1,0:T(8,128)(2,1)}, bf16[64,2560]{1,0:T(8,128)(2,1)S(1)}, u32[]{:S(2)}, u32[]{:S(2)}) collective-permute-start(bf16[64,2560]{1,0:T(8,128)(2,1)} %refs_3_), channel_id=1, source_target_pairs={{0,14},{2,0},{4,2},{6,4},{8,6},{10,8},{12,10},{14,12},{1,15},{3,1}... | collective-permute-start | bytes 983048 | tf_op jit(solution)/shard_map/ppermute | solution.py:290
  9.3 12.4 %collective-permute-start = (bf16[64,2560]{1,0:T(8,128)(2,1)}, bf16[64,2560]{1,0:T(8,128)(2,1)S(1)}, u32[]{:S(2)}, u32[]{:S(2)}) collective-permute-start(bf16[64,2560]{1,0:T(8,128)(2,1)} %refs_3_), channel_id=1, source_target_pairs={{0,2},{2,4},{4,6},{6,8},{8,10},{10,12},{12,14},{14,0},{1,3},{3,5},... | collective-permute-start | bytes 983048 | tf_op jit(solution)/shard_map/ppermute | solution.py:290
  9.3 12.4 %all-to-all-start = ((bf16[8,64,128]{2,1,0:T(8,128)(2,1)}), bf16[8,64,128]{2,1,0:T(8,128)(2,1)S(1)}, u32[]{:S(2)}, u32[]{:S(2)}) async-start(bf16[8,64,128]{2,1,0:T(8,128)(2,1)} %proj.1), calls=%async_computation | async-start | bytes 262144 | tf_op jit(solution)/shard_map/all_to_all | solution.py:31
  21.7 11.4 %collective-permute-start.4 = (bf16[64,2560]{1,0:T(8,128)(2,1)S(1)}, bf16[64,2560]{1,0:T(8,128)(2,1)S(1)}, u32[]{:S(2)}, u32[]{:S(2)}) collective-permute-start(bf16[64,2560]{1,0:T(8,128)(2,1)S(1)} %collective-permute-done.refs_4_), channel_id=1, source_target_pairs={{0,2},{2,4},{4,6},{6,8},{8,10},{10,12},{12,14},{14,0},{1,3},{3,5},... | collective-permute-start | bytes 983048 | tf_op jit(solution)/shard_map/ppermute | solution.py:290
  21.7 4.2 %collective-permute-start.2 = (bf16[8,64,128]{2,1,0:T(8,128)(2,1)S(1)}, bf16[8,64,128]{2,1,0:T(8,128)(2,1)S(1)}, u32[]{:S(2)}, u32[]{:S(2)}) collective-permute-start(bf16[8,64,128]{2,1,0:T(8,128)(2,1)S(1)} %all-to-all-done.own_ref), channel_id=1, source_target_pairs={{0,1},{1,0},{2,3},{3,2},{4,5},{5,4},{6,7},{7,6},{8,9},{9,8},{10,11... | collective-permute-start | bytes 393224 | tf_op jit(solution)/shard_map/ppermute | solution.py:280
  27.5 12.1 %all-to-all-start.1 = ((bf16[4,432,128]{2,1,0:T(8,128)(2,1)}), bf16[4,432,128]{2,1,0:T(8,128)(2,1)S(1)}, u32[]{:S(2)}, u32[]{:S(2)}) async-start(bf16[4,432,128]{2,1,0:T(8,128)(2,1)} %local_left.1), calls=%async_computation.1 | async-start | bytes 884736 | tf_op jit(solution)/shard_map/all_to_all | solution.py:31
  31.5 27.1 %copy-start.1 = (bf16[64,2560]{1,0:T(8,128)(2,1)S(1)}, bf16[64,2560]{1,0:T(8,128)(2,1)}, u32[]{:S(2)}) copy-start(bf16[64,2560]{1,0:T(8,128)(2,1)} %refs_3_) | copy-start | bytes 983044
  31.5 13.1 %collective-permute-start.7 = (bf16[64,2560]{1,0:T(8,128)(2,1)S(1)}, bf16[64,2560]{1,0:T(8,128)(2,1)}, u32[]{:S(2)}, u32[]{:S(2)}) collective-permute-start(bf16[64,2560]{1,0:T(8,128)(2,1)S(1)} %collective-permute-done.1.refs_10_), channel_id=1, source_target_pairs={{0,14},{2,0},{4,2},{6,4},{8,6},{10,8},{12,10},{14,12},{1,15},{3,1}... | collective-permute-start | bytes 983048 | tf_op jit(solution)/shard_map/ppermute | solution.py:290
  33.2 13.1 %collective-permute-start.5 = (bf16[64,2560]{1,0:T(8,128)(2,1)S(1)}, bf16[64,2560]{1,0:T(8,128)(2,1)}, u32[]{:S(2)}, u32[]{:S(2)}) collective-permute-start(bf16[64,2560]{1,0:T(8,128)(2,1)S(1)} %collective-permute-done.4.refs_5_), channel_id=1, source_target_pairs={{0,2},{2,4},{4,6},{6,8},{8,10},{10,12},{12,14},{14,0},{1,3},{3,5},... | collective-permute-start | bytes 983048 | tf_op jit(solution)/shard_map/ppermute | solution.py:290
  40.3 10.7 %all-to-all-start.2 = ((bf16[4,432,128]{2,1,0:T(8,128)(2,1)}), bf16[4,432,128]{2,1,0:T(8,128)(2,1)S(1)}, u32[]{:S(2)}, u32[]{:S(2)}) async-start(bf16[4,432,128]{2,1,0:T(8,128)(2,1)} %row_sum.1), calls=%async_computation.2 | async-start | bytes 884736 | tf_op jit(solution)/shard_map/all_to_all | solution.py:31
  44.5 14.0 %collective-permute-start.8 = (bf16[64,2560]{1,0:T(8,128)(2,1)}, bf16[64,2560]{1,0:T(8,128)(2,1)}, u32[]{:S(2)}, u32[]{:S(2)}) collective-permute-start(bf16[64,2560]{1,0:T(8,128)(2,1)} %collective-permute-done.7.refs_9_), channel_id=1, source_target_pairs={{0,14},{2,0},{4,2},{6,4},{8,6},{10,8},{12,10},{14,12},{1,15},{3,1}... | collective-permute-start | bytes 983048 | tf_op jit(solution)/shard_map/ppermute | solution.py:290
  46.2 12.4 %collective-permute-start.6 = (bf16[64,2560]{1,0:T(8,128)(2,1)}, bf16[64,2560]{1,0:T(8,128)(2,1)}, u32[]{:S(2)}, u32[]{:S(2)}) collective-permute-start(bf16[64,2560]{1,0:T(8,128)(2,1)} %collective-permute-done.5.refs_6_), channel_id=1, source_target_pairs={{0,2},{2,4},{4,6},{6,8},{8,10},{10,12},{12,14},{14,0},{1,3},{3,5},... | collective-permute-start | bytes 983048 | tf_op jit(solution)/shard_map/ppermute | solution.py:290
  52.8 5.8 %copy-start.2 = (bf16[432,128]{1,0:T(8,128)(2,1)}, bf16[432,128]{1,0:T(8,128)(2,1)S(1)}, u32[]{:S(2)}) copy-start(bf16[432,128]{1,0:T(8,128)(2,1)S(1)} %get-tuple-element.45.left_ref) | copy-start | bytes 331780
  52.8 5.7 %collective-permute-start.3 = (bf16[512,128]{1,0:T(8,128)(2,1)S(1)}, bf16[512,128]{1,0:T(8,128)(2,1)S(1)}, u32[]{:S(2)}, u32[]{:S(2)}) collective-permute-start(bf16[512,128]{1,0:T(8,128)(2,1)S(1)} %get-tuple-element.33), channel_id=1, source_target_pairs={{0,1},{1,0},{2,3},{3,2},{4,5},{5,4},{6,7},{7,6},{8,9},{9,8},{10,11... | collective-permute-start | bytes 393224 | tf_op jit(solution)/shard_map/ppermute | solution.py:280
  62.5 12.6 %collective-permute-start.9 = (bf16[512,2560]{1,0:T(8,128)(2,1)}, bf16[512,2560]{1,0:T(8,128)(2,1)}, u32[]{:S(2)}, u32[]{:S(2)}) collective-permute-start(bf16[512,2560]{1,0:T(8,128)(2,1)} %get-tuple-element.38.half_ref), channel_id=1, source_target_pairs={{0,1},{1,0},{2,3},{3,2},{4,5},{5,4},{6,7},{7,6},{8,9},{9,8},{10,11... | collective-permute-start | bytes 7864328 | tf_op jit(solution)/shard_map/ppermute | solution.py:280
  62.6 12.5 %all-to-all-start.3 = ((bf16[16,16,640]{2,1,0:T(8,128)(2,1)}), bf16[16,16,640]{2,1,0:T(8,128)(2,1)S(1)}, u32[]{:S(2)}, u32[]{:S(2)}) async-start(bf16[16,16,640]{2,1,0:T(8,128)(2,1)} %get-tuple-element.37), calls=%async_computation.3 | async-start | bytes 655360 | tf_op jit(solution)/shard_map/all_to_all | solution.py:31
  66.8 1.5 %collective-permute-start.10 = (f32[32,128]{1,0:T(8,128)S(1)}, f32[32,128]{1,0:T(8,128)S(1)}, u32[]{:S(2)}, u32[]{:S(2)}) collective-permute-start(f32[32,128]{1,0:T(8,128)S(1)} %get-tuple-element.39.gram_ref), channel_id=1, source_target_pairs={{0,1},{1,0},{2,3},{3,2},{4,5},{5,4},{6,7},{7,6},{8,9},{9,8},{10,11... | collective-permute-start | bytes 49160 | tf_op jit(solution)/shard_map/ppermute | solution.py:280
  75.2 2.7 %collective-permute-start.11 = (bf16[16,640]{1,0:T(8,128)(2,1)S(1)}, bf16[16,640]{1,0:T(8,128)(2,1)S(1)}, u32[]{:S(2)}, u32[]{:S(2)}) collective-permute-start(bf16[16,640]{1,0:T(8,128)(2,1)S(1)} %replica_sum.1.own_ref), channel_id=1, source_target_pairs={{0,1},{1,0},{2,3},{3,2},{4,5},{5,4},{6,7},{7,6},{8,9},{9,8},{10,11... | collective-permute-start | bytes 61448 | tf_op jit(solution)/shard_map/ppermute | solution.py:280
  78.6 15.7 %all-to-all-start.4 = ((bf16[8,16,1024]{2,1,0:T(8,128)(2,1)}), bf16[8,16,1024]{2,1,0:T(8,128)(2,1)S(1)}, u32[]{:S(2)}, u32[]{:S(2)}) async-start(bf16[8,16,1024]{2,1,0:T(8,128)(2,1)} %core_sum.1), calls=%async_computation.4 | async-start | bytes 524288 | tf_op jit(solution)/shard_map/all_to_all | solution.py:31
  82.1 18.1 %copy-start.3 = (bf16[432,128]{1,0:T(8,128)(2,1)S(1)}, bf16[432,128]{1,0:T(8,128)(2,1)}, u32[]{:S(2)}) copy-start(bf16[432,128]{1,0:T(8,128)(2,1)} %copy-done.2) | copy-start | bytes 331780
  95.1 11.5 %all-to-all-start.5 = ((bf16[16,16,640]{2,1,0:T(8,128)(2,1)}), bf16[16,16,640]{2,1,0:T(8,128)(2,1)S(1)}, u32[]{:S(2)}, u32[]{:S(2)}) async-start(bf16[16,16,640]{2,1,0:T(8,128)(2,1)} %get-tuple-element.48), calls=%async_computation.5 | async-start | bytes 655360 | tf_op jit(solution)/shard_map/all_to_all | solution.py:31
  98.7 1.5 %collective-permute-start.12 = (f32[16,128]{1,0:T(8,128)S(1)}, f32[16,128]{1,0:T(8,128)S(1)}, u32[]{:S(2)}, u32[]{:S(2)}) collective-permute-start(f32[16,128]{1,0:T(8,128)S(1)} %get-tuple-element.44.gram_ref), channel_id=1, source_target_pairs={{0,1},{1,0},{2,3},{3,2},{4,5},{5,4},{6,7},{7,6},{8,9},{9,8},{10,11... | collective-permute-start | bytes 24584 | tf_op jit(solution)/shard_map/ppermute | solution.py:280

commit v7 on v6

--- a/solution.py
+++ b/solution.py
@@ -157,17 +157,24 @@
     rank = right_ref.shape[0]
     both = keep_ref[...].astype(f32) + other_ref[...].astype(f32)
     both = jnp.concatenate(split((both[:, :rank] + both[:, rank:]).T), axis=0)
-    for copy in copies:
+    tokens = chunk_refs[0].shape[0]
+    kept = []
+    for i, copy in enumerate(copies):
         copy.wait()
-    half_copy = pltpu.make_async_copy(half_ref, half_hbm, sems.at[count])
-    half_copy.start()
+        row = lax.rem(lax.axis_index("mp_0") + (count - i), count) * tokens
+        rows = pl.ds(pl.multiple_of(row, tokens), tokens)
+        kept.append(
+            pltpu.make_async_copy(half_ref.at[rows, :], half_hbm.at[rows, :], sems.at[count + i])
+        )
+        kept[i].start()
     both = product(both, half_ref[...], 1, 0)
     right = (right_ref[...] + both[:rank] + both[rank:]).astype(bf16)
     height, width = out_ref.shape[1:]
     for a in range(4):
         for b in range(4):
             out_ref[4 * a + b] = right[a * height : (a + 1) * height, b * width : (b + 1) * width]
-    half_copy.wait()
+    for copy in kept:
+        copy.wait()
 
 
 def merged_kernel(act_ref, own_ref, half_ref, other_ref, out_ref, full_ref):
@@ -386,7 +393,7 @@
         limit=50,
         in_specs=[whole, whole, whole] + [anywhere] * len(chunks),
         out_specs=(whole, in_hbm),
-        scratch_shapes=[VMEM((half, features), bf16), pltpu.SemaphoreType.DMA((len(chunks) + 1,))],
+        scratch_shapes=[VMEM((half, features), bf16), pltpu.SemaphoreType.DMA((2 * len(chunks),))],
         name="right_product",
     )(keep, swapped(give), right, *chunks)
 

time: 114 us -> 113 us (level)
  transfers between devices with their start and end apart: 19 -> 19, of which waited for: 10 -> 10; matrix products, arithmetic and copies ran while one was open for 4% -> 4% of each run, Pallas kernels for 18% -> 19%
where the time goes in v7:
time: 113 us; the launch traced here: 112 us
  starting transfers between devices  42.7 us (38%)
  Pallas kernels  34.3 us (30%)
  waiting for transfers between devices  29.9 us (26%)
  matrix products  3.56 us (3%)
  other arithmetic  1.16 us (1%)
    all_to_all x6, waiting for transfers between devices, sent(): return lax.all_to_all(array, axis, 0, 0, tiled=True)  26.4 us
    all_to_all x6, starting transfers between devices, sent(): return lax.all_to_all(array, axis, 0, 0, tiled=True)  23.4 us
    pallas_call x1, Pallas kernels, per_device(): call(merged_kernel, of(own.shape, bf16), limit=58, grid=(4,), in_specs=[p...  10.5 us
    ppermute x7, starting transfers between devices, passed(): lax.ppermute(array, 'mp_0', [(i, (i + hop) % self.size) for i in range(se...  9.76 us
    ppermute x6, starting transfers between devices, swapped(): return lax.ppermute(array, 'mp_1', [(0, 1), (1, 0)])  9.53 us
    pallas_call x1, Pallas kernels, per_device(): call(functools.partial(residual_kernel, replicas), (of(own.shape, bf16),...  6.22 us
    pallas_call x1, Pallas kernels, per_device(): call(inverse_kernel, (of((rank, 3 * rank), bf16), of((2 * rows, 3 * rank)...  3.59 us
    dot_general x1, matrix products, product(): lax.dot_general(left, right, (((left_dim,), (right_dim,)), ((), ())), pre...  3.56 us
  transfers between devices with their start and end apart: 19, of which 10 were waited for; matrix products, arithmetic and copies ran while one was open for 4% of the time, Pallas kernels for 19%

profile of v7, /device:TPU:1, one launch (start us, length us, event | category | flops | bytes accessed | tf_op | source)
XLA Modules:
  0.0 112.4 jit_solution(12886666027363529966)
XLA Ops:
  0.6 2.3 %proj.1 = bf16[8,64,128]{2,1,0:T(8,128)(2,1)} custom-call(bf16[64,2560]{1,0:T(8,128)(2,1)} %refs_3_, f32[64,2560]{1,0:T(8,128)} %bitcast.16), custom_call_target="tpu_custom_call" | custom-call | tf_op jit(solution)/shard_map/proj/pallas_call | solution.py:325
  2.9 0.0 copy-start
  2.9 6.4 %collective-permute-start.1 = (bf16[64,2560]{1,0:T(8,128)(2,1)}, bf16[64,2560]{1,0:T(8,128)(2,1)S(1)}, u32[]{:S(2)}, u32[]{:S(2)}) collective-permute-start(bf16[64,2560]{1,0:T(8,128)(2,1)} %refs_3_), channel_id=1, source_target_pairs={{0,14},{2,0},{4,2},{6,4},{8,6},{10,8},{12,10},{14,12},{1,15},{3,1}... | collective-permute-start | bytes 983048 | tf_op jit(solution)/shard_map/ppermute | solution.py:297
  9.3 0.0 collective-permute-start
  9.3 4.1 %all-to-all-start = ((bf16[8,64,128]{2,1,0:T(8,128)(2,1)}), bf16[8,64,128]{2,1,0:T(8,128)(2,1)S(1)}, u32[]{:S(2)}, u32[]{:S(2)}) async-start(bf16[8,64,128]{2,1,0:T(8,128)(2,1)} %proj.1), calls=%async_computation | async-start | bytes 262144 | tf_op jit(solution)/shard_map/all_to_all | solution.py:31
  13.4 1.2 %reduce-precision_convert_fusion = (bf16[2560,64]{0,1:T(8,128)(2,1)S(1)}, bf16[2560,64]{0,1:T(8,128)(2,1)S(1)}) fusion(f32[2560,64]{0,1:T(8,128)} %param.7), kind=kLoop, calls=%fused_computation.2 | loop fusion | flops 655360 | bytes 1310720 | tf_op jit(solution)/shard_map/convert_element_type | solution.py:36
  14.5 3.6 %convolution_bitcast_fusion.carried_ref = f32[864,128]{1,0:T(8,128)S(1)} fusion(bf16[2560,64]{0,1:T(8,128)(2,1)S(1)} %get-tuple-element.53, bf16[2560,64]{0,1:T(8,128)(2,1)S(1)} %get-tuple-element.52, bf16[1,864,2560]{2,1,0:T(8,128)(2,1)} %param.6), kind=kOutput, calls=%fused_computation | convolution fusion | flops 567541760 | bytes 5521408 | tf_op jit(solution)/shard_map/dot_general | solution.py:25
  18.1 3.6 %all-to-all-done.own_ref = bf16[8,64,128]{2,1,0:T(8,128)(2,1)S(1)} async-done(((bf16[8,64,128]{2,1,0:T(8,128)(2,1)}), bf16[8,64,128]{2,1,0:T(8,128)(2,1)S(1)}, u32[]{:S(2)}, u32[]{:S(2)}) %all-to-all-start) | async-done | bytes 131104 | tf_op jit(solution)/shard_map/all_to_all | solution.py:31
  21.7 0.0 collective-permute-done.1.refs_10_
  21.7 0.0 collective-permute-done.refs_4_
  21.7 0.0 collective-permute-start.4
  21.7 3.2 %collective-permute-start.2 = (bf16[8,64,128]{2,1,0:T(8,128)(2,1)S(1)}, bf16[8,64,128]{2,1,0:T(8,128)(2,1)S(1)}, u32[]{:S(2)}, u32[]{:S(2)}) collective-permute-start(bf16[8,64,128]{2,1,0:T(8,128)(2,1)S(1)} %all-to-all-done.own_ref), channel_id=1, source_target_pairs={{0,1},{1,0},{2,3},{3,2},{4,5},{5,4},{6,7},{7,6},{8,9},{9,8},{10,11... | collective-permute-start | bytes 393224 | tf_op jit(solution)/shard_map/ppermute | solution.py:287
  24.9 1.0 collective-permute-done.2.other_ref
  25.9 0.0 copy-done
  25.9 1.5 %local_left.1 = bf16[4,432,128]{2,1,0:T(8,128)(2,1)} custom-call(bf16[8,64,128]{2,1,0:T(8,128)(2,1)S(1)} %all-to-all-done.own_ref, bf16[8,64,128]{2,1,0:T(8,128)(2,1)S(1)} %collective-permute-done.2.other_ref, f32[864,128]{1,0:T(8,128)S(1)} %convolution_bitcast_fusion.carried_ref, bf16[864,1024]{1,0:T(8,128)(2,1)S(1)} %bitcast.11), custom_call_target="tpu_custom_call" | custom-call | tf_op jit(solution)/shard_map/local_left/pallas_call | solution.py:339
  27.5 4.0 %all-to-all-start.1 = ((bf16[4,432,128]{2,1,0:T(8,128)(2,1)}), bf16[4,432,128]{2,1,0:T(8,128)(2,1)S(1)}, u32[]{:S(2)}, u32[]{:S(2)}) async-start(bf16[4,432,128]{2,1,0:T(8,128)(2,1)} %local_left.1), calls=%async_computation.1 | async-start | bytes 884736 | tf_op jit(solution)/shard_map/all_to_all | solution.py:31
  31.5 0.0 copy-start.1
  31.5 1.7 %collective-permute-start.7 = (bf16[64,2560]{1,0:T(8,128)(2,1)S(1)}, bf16[64,2560]{1,0:T(8,128)(2,1)}, u32[]{:S(2)}, u32[]{:S(2)}) collective-permute-start(bf16[64,2560]{1,0:T(8,128)(2,1)S(1)} %collective-permute-done.1.refs_10_), channel_id=1, source_target_pairs={{0,14},{2,0},{4,2},{6,4},{8,6},{10,8},{12,10},{14,12},{1,15},{3,1}... | collective-permute-start | bytes 983048 | tf_op jit(solution)/shard_map/ppermute | solution.py:297
  33.2 0.0 collective-permute-done.4.refs_5_
  33.2 0.0 collective-permute-start.5
  33.2 6.4 %all-to-all-done.1.parts_ref = bf16[4,432,128]{2,1,0:T(8,128)(2,1)S(1)} async-done(((bf16[4,432,128]{2,1,0:T(8,128)(2,1)}), bf16[4,432,128]{2,1,0:T(8,128)(2,1)S(1)}, u32[]{:S(2)}, u32[]{:S(2)}) %all-to-all-start.1) | async-done | bytes 442400 | tf_op jit(solution)/shard_map/all_to_all | solution.py:31
  39.5 0.8 row_sum.1
  40.3 4.2 %all-to-all-start.2 = ((bf16[4,432,128]{2,1,0:T(8,128)(2,1)}), bf16[4,432,128]{2,1,0:T(8,128)(2,1)S(1)}, u32[]{:S(2)}, u32[]{:S(2)}) async-start(bf16[4,432,128]{2,1,0:T(8,128)(2,1)} %row_sum.1), calls=%async_computation.2 | async-start | bytes 884736 | tf_op jit(solution)/shard_map/all_to_all | solution.py:31
  44.5 0.0 collective-permute-done.7.refs_9_
  44.5 1.7 %collective-permute-start.8 = (bf16[64,2560]{1,0:T(8,128)(2,1)}, bf16[64,2560]{1,0:T(8,128)(2,1)}, u32[]{:S(2)}, u32[]{:S(2)}) collective-permute-start(bf16[64,2560]{1,0:T(8,128)(2,1)} %collective-permute-done.7.refs_9_), channel_id=1, source_target_pairs={{0,14},{2,0},{4,2},{6,4},{8,6},{10,8},{12,10},{14,12},{1,15},{3,1}... | collective-permute-start | bytes 983048 | tf_op jit(solution)/shard_map/ppermute | solution.py:297
  46.2 0.0 collective-permute-done.5.refs_6_
  46.2 0.0 collective-permute-start.6
  46.2 4.9 %all-to-all-done.2.parts_ref = bf16[4,432,128]{2,1,0:T(8,128)(2,1)S(1)} async-done(((bf16[4,432,128]{2,1,0:T(8,128)(2,1)}), bf16[4,432,128]{2,1,0:T(8,128)(2,1)S(1)}, u32[]{:S(2)}, u32[]{:S(2)}) %all-to-all-start.2) | async-done | bytes 442400 | tf_op jit(solution)/shard_map/all_to_all | solution.py:31
  51.1 1.7 %left_sum.1 = (bf16[432,128]{1,0:T(8,128)(2,1)S(1)}, bf16[128,432]{1,0:T(8,128)(2,1)S(1)}, f32[32,128]{1,0:T(8,128)S(1)}, bf16[512,128]{1,0:T(8,128)(2,1)S(1)}, bf16[512,128]{1,0:T(8,128)(2,1)S(1)}) custom-call(bf16[4,432,128]{2,1,0:T(8,128)(2,1)S(1)} %all-to-all-done.2.parts_ref, bf16[864,1024]{1,0:T(8,128)(2,1)S(1)} %bitcast.12), custom_call_target="tpu_custom_call" | custom-call | tf_op jit(solution)/shard_map/left_sum/pallas_call | solution.py:361
  52.8 0.0 copy-start.2
  52.8 3.1 %collective-permute-start.3 = (bf16[512,128]{1,0:T(8,128)(2,1)S(1)}, bf16[512,128]{1,0:T(8,128)(2,1)S(1)}, u32[]{:S(2)}, u32[]{:S(2)}) collective-permute-start(bf16[512,128]{1,0:T(8,128)(2,1)S(1)} %get-tuple-element.33), channel_id=1, source_target_pairs={{0,1},{1,0},{2,3},{3,2},{4,5},{5,4},{6,7},{7,6},{8,9},{9,8},{10,11... | collective-permute-start | bytes 393224 | tf_op jit(solution)/shard_map/ppermute | solution.py:287
  55.9 2.6 %own_product.1.refs_2_ = f32[64,2560]{1,0:T(8,128)S(1)} custom-call(bf16[128,432]{1,0:T(8,128)(2,1)S(1)} %get-tuple-element.34.turned_ref, bf16[864,2560]{1,0:T(8,128)(2,1)} %bitcast.14), custom_call_target="tpu_custom_call" | custom-call | tf_op jit(solution)/shard_map/own_product/pallas_call | solution.py:380
  58.6 0.0 collective-permute-done.8.refs_8_
  58.6 0.0 collective-permute-done.3.refs_1_
  58.6 0.0 copy-done.2
  58.6 0.0 collective-permute-done.6.refs_7_
  58.6 0.0 copy-done.1
  58.6 3.4 %right_product.1 = (bf16[16,16,640]{2,1,0:T(8,128)(2,1)}, bf16[512,2560]{1,0:T(8,128)(2,1)}) custom-call(bf16[512,128]{1,0:T(8,128)(2,1)S(1)} %get-tuple-element.32.refs_0_, bf16[512,128]{1,0:T(8,128)(2,1)S(1)} %collective-permute-done.3.refs_1_, f32[64,2560]{1,0:T(8,128)S(1)} %own_product.1.refs_2_, bf16[64,2560]{1,0:T(8,128)(2,1)S(1)} %copy-done.1, ...), custom_call_target="tpu_custom_call" | custom-call | tf_op jit(solution)/shard_map/right_product/pallas_call | solution.py:390
  62.0 0.1 collective-permute-start.9
  62.1 4.2 %all-to-all-start.3 = ((bf16[16,16,640]{2,1,0:T(8,128)(2,1)}), bf16[16,16,640]{2,1,0:T(8,128)(2,1)S(1)}, u32[]{:S(2)}, u32[]{:S(2)}) async-start(bf16[16,16,640]{2,1,0:T(8,128)(2,1)} %get-tuple-element.37), calls=%async_computation.3 | async-start | bytes 655360 | tf_op jit(solution)/shard_map/all_to_all | solution.py:31
  66.3 0.6 collective-permute-start.10
  66.9 0.9 collective-permute-done.10.other_gram_ref
  67.8 6.9 %all-to-all-done.3.parts_ref = bf16[16,16,640]{2,1,0:T(8,128)(2,1)S(1)} async-done(((bf16[16,16,640]{2,1,0:T(8,128)(2,1)}), bf16[16,16,640]{2,1,0:T(8,128)(2,1)S(1)}, u32[]{:S(2)}, u32[]{:S(2)}) %all-to-all-start.3) | async-done | bytes 327712 | tf_op jit(solution)/shard_map/all_to_all | solution.py:31
  74.6 0.0 collective-permute-done.9.other_ref
  74.7 0.1 replica_sum.1.own_ref
  74.7 1.9 %collective-permute-start.11 = (bf16[16,640]{1,0:T(8,128)(2,1)S(1)}, bf16[16,640]{1,0:T(8,128)(2,1)S(1)}, u32[]{:S(2)}, u32[]{:S(2)}) collective-permute-start(bf16[16,640]{1,0:T(8,128)(2,1)S(1)} %replica_sum.1.own_ref), channel_id=1, source_target_pairs={{0,1},{1,0},{2,3},{3,2},{4,5},{5,4},{6,7},{7,6},{8,9},{9,8},{10,11... | collective-permute-start | bytes 61448 | tf_op jit(solution)/shard_map/ppermute | solution.py:287
  76.6 0.8 collective-permute-done.11.other_ref
  77.4 0.7 core_sum.1
  78.2 3.4 %all-to-all-start.4 = ((bf16[8,16,1024]{2,1,0:T(8,128)(2,1)}), bf16[8,16,1024]{2,1,0:T(8,128)(2,1)S(1)}, u32[]{:S(2)}, u32[]{:S(2)}) async-start(bf16[8,16,1024]{2,1,0:T(8,128)(2,1)} %core_sum.1), calls=%async_computation.4 | async-start | bytes 524288 | tf_op jit(solution)/shard_map/all_to_all | solution.py:31
  81.6 0.0 copy-start.3
  81.6 10.5 %merged.1.merged_ref = bf16[864,2560]{1,0:T(8,128)(2,1)} custom-call(bf16[864,1024]{1,0:T(8,128)(2,1)} %bitcast.10, bf16[864,2560]{1,0:T(8,128)(2,1)} %bitcast.15, bf16[512,2560]{1,0:T(8,128)(2,1)} %get-tuple-element.38.half_ref, bf16[512,2560]{1,0:T(8,128)(2,1)} %collective-permute-done.9.other_ref), custom_call_target="tpu_custom_call" | custom-call | tf_op jit(solution)/shard_map/merged/pallas_call | solution.py:405
  92.1 1.8 %all-to-all-done.4.parts_ref = bf16[8,16,1024]{2,1,0:T(8,128)(2,1)S(1)} async-done(((bf16[8,16,1024]{2,1,0:T(8,128)(2,1)}), bf16[8,16,1024]{2,1,0:T(8,128)(2,1)S(1)}, u32[]{:S(2)}, u32[]{:S(2)}) %all-to-all-start.4) | async-done | bytes 262176 | tf_op jit(solution)/shard_map/all_to_all | solution.py:31
  93.8 0.8 chip_sum.1
  94.6 3.5 %all-to-all-start.5 = ((bf16[16,16,640]{2,1,0:T(8,128)(2,1)}), bf16[16,16,640]{2,1,0:T(8,128)(2,1)S(1)}, u32[]{:S(2)}, u32[]{:S(2)}) async-start(bf16[16,16,640]{2,1,0:T(8,128)(2,1)} %get-tuple-element.48), calls=%async_computation.5 | async-start | bytes 655360 | tf_op jit(solution)/shard_map/all_to_all | solution.py:31
  98.2 0.7 collective-permute-start.12
  98.8 0.8 collective-permute-done.12.other_ref
  99.7 0.0 copy-done.3
  99.7 3.6 %inverse.1 = (bf16[64,192]{1,0:T(8,128)(2,1)S(1)}, bf16[864,192]{1,0:T(8,128)(2,1)S(1)}) custom-call(f32[16,128]{1,0:T(8,128)S(1)} %get-tuple-element.44.gram_ref, f32[16,128]{1,0:T(8,128)S(1)} %collective-permute-done.12.other_ref, bf16[432,128]{1,0:T(8,128)(2,1)S(1)} %copy-done.3), custom_call_target="tpu_custom_call" | custom-call | tf_op jit(solution)/shard_map/inverse/pallas_call | solution.py:443
  103.3 2.9 %all-to-all-done.5 = bf16[16,16,640]{2,1,0:T(8,128)(2,1)S(1)} async-done(((bf16[16,16,640]{2,1,0:T(8,128)(2,1)}), bf16[16,16,640]{2,1,0:T(8,128)(2,1)S(1)}, u32[]{:S(2)}, u32[]{:S(2)}) %all-to-all-start.5) | async-done | bytes 327712 | tf_op jit(solution)/shard_map/all_to_all | solution.py:31
  106.2 6.2 %residual.1 = (bf16[864,2560]{1,0:T(8,128)(2,1)}, f32[64,2560]{1,0:T(8,128)}) custom-call(bf16[64,192]{1,0:T(8,128)(2,1)S(1)} %get-tuple-element.46.terms_ref, bf16[864,192]{1,0:T(8,128)(2,1)S(1)} %get-tuple-element.47.ortho_ref, bf16[4,4,16,640]{3,2,1,0:T(8,128)(2,1)S(1)} %bitcast.13, bf16[864,2560]{1,0:T(8,128)(2,1)} %merged.1.merged_ref), custom_call_target="tpu_custom_call" | custom-call | tf_op jit(solution)/shard_map/residual/pallas_call | solution.py:452
Async XLA Ops:
  2.9 23.0 %copy-start = (bf16[1024,864]{0,1:T(8,128)(2,1)S(1)}, bf16[1024,864]{0,1:T(8,128)(2,1)}, u32[]{:S(2)}) copy-start(bf16[1024,864]{0,1:T(8,128)(2,1)} %param.5) | copy-start | bytes 5308420
  2.9 18.8 %collective-permute-start.1 = (bf16[64,2560]{1,0:T(8,128)(2,1)}, bf16[64,2560]{1,0:T(8,128)(2,1)S(1)}, u32[]{:S(2)}, u32[]{:S(2)}) collective-permute-start(bf16[64,2560]{1,0:T(8,128)(2,1)} %refs_3_), channel_id=1, source_target_pairs={{0,14},{2,0},{4,2},{6,4},{8,6},{10,8},{12,10},{14,12},{1,15},{3,1}... | collective-permute-start | bytes 983048 | tf_op jit(solution)/shard_map/ppermute | solution.py:297
  9.3 12.4 %collective-permute-start = (bf16[64,2560]{1,0:T(8,128)(2,1)}, bf16[64,2560]{1,0:T(8,128)(2,1)S(1)}, u32[]{:S(2)}, u32[]{:S(2)}) collective-permute-start(bf16[64,2560]{1,0:T(8,128)(2,1)} %refs_3_), channel_id=1, source_target_pairs={{0,2},{2,4},{4,6},{6,8},{8,10},{10,12},{12,14},{14,0},{1,3},{3,5},... | collective-permute-start | bytes 983048 | tf_op jit(solution)/shard_map/ppermute | solution.py:297
  9.3 12.4 %all-to-all-start = ((bf16[8,64,128]{2,1,0:T(8,128)(2,1)}), bf16[8,64,128]{2,1,0:T(8,128)(2,1)S(1)}, u32[]{:S(2)}, u32[]{:S(2)}) async-start(bf16[8,64,128]{2,1,0:T(8,128)(2,1)} %proj.1), calls=%async_computation | async-start | bytes 262144 | tf_op jit(solution)/shard_map/all_to_all | solution.py:31
  21.7 11.4 %collective-permute-start.4 = (bf16[64,2560]{1,0:T(8,128)(2,1)S(1)}, bf16[64,2560]{1,0:T(8,128)(2,1)S(1)}, u32[]{:S(2)}, u32[]{:S(2)}) collective-permute-start(bf16[64,2560]{1,0:T(8,128)(2,1)S(1)} %collective-permute-done.refs_4_), channel_id=1, source_target_pairs={{0,2},{2,4},{4,6},{6,8},{8,10},{10,12},{12,14},{14,0},{1,3},{3,5},... | collective-permute-start | bytes 983048 | tf_op jit(solution)/shard_map/ppermute | solution.py:297
  21.7 4.2 %collective-permute-start.2 = (bf16[8,64,128]{2,1,0:T(8,128)(2,1)S(1)}, bf16[8,64,128]{2,1,0:T(8,128)(2,1)S(1)}, u32[]{:S(2)}, u32[]{:S(2)}) collective-permute-start(bf16[8,64,128]{2,1,0:T(8,128)(2,1)S(1)} %all-to-all-done.own_ref), channel_id=1, source_target_pairs={{0,1},{1,0},{2,3},{3,2},{4,5},{5,4},{6,7},{7,6},{8,9},{9,8},{10,11... | collective-permute-start | bytes 393224 | tf_op jit(solution)/shard_map/ppermute | solution.py:287
  27.5 12.1 %all-to-all-start.1 = ((bf16[4,432,128]{2,1,0:T(8,128)(2,1)}), bf16[4,432,128]{2,1,0:T(8,128)(2,1)S(1)}, u32[]{:S(2)}, u32[]{:S(2)}) async-start(bf16[4,432,128]{2,1,0:T(8,128)(2,1)} %local_left.1), calls=%async_computation.1 | async-start | bytes 884736 | tf_op jit(solution)/shard_map/all_to_all | solution.py:31
  31.5 27.1 %copy-start.1 = (bf16[64,2560]{1,0:T(8,128)(2,1)S(1)}, bf16[64,2560]{1,0:T(8,128)(2,1)}, u32[]{:S(2)}) copy-start(bf16[64,2560]{1,0:T(8,128)(2,1)} %refs_3_) | copy-start | bytes 983044
  31.5 13.1 %collective-permute-start.7 = (bf16[64,2560]{1,0:T(8,128)(2,1)S(1)}, bf16[64,2560]{1,0:T(8,128)(2,1)}, u32[]{:S(2)}, u32[]{:S(2)}) collective-permute-start(bf16[64,2560]{1,0:T(8,128)(2,1)S(1)} %collective-permute-done.1.refs_10_), channel_id=1, source_target_pairs={{0,14},{2,0},{4,2},{6,4},{8,6},{10,8},{12,10},{14,12},{1,15},{3,1}... | collective-permute-start | bytes 983048 | tf_op jit(solution)/shard_map/ppermute | solution.py:297
  33.2 13.1 %collective-permute-start.5 = (bf16[64,2560]{1,0:T(8,128)(2,1)S(1)}, bf16[64,2560]{1,0:T(8,128)(2,1)}, u32[]{:S(2)}, u32[]{:S(2)}) collective-permute-start(bf16[64,2560]{1,0:T(8,128)(2,1)S(1)} %collective-permute-done.4.refs_5_), channel_id=1, source_target_pairs={{0,2},{2,4},{4,6},{6,8},{8,10},{10,12},{12,14},{14,0},{1,3},{3,5},... | collective-permute-start | bytes 983048 | tf_op jit(solution)/shard_map/ppermute | solution.py:297
  40.3 10.7 %all-to-all-start.2 = ((bf16[4,432,128]{2,1,0:T(8,128)(2,1)}), bf16[4,432,128]{2,1,0:T(8,128)(2,1)S(1)}, u32[]{:S(2)}, u32[]{:S(2)}) async-start(bf16[4,432,128]{2,1,0:T(8,128)(2,1)} %row_sum.1), calls=%async_computation.2 | async-start | bytes 884736 | tf_op jit(solution)/shard_map/all_to_all | solution.py:31
  44.5 14.0 %collective-permute-start.8 = (bf16[64,2560]{1,0:T(8,128)(2,1)}, bf16[64,2560]{1,0:T(8,128)(2,1)}, u32[]{:S(2)}, u32[]{:S(2)}) collective-permute-start(bf16[64,2560]{1,0:T(8,128)(2,1)} %collective-permute-done.7.refs_9_), channel_id=1, source_target_pairs={{0,14},{2,0},{4,2},{6,4},{8,6},{10,8},{12,10},{14,12},{1,15},{3,1}... | collective-permute-start | bytes 983048 | tf_op jit(solution)/shard_map/ppermute | solution.py:297
  46.2 12.4 %collective-permute-start.6 = (bf16[64,2560]{1,0:T(8,128)(2,1)}, bf16[64,2560]{1,0:T(8,128)(2,1)}, u32[]{:S(2)}, u32[]{:S(2)}) collective-permute-start(bf16[64,2560]{1,0:T(8,128)(2,1)} %collective-permute-done.5.refs_6_), channel_id=1, source_target_pairs={{0,2},{2,4},{4,6},{6,8},{8,10},{10,12},{12,14},{14,0},{1,3},{3,5},... | collective-permute-start | bytes 983048 | tf_op jit(solution)/shard_map/ppermute | solution.py:297
  52.8 5.8 %copy-start.2 = (bf16[432,128]{1,0:T(8,128)(2,1)}, bf16[432,128]{1,0:T(8,128)(2,1)S(1)}, u32[]{:S(2)}) copy-start(bf16[432,128]{1,0:T(8,128)(2,1)S(1)} %get-tuple-element.45.left_ref) | copy-start | bytes 331780
  52.8 5.7 %collective-permute-start.3 = (bf16[512,128]{1,0:T(8,128)(2,1)S(1)}, bf16[512,128]{1,0:T(8,128)(2,1)S(1)}, u32[]{:S(2)}, u32[]{:S(2)}) collective-permute-start(bf16[512,128]{1,0:T(8,128)(2,1)S(1)} %get-tuple-element.33), channel_id=1, source_target_pairs={{0,1},{1,0},{2,3},{3,2},{4,5},{5,4},{6,7},{7,6},{8,9},{9,8},{10,11... | collective-permute-start | bytes 393224 | tf_op jit(solution)/shard_map/ppermute | solution.py:287
  62.0 12.6 %collective-permute-start.9 = (bf16[512,2560]{1,0:T(8,128)(2,1)}, bf16[512,2560]{1,0:T(8,128)(2,1)}, u32[]{:S(2)}, u32[]{:S(2)}) collective-permute-start(bf16[512,2560]{1,0:T(8,128)(2,1)} %get-tuple-element.38.half_ref), channel_id=1, source_target_pairs={{0,1},{1,0},{2,3},{3,2},{4,5},{5,4},{6,7},{7,6},{8,9},{9,8},{10,11... | collective-permute-start | bytes 7864328 | tf_op jit(solution)/shard_map/ppermute | solution.py:287
  62.1 12.5 %all-to-all-start.3 = ((bf16[16,16,640]{2,1,0:T(8,128)(2,1)}), bf16[16,16,640]{2,1,0:T(8,128)(2,1)S(1)}, u32[]{:S(2)}, u32[]{:S(2)}) async-start(bf16[16,16,640]{2,1,0:T(8,128)(2,1)} %get-tuple-element.37), calls=%async_computation.3 | async-start | bytes 655360 | tf_op jit(solution)/shard_map/all_to_all | solution.py:31
  66.3 1.5 %collective-permute-start.10 = (f32[32,128]{1,0:T(8,128)S(1)}, f32[32,128]{1,0:T(8,128)S(1)}, u32[]{:S(2)}, u32[]{:S(2)}) collective-permute-start(f32[32,128]{1,0:T(8,128)S(1)} %get-tuple-element.39.gram_ref), channel_id=1, source_target_pairs={{0,1},{1,0},{2,3},{3,2},{4,5},{5,4},{6,7},{7,6},{8,9},{9,8},{10,11... | collective-permute-start | bytes 49160 | tf_op jit(solution)/shard_map/ppermute | solution.py:287
  74.7 2.7 %collective-permute-start.11 = (bf16[16,640]{1,0:T(8,128)(2,1)S(1)}, bf16[16,640]{1,0:T(8,128)(2,1)S(1)}, u32[]{:S(2)}, u32[]{:S(2)}) collective-permute-start(bf16[16,640]{1,0:T(8,128)(2,1)S(1)} %replica_sum.1.own_ref), channel_id=1, source_target_pairs={{0,1},{1,0},{2,3},{3,2},{4,5},{5,4},{6,7},{7,6},{8,9},{9,8},{10,11... | collective-permute-start | bytes 61448 | tf_op jit(solution)/shard_map/ppermute | solution.py:287
  78.2 15.7 %all-to-all-start.4 = ((bf16[8,16,1024]{2,1,0:T(8,128)(2,1)}), bf16[8,16,1024]{2,1,0:T(8,128)(2,1)S(1)}, u32[]{:S(2)}, u32[]{:S(2)}) async-start(bf16[8,16,1024]{2,1,0:T(8,128)(2,1)} %core_sum.1), calls=%async_computation.4 | async-start | bytes 524288 | tf_op jit(solution)/shard_map/all_to_all | solution.py:31
  81.6 18.1 %copy-start.3 = (bf16[432,128]{1,0:T(8,128)(2,1)S(1)}, bf16[432,128]{1,0:T(8,128)(2,1)}, u32[]{:S(2)}) copy-start(bf16[432,128]{1,0:T(8,128)(2,1)} %copy-done.2) | copy-start | bytes 331780
  94.6 11.5 %all-to-all-start.5 = ((bf16[16,16,640]{2,1,0:T(8,128)(2,1)}), bf16[16,16,640]{2,1,0:T(8,128)(2,1)S(1)}, u32[]{:S(2)}, u32[]{:S(2)}) async-start(bf16[16,16,640]{2,1,0:T(8,128)(2,1)} %get-tuple-element.48), calls=%async_computation.5 | async-start | bytes 655360 | tf_op jit(solution)/shard_map/all_to_all | solution.py:31
  98.2 1.5 %collective-permute-start.12 = (f32[16,128]{1,0:T(8,128)S(1)}, f32[16,128]{1,0:T(8,128)S(1)}, u32[]{:S(2)}, u32[]{:S(2)}) collective-permute-start(f32[16,128]{1,0:T(8,128)S(1)} %get-tuple-element.44.gram_ref), channel_id=1, source_target_pairs={{0,1},{1,0},{2,3},{3,2},{4,5},{5,4},{6,7},{7,6},{8,9},{9,8},{10,11... | collective-permute-start | bytes 24584 | tf_op jit(solution)/shard_map/ppermute | solution.py:287
